TPU v7x, 512 devices: a whole 4x4x16 slice. The times are simulated.
512 devices in a mesh: batch: 16 (over y, x_hi, core), seq: 32 (over z, x_lo).
Axes of the slice: x: 4 (x_hi: 2, x_lo: 2; x = x_hi * 2 + x_lo), y: 4, z: 16, core: 2. Of those that a mesh axis runs over, the one named last changes fastest.
Arguments:
- history_keys: bfloat16 [131072, 1024], P(('batch', 'seq')), parts along dimension 0, may hold values from -6 to 6
- history_values: bfloat16 [131072, 1024], P(('batch', 'seq')), parts along dimension 0, may hold values from -6 to 6
- lengths: int32 [16], P('batch'), parts along dimension 0, may hold values from 1024 to 8192, as said below
- item_ids: int32 [8192], P('batch'), parts along dimension 0, may hold values from 0 to 16383
- item_table: bfloat16 [16384, 1024], P('seq'), may hold values from -6 to 6
- w_proj: bfloat16 [1024, 4, 1024], P(None, None, 'seq'), may hold values from -0.1875 to 0.1875
- rab: float32 [8, 16], replicated, may hold values from -4 to 4
- norm_gain: float32 [1024], replicated, may hold values from 0.1 to 1.9
- w_out: bfloat16 [1024, 1024], P('seq'), may hold values from -0.1875 to 0.1875
Outputs:
- scored: bfloat16 [8192, 1024], P(('batch', 'seq')), parts along dimension 0
There are 16 independent parts, one for each index of `batch`. A program takes and returns all parts, laid end to end along the dimension named above; an argument that names none is the same for every part. Nothing has to cross between parts.
Inputs may be any that keep to these rules, and one draw needn't show every extreme that they name: `lengths`: in every fourth part, starting with the fourth, the history is full: L = 8192.
All inputs are finite; a program needn't handle non-finite values.
Results may differ from a plain program's by a relative error of at most 0.0085.
Values may be sent and summed in bfloat16 or wider, within the bound.
No kernel may reach another device: no remote copies, remote signals or barrier semaphores. Data moves between devices by JAX's collectives and lax.ppermute only.
A program may use at most 64 MiB of HBM per device.

v0:
```python
import jax
import jax.numpy as jnp
from jax import lax
from jax.sharding import PartitionSpec as P

block_rows = 128


def bucket_bias(rab_table, distance):
    bucket_count = rab_table.shape[1]
    powers = 2 ** jnp.arange(bucket_count - 1, dtype=jnp.int32)
    bucket = jnp.sum((distance[:, None] >= powers[None, :]).astype(jnp.int32), axis=1)
    hits = (bucket[None, :] == jnp.arange(bucket_count, dtype=jnp.int32)[:, None]).astype(
        jnp.float32
    )
    return jnp.dot(
        rab_table, hits, precision=lax.Precision.HIGHEST, preferred_element_type=jnp.float32
    )


def local(
    history_keys, history_values, lengths, item_ids, item_table, w_proj, rab, norm_gain, w_out
):
    device_count = lax.axis_size("seq")
    index_here = lax.axis_index("seq")
    events_here, width = history_keys.shape
    head_count = rab.shape[0]
    head_size = width // head_count
    scale = head_size ** (-0.5)
    table_rows = item_table.shape[0]
    cand_total = item_ids.shape[0]
    cand_here = cand_total // device_count
    feature_here = w_proj.shape[2]
    length = lengths[0]
    local_ids = item_ids - index_here * table_rows
    one_hot = (local_ids[:, None] == jnp.arange(table_rows, dtype=jnp.int32)[None, :]).astype(
        jnp.bfloat16
    )
    partial_rows = jnp.dot(one_hot, item_table, preferred_element_type=jnp.float32)
    embedded = lax.psum(partial_rows.astype(jnp.bfloat16), "seq")
    proj = jax.nn.silu(
        jnp.dot(
            embedded, w_proj.reshape(width, 4 * feature_here), preferred_element_type=jnp.float32
        )
    )
    proj = proj.reshape(cand_total, 4, feature_here).astype(jnp.bfloat16)
    queries = lax.all_gather(proj[:, 2, :], "seq", axis=1, tiled=True)
    gate_u, own_v, own_k = (
        lax.all_to_all(proj[:, 0, :], "seq", split_axis=0, concat_axis=1, tiled=True),
        lax.all_to_all(proj[:, 1, :], "seq", split_axis=0, concat_axis=1, tiled=True),
        lax.all_to_all(proj[:, 3, :], "seq", split_axis=0, concat_axis=1, tiled=True),
    )
    first_event = index_here * events_here
    live_blocks = jnp.clip(
        (length - first_event + block_rows - 1) // block_rows, 0, events_here // block_rows
    )
    heads_first = queries.reshape(cand_total, head_count, head_size).transpose(1, 0, 2)

    def visit(block_index, carried):
        key_block = lax.dynamic_slice_in_dim(history_keys, block_index * block_rows, block_rows, 0)
        value_block = lax.dynamic_slice_in_dim(
            history_values, block_index * block_rows, block_rows, 0
        )
        key_block = key_block.reshape(block_rows, head_count, head_size)
        value_block = value_block.reshape(block_rows, head_count, head_size)
        positions = first_event + block_index * block_rows + jnp.arange(block_rows, dtype=jnp.int32)
        bias = bucket_bias(rab, length - positions)
        scores = (
            lax.dot_general(
                heads_first,
                key_block,
                (((2,), (2,)), ((0,), (1,))),
                preferred_element_type=jnp.float32,
            )
            * scale
        )
        scores = scores + bias[:, None, :]
        weights = jnp.where((positions < length)[None, None, :], jax.nn.silu(scores), 0.0).astype(
            jnp.bfloat16
        )
        return carried + lax.dot_general(
            weights, value_block, (((2,), (0,)), ((0,), (1,))), preferred_element_type=jnp.float32
        )

    summed = lax.fori_loop(
        0,
        live_blocks,
        visit,
        jnp.zeros((head_count, cand_here * lax.axis_size("seq"), head_size), jnp.float32),
    )
    history_sum = lax.psum_scatter(
        summed.transpose(1, 0, 2).reshape(cand_here * lax.axis_size("seq"), width),
        "seq",
        scatter_dimension=0,
        tiled=True,
    )
    own_queries = lax.dynamic_slice_in_dim(queries, index_here * cand_here, cand_here, 0)
    self_scores = jnp.sum(
        (own_queries.astype(jnp.float32) * own_k.astype(jnp.float32)).reshape(
            cand_here, head_count, head_size
        ),
        axis=2,
    )
    self_scores = self_scores * scale + rab[:, 0][None, :]
    self_term = jax.nn.silu(self_scores)[:, :, None] * own_v.astype(jnp.float32).reshape(
        cand_here, head_count, head_size
    )
    attended = history_sum * lax.rsqrt(length.astype(jnp.float32)) + self_term.reshape(
        cand_here, width
    )
    centre = jnp.mean(attended, axis=1, keepdims=True)
    spread = jnp.mean((attended - centre) ** 2, axis=1, keepdims=True)
    normed = (
        (attended - centre)
        * lax.rsqrt(spread + 1e-05)
        * norm_gain[None, :]
        * gate_u.astype(jnp.float32)
    )
    normed = normed.astype(jnp.bfloat16)
    projected = jnp.dot(
        normed, lax.all_gather(w_out, "seq", axis=0, tiled=True), preferred_element_type=jnp.float32
    )
    own_embedded = lax.dynamic_slice_in_dim(embedded, index_here * cand_here, cand_here, 0)
    return (projected + own_embedded.astype(jnp.float32)).astype(jnp.bfloat16)


def solution(mesh):
    return jax.shard_map(
        local,
        mesh=mesh,
        in_specs=(
            P(("batch", "seq"), None),
            P(("batch", "seq"), None),
            P("batch"),
            P("batch"),
            P("seq", None),
            P(None, None, "seq"),
            P(),
            P(),
            P("seq", None),
        ),
        out_specs=P(("batch", "seq"), None),
        check_vma=False,
    )
```

profile of v0, /device:TPU:8, one launch (start us, length us, event | category | flops | bytes accessed | tf_op | source)
XLA Modules:
  0.0 714.3 jit_solution(11570158078600249780)
XLA Ops:
  6.5 0.8 broadcast_subtract_fusion
  7.3 0.4 copy-done
  7.8 1.7 convolution_convert_fusion
  9.6 270.7 %all-reduce.2.cloned.1.call-done = bf16[512,1024]{1,0:T(8,128)(2,1)} async-done(((bf16[512,1024]{1,0:T(8,128)(2,1)}), bf16[512,1024]{1,0:T(8,128)(2,1)}) %all-reduce.2.cloned.1.call-update) | async-done | bytes 1048592 | tf_op jit(solution)/shard_map/psum | solution.py:40
  280.3 1.8 multiply_convert_fusion
  282.0 0.6 fusion.26
  283.4 129.3 %all-gather.6.cloned.1.call-done = bf16[512,1,1024]{0,2,1:T(8,128)(2,1)} async-done(((bf16[512,1,32]{0,2,1:T(8,128)(2,1)}), bf16[512,1,1024]{0,2,1:T(8,128)(2,1)}) %all-gather.6.cloned.1.call-update) | async-done | bytes 1048592 | tf_op jit(solution)/shard_map/all_gather | solution.py:47
  412.7 2.4 copy.60
  415.0 1.5 broadcast_in_dim.14
  416.6 12.9 %while.10 = (s32[]{:T(128)}, f32[8,512,128]{2,1,0:T(8,128)}, s32[]{:T(128)}, s32[]{:T(128)}, s32[]{:T(128)}, /*index=5*/bf16[256,1024]{1,0:T(8,128)(2,1)S(1)}, b...) while((s32[]{:T(128)}, f32[8,512,128]{2,1,0:T(8,128)}, ...), condition=%wide.region_3.4_spmd, body=%wide.region_1.3_spmd.sunk | while | flops 273359264 | bytes 7875651 | solution.py:85
  416.6 0.2 copy.83
  416.8 0.2 copy.84
  417.0 0.7 fusion.45
  417.8 0.1 convolution_bitcast_fusion.2
  417.9 0.7 fusion.46
  418.5 4.5 convolution_add_fusion.3
  423.1 0.2 copy.83
  423.2 0.2 copy.84
  423.4 0.7 fusion.45
  424.2 0.1 convolution_bitcast_fusion.2
  424.3 0.7 fusion.46
  425.0 4.5 convolution_add_fusion.3
  429.5 1.9 copy.62
  431.4 1.8 copy.74
  433.3 0.5 all-gather.4.cloned.1.call-update
  433.8 0.1 copy.64
  434.0 0.7 reshape.140
  434.7 9.9 %all-to-all-start = ((bf16[32,2,256]{2,1,0:T(2,128)(2,1)}), bf16[32,2,256]{2,1,0:T(2,128)(2,1)S(1)}, u32[]{:S(2)}, u32[]{:S(2)}) async-start(bf16[32,2,256]{2,1,0:T(2,128)(2,1)} %reshape.140), calls=%async_computation | async-start | bytes 65536 | tf_op jit(solution)/shard_map/all_to_all | solution.py:51
  444.8 0.1 copy.67
  444.9 0.7 reshape.138
  445.8 0.8 reshape.136
  446.6 11.5 %all-to-all-done = bf16[32,2,256]{2,1,0:T(2,128)(2,1)S(1)} async-done(((bf16[32,2,256]{2,1,0:T(2,128)(2,1)}), bf16[32,2,256]{2,1,0:T(2,128)(2,1)S(1)}, u32[]{:S(2)}, u32[]{:S(2)}) %all-to-all-start) | async-done | bytes 32800 | tf_op jit(solution)/shard_map/all_to_all | solution.py:51
  458.1 3.8 all-to-all-start.1
  462.0 0.1 reshape.141
  462.1 0.2 copy.65
  462.4 13.3 %all-to-all-done.1 = bf16[32,2,256]{2,1,0:T(2,128)(2,1)S(1)} async-done(((bf16[32,2,256]{2,1,0:T(2,128)(2,1)}), bf16[32,2,256]{2,1,0:T(2,128)(2,1)S(1)}, u32[]{:S(2)}, u32[]{:S(2)}) %all-to-all-start.1) | async-done | bytes 32800 | tf_op jit(solution)/shard_map/all_to_all | solution.py:50
  475.7 3.9 all-to-all-start.2
  479.5 0.1 reshape.139
  479.8 0.1 reshape.127
  479.9 13.2 %all-to-all-done.2 = bf16[32,2,256]{2,1,0:T(2,128)(2,1)S(1)} async-done(((bf16[32,2,256]{2,1,0:T(2,128)(2,1)}), bf16[32,2,256]{2,1,0:T(2,128)(2,1)S(1)}, u32[]{:S(2)}, u32[]{:S(2)}) %all-to-all-start.2) | async-done | bytes 32800 | tf_op jit(solution)/shard_map/all_to_all | solution.py:49
  493.1 0.1 reshape.137
  493.4 0.1 reshape.128
  493.5 1.1 bitcast_reduce_fusion
  494.8 75.9 %reduce-scatter.4.cloned.1.call-done = f32[16,1024]{1,0:T(8,128)} async-done(((f32[512,1024]{1,0:T(8,128)}), f32[16,1024]{1,0:T(8,128)}) %reduce-scatter.4.cloned.1.call-update) | async-done | bytes 65552 | tf_op jit(solution)/shard_map/reduce_scatter | solution.py:91
  570.8 1.0 fusion.24
  571.8 0.2 multiply_reduce_fusion
  572.0 133.2 %all-gather.4.cloned.1.call-done = bf16[1024,1024]{1,0:T(8,128)(2,1)} async-done(((bf16[32,1024]{1,0:T(8,128)(2,1)}), bf16[1024,1024]{1,0:T(8,128)(2,1)}) %all-gather.4.cloned.1.call-update) | async-done | bytes 2097168 | tf_op jit(solution)/shard_map/all_gather | solution.py:121
  705.1 2.6 fusion.18
  (36 shorter events, 1.2 us)
Async XLA Ops:
  6.5 1.2 copy-start
  6.5 273.7 %copy-start.5 = (bf16[1024,4,32]{0,2,1:T(8,128)(2,1)S(1)}, bf16[1024,4,32]{0,2,1:T(8,128)(2,1)}, u32[]{:S(2)}) copy-start(bf16[1024,4,32]{0,2,1:T(8,128)(2,1)} %param.16) | copy-start | bytes 786436
  6.5 273.7 %all-reduce.2.cloned.1.call-start = ((), (), s32[]{:S(2)}) async-start(), calls=%async_computation.4 | async-start | bytes 2097152 | tf_op jit(solution)/shard_map/psum | solution.py:40
  9.5 403.1 %all-gather.6.cloned.1.call-start = ((), (), s32[]{:S(2)}) async-start(), calls=%async_computation.6 | async-start | bytes 1081344 | tf_op jit(solution)/shard_map/all_gather | solution.py:47
  282.7 288.0 %reduce-scatter.4.cloned.1.call-start = ((), (), s32[]{:S(2)}) async-start(), calls=%async_computation.7 | async-start | bytes 2162688 | tf_op jit(solution)/shard_map/reduce_scatter | solution.py:91
  412.7 3.9 copy-start.1
  412.7 3.9 copy-start.2
  412.7 3.9 copy-start.3
  433.3 271.9 %all-gather.4.cloned.1.call-start = ((), (), s32[]{:S(2)}) async-start(), calls=%async_computation.5 | async-start | bytes 2162688 | tf_op jit(solution)/shard_map/all_gather | solution.py:121
  434.7 23.4 %all-to-all-start = ((bf16[32,2,256]{2,1,0:T(2,128)(2,1)}), bf16[32,2,256]{2,1,0:T(2,128)(2,1)S(1)}, u32[]{:S(2)}, u32[]{:S(2)}) async-start(bf16[32,2,256]{2,1,0:T(2,128)(2,1)} %reshape.140), calls=%async_computation | async-start | bytes 65536 | tf_op jit(solution)/shard_map/all_to_all | solution.py:51
  458.1 17.6 %all-to-all-start.1 = ((bf16[32,2,256]{2,1,0:T(2,128)(2,1)}), bf16[32,2,256]{2,1,0:T(2,128)(2,1)S(1)}, u32[]{:S(2)}, u32[]{:S(2)}) async-start(bf16[32,2,256]{2,1,0:T(2,128)(2,1)} %reshape.138), calls=%async_computation.1 | async-start | bytes 65536 | tf_op jit(solution)/shard_map/all_to_all | solution.py:50
  462.3 242.8 %copy-start.4 = (f32[1024]{0:T(1024)S(1)}, f32[1024]{0:T(1024)}, u32[]{:S(2)}) copy-start(f32[1024]{0:T(1024)} %param.18) | copy-start | bytes 12292
  475.7 17.5 %all-to-all-start.2 = ((bf16[32,2,256]{2,1,0:T(2,128)(2,1)}), bf16[32,2,256]{2,1,0:T(2,128)(2,1)S(1)}, u32[]{:S(2)}, u32[]{:S(2)}) async-start(bf16[32,2,256]{2,1,0:T(2,128)(2,1)} %reshape.136), calls=%async_computation.2 | async-start | bytes 65536 | tf_op jit(solution)/shard_map/all_to_all | solution.py:49
Sparse Core Ops, SparseCore 0:
  10.3 269.9 all-reduce.1
  282.8 129.8 all-gather.5
  433.4 137.2 reduce-scatter.3
  572.6 132.4 all-gather.3
where the time goes:
time: 715 us; the launch traced here: 714 us
  waiting for transfers between devices  648 us (91%)
  starting transfers between devices  17.8 us (2%)
  matrix products  15.3 us (2%)
  between operations  14 us (2%)
  local copies, waits for them, and re-layouts  13.4 us (2%)
    psum x1, waiting for transfers between devices, local(): embedded = lax.psum(partial_rows.astype(jnp.bfloat16), 'seq')  271 us
    all_gather x1, waiting for transfers between devices, local(): lax.all_gather(w_out, 'seq', axis=0, tiled=True)  133 us
    all_gather x1, waiting for transfers between devices, local(): queries = lax.all_gather(proj[:, 2, :], 'seq', axis=1, tiled=True)  129 us
    reduce_scatter x1, waiting for transfers between devices, local(): lax.psum_scatter(summed.transpose(1, 0, 2).reshape(cand_here * lax.axis_s...  75.9 us
  transfers between devices with their start and end apart: 7, of which 7 were waited for; matrix products, arithmetic and copies ran while one was open for 1% of the time, Pallas kernels for 0%

commit v1 on v0

v1 whole, which is shorter than its diff:
```python
import jax
import jax.numpy as jnp
from jax import lax
from jax.experimental import pallas as pl
from jax.experimental.pallas import tpu as pltpu
from jax.sharding import PartitionSpec as P

slot_rows = 32


near_places = 4


def groups_of(places):
    return [[2 * place + side for place in group] for side in range(2) for group in places]


def column_groups():
    return groups_of([list(range(lax.axis_size("seq") // 2))])


def exchange(blocks, groups):
    return lax.all_to_all(
        blocks, "seq", split_axis=0, concat_axis=0, tiled=True, axis_index_groups=groups
    )


def two_step_gather(block):
    column = lax.axis_size("seq") // 2
    far_places = column // near_places
    far = groups_of([list(range(at, column, near_places)) for at in range(near_places)])
    near = groups_of(
        [list(range(at, at + near_places)) for at in range(0, column, near_places)]
    )
    blocks = exchange(jnp.broadcast_to(block[None], (far_places,) + block.shape), far)
    return exchange(
        jnp.broadcast_to(blocks[None], (near_places,) + blocks.shape).reshape(
            (column,) + block.shape
        ),
        near,
    )


def swap_pair(block):
    return lax.ppermute(block, "seq", [(i, i ^ 1) for i in range(lax.axis_size("seq"))])


def bucket_bias(rab_table, distance):
    bucket_count = rab_table.shape[1]
    powers = 2 ** jnp.arange(bucket_count - 1, dtype=jnp.int32)
    bucket = jnp.sum((distance[:, None] >= powers[None, :]).astype(jnp.int32), axis=1)
    hits = (bucket[None, :] == jnp.arange(bucket_count, dtype=jnp.int32)[:, None]).astype(
        jnp.float32
    )
    return jnp.dot(
        rab_table, hits, precision=lax.Precision.HIGHEST, preferred_element_type=jnp.float32
    )


def attend_kernel(
    scale, queries, keys_a, keys_b, values_a, values_b, bias_a, bias_b, live_a, live_b, summed
):
    head = pl.program_id(0)
    head_queries = queries[...].T
    total = None
    for keys, values, bias, live in (
        (keys_a, values_a, bias_a, live_a),
        (keys_b, values_b, bias_b, live_b),
    ):
        scores = lax.dot_general(
            head_queries, keys[...], (((1,), (1,)), ((), ())), preferred_element_type=jnp.float32
        )
        scores = scores * scale + bias[pl.ds(head, 1), :]
        weights = scores * (0.5 + 0.5 * jnp.tanh(0.5 * scores))
        weights = jnp.where(live[...] > 0.0, weights, 0.0).astype(jnp.bfloat16)
        part = jnp.dot(weights, values[...], preferred_element_type=jnp.float32)
        total = part if total is None else total + part
    summed[...] = total.astype(summed.dtype)


def attend(queries, keys, values, bias, live, head_count):
    width, cand = queries.shape
    events = keys[0].shape[0]
    head_size = width // head_count
    event_spec = pl.BlockSpec((events, head_size), lambda h: (0, h))
    bias_spec = pl.BlockSpec((head_count, events), lambda h: (0, 0))
    live_spec = pl.BlockSpec((1, events), lambda h: (0, 0))

    def body(*refs):
        attend_kernel(head_size ** (-0.5), *refs)

    return pl.pallas_call(
        body,
        grid=(head_count,),
        in_specs=[pl.BlockSpec((head_size, cand), lambda h: (h, 0))]
        + [event_spec] * 4
        + [bias_spec] * 2
        + [live_spec] * 2,
        out_specs=pl.BlockSpec((cand, head_size), lambda h: (0, h)),
        out_shape=jax.ShapeDtypeStruct((cand, width), jnp.bfloat16),
        compiler_params=pltpu.CompilerParams(vmem_limit_bytes=32 * 1024 * 1024),
        cost_estimate=pl.CostEstimate(
            flops=8 * cand * events * width,
            bytes_accessed=8 * events * width + 4 * cand * width,
            transcendentals=2 * cand * events * head_count,
        ),
    )(queries, keys[0], keys[1], values[0], values[1], bias[0], bias[1], live[0], live[1])


def local(
    history_keys, history_values, lengths, item_ids, item_table, w_proj, rab, norm_gain, w_out
):
    device_count = lax.axis_size("seq")
    column = device_count // 2
    index_here = lax.axis_index("seq")
    place, side = index_here // 2, index_here % 2
    events_here, width = history_keys.shape
    head_count = rab.shape[0]
    head_size = width // head_count
    scale = head_size ** (-0.5)
    table_rows = item_table.shape[0]
    cand_total = item_ids.shape[0]
    cand_here = cand_total // device_count
    cand_side = cand_total // 2
    feature_here = w_proj.shape[2]
    length = lengths[0]

    ids = item_ids.reshape(column, 2, cand_here).transpose(1, 0, 2).reshape(cand_total)
    shard = ids // table_rows
    row_there = ids - shard * table_rows
    same = shard[:, None] == shard[None, :]
    order = jnp.arange(cand_total, dtype=jnp.int32)
    rank = jnp.sum((same & (order[None, :] < order[:, None])).astype(jnp.int32), axis=1)
    most = jnp.max(rank) + 1

    w_mine = w_proj.reshape(width, 4 * feature_here)
    w_other = swap_pair(w_mine)
    w_first = jnp.where(side == 0, w_mine, w_other).reshape(width, 4, 1, feature_here)
    w_second = jnp.where(side == 0, w_other, w_mine).reshape(width, 4, 1, feature_here)
    w_pair = jnp.concatenate([w_first, w_second], axis=2).reshape(width, 8 * feature_here)
    w_query = w_pair[:, 4 * feature_here : 6 * feature_here]
    keys = (history_keys, swap_pair(history_keys))
    values = (history_values, swap_pair(history_values))
    w_out_all = lax.all_gather(w_out, "seq", axis=0, tiled=True)

    def lookup(first_rank):
        slot = rank - first_rank
        slots_here = jnp.arange(slot_rows, dtype=jnp.int32)
        taken = (shard == index_here)[:, None] & (slot[:, None] == slots_here[None, :])
        slot_row = jnp.sum(jnp.where(taken, row_there[:, None], 0), axis=0)
        picks = (
            slot_row[:, None] == jnp.arange(table_rows, dtype=jnp.int32)[None, :]
        ).astype(jnp.bfloat16)
        packed = jnp.dot(picks, item_table, preferred_element_type=jnp.float32)
        rows = two_step_gather(packed.astype(jnp.bfloat16)).reshape(column * slot_rows, width)
        inside = (shard % 2 == side) & (slot >= 0) & (slot < slot_rows)
        source = shard // 2
        block = (source % near_places) * (column // near_places) + source // near_places
        at = jnp.where(inside, block * slot_rows + slot, -1)
        chosen = (
            at[:, None] == jnp.arange(column * slot_rows, dtype=jnp.int32)[None, :]
        ).astype(jnp.bfloat16)
        queries = jax.nn.silu(
            lax.dot_general(
                w_query, rows, (((0,), (1,)), ((), ())), preferred_element_type=jnp.float32
            )
        ).astype(jnp.bfloat16)
        queries = lax.dot_general(
            queries, chosen, (((1,), (1,)), ((), ())), preferred_element_type=jnp.float32
        ).astype(jnp.bfloat16)
        proj = jax.nn.silu(jnp.dot(rows, w_pair, preferred_element_type=jnp.float32)).astype(
            jnp.bfloat16
        )
        proj = jnp.dot(chosen, proj, preferred_element_type=jnp.float32).astype(jnp.bfloat16)
        pair_chosen = lax.dynamic_slice_in_dim(
            chosen.reshape(2, cand_side, column * slot_rows), place * cand_here, cand_here, 1
        ).reshape(2 * cand_here, column * slot_rows)
        embedded = jnp.dot(pair_chosen, rows, preferred_element_type=jnp.float32).astype(
            jnp.bfloat16
        )
        return queries, proj, embedded

    def another(state):
        first_rank, found = state
        more = lookup(first_rank)
        return first_rank + slot_rows, tuple(a + b for a, b in zip(found, more))

    _, (queries, proj, embedded) = lax.while_loop(
        lambda state: state[0] < most, another, (jnp.int32(slot_rows), lookup(jnp.int32(0)))
    )

    def join(both, axis, size):
        mine = lax.dynamic_slice_in_dim(both, side * size, size, axis)
        other = lax.dynamic_slice_in_dim(both, (1 - side) * size, size, axis)
        return mine + swap_pair(other)

    side_queries = join(queries, 1, cand_side)
    own_embedded = join(embedded, 0, cand_here)
    all_queries = lax.all_gather(
        side_queries, "seq", axis=0, tiled=True, axis_index_groups=column_groups()
    )
    own_proj = exchange(
        join(proj, 0, cand_side).reshape(column, cand_here, 8 * feature_here), column_groups()
    )
    own_proj = (
        own_proj.reshape(column, cand_here, 4, 2 * feature_here)
        .transpose(2, 1, 0, 3)
        .reshape(4, cand_here, width)
        .astype(jnp.float32)
    )
    gate_u, own_v, own_queries, own_k = own_proj[0], own_proj[1], own_proj[2], own_proj[3]

    def bias_of(index):
        positions = index * events_here + jnp.arange(events_here, dtype=jnp.int32)
        return (
            bucket_bias(rab, length - positions),
            (positions < length).astype(jnp.float32)[None, :],
        )

    bias, live = zip(bias_of(index_here), bias_of(index_here + 1 - 2 * side))
    summed = attend(all_queries, keys, values, bias, live, head_count)
    parts = exchange(summed.reshape(column, cand_here, width), column_groups())
    history_sum = jnp.sum(parts.astype(jnp.float32), axis=0)

    self_scores = jnp.sum((own_queries * own_k).reshape(cand_here, head_count, head_size), axis=2)
    self_scores = self_scores * scale + rab[:, 0][None, :]
    self_term = jax.nn.silu(self_scores)[:, :, None] * own_v.reshape(
        cand_here, head_count, head_size
    )
    attended = history_sum * lax.rsqrt(length.astype(jnp.float32)) + self_term.reshape(
        cand_here, width
    )
    centre = jnp.mean(attended, axis=1, keepdims=True)
    spread = jnp.mean((attended - centre) ** 2, axis=1, keepdims=True)
    normed = (attended - centre) * lax.rsqrt(spread + 1e-05) * norm_gain[None, :] * gate_u
    normed = normed.astype(jnp.bfloat16)
    projected = jnp.dot(normed, w_out_all, preferred_element_type=jnp.float32)
    return (projected + own_embedded.astype(jnp.float32)).astype(jnp.bfloat16)


def solution(mesh):
    return jax.shard_map(
        local,
        mesh=mesh,
        in_specs=(
            P(("batch", "seq"), None),
            P(("batch", "seq"), None),
            P("batch"),
            P("batch"),
            P("seq", None),
            P(None, None, "seq"),
            P(),
            P(),
            P("seq", None),
        ),
        out_specs=P(("batch", "seq"), None),
        check_vma=False,
    )
```

time: 715 us -> 208 us (0.29)
  the two profiles are of different devices: /device:TPU:8 before, /device:TPU:16 now
where the time goes in v1:
time: 208 us; the launch traced here: 207 us
  blocking collectives  67.2 us (32%)
  waiting for transfers between devices  53.3 us (26%)
  starting transfers between devices  40.1 us (19%)
  between operations  15.1 us (7%)
  matrix products  9.62 us (5%)
  local copies, waits for them, and re-layouts  9.43 us (5%)
  other arithmetic  6.69 us (3%)
  Pallas kernels  5.25 us (3%)
    all_to_all x1, blocking collectives, exchange(): lax.all_to_all(blocks, 'seq', split_axis=0, concat_axis=0, tiled=True, ax...  33.8 us
    all_gather x1, blocking collectives, local(): lax.all_gather(side_queries, 'seq', axis=0, tiled=True, axis_index_groups...  33.4 us
    all_gather x1, waiting for transfers between devices, local(): w_out_all = lax.all_gather(w_out, 'seq', axis=0, tiled=True)  25.7 us
    all_to_all x3, waiting for transfers between devices, exchange(): lax.all_to_all(blocks, 'seq', split_axis=0, concat_axis=0, tiled=True, ax...  23.9 us
    all_to_all x3, starting transfers between devices, exchange(): lax.all_to_all(blocks, 'seq', split_axis=0, concat_axis=0, tiled=True, ax...  22.5 us
    ppermute x6, starting transfers between devices, swap_pair(): lax.ppermute(block, 'seq', [(i, i ^ 1) for i in range(lax.axis_size('seq'...  17.6 us
    pallas_call x1, Pallas kernels, attend(): pl.pallas_call(body, grid=(head_count,), in_specs=[pl.BlockSpec((head_siz...  5.25 us
  transfers between devices with their start and end apart: 10, of which 4 were waited for; matrix products, arithmetic and copies ran while one was open for 9% of the time, Pallas kernels for 3%

profile of v1, /device:TPU:16, one launch (start us, length us, event | category | flops | bytes accessed | tf_op | source)
XLA Modules:
  0.0 206.7 jit_solution(3889067986538222629)
XLA Ops:
  6.5 0.8 reshape.572
  7.3 0.1 reshape.573
  7.4 0.3 convert_reduce_fusion.1
  7.7 0.6 fusion.67
  8.3 0.1 select_reduce_fusion.1
  8.4 1.5 convolution_convert_fusion.6
  10.1 33.8 %all_to_all.44 = bf16[4,32,1024]{2,1,0:T(8,128)(2,1)S(1)} all-to-all(bf16[4,32,1024]{2,1,0:T(8,128)(2,1)S(1)} %broadcast_in_dim.80), channel_id=1, replica_groups={{0,8,16,24},{2,10,18,26},{4,12,20,28},{6,14,22,30},{1,9,17,25},{3,11,19..., dimensions={0} | all-to-all | bytes 524288 | tf_op jit(solution)/shard_map/all_to_all | solution.py:23
  43.9 1.1 broadcast_in_dim.81
  45.0 5.3 %all-to-all-start.3 = ((bf16[16,32,1024]{2,1,0:T(8,128)(2,1)}), bf16[16,32,1024]{2,1,0:T(8,128)(2,1)S(1)}, u32[]{:S(2)}, u32[]{:S(2)}) async-start(bf16[16,32,1024]{2,1,0:T(8,128)(2,1)} %bitcast.10), calls=%async_computation.3 | async-start | bytes 2097152 | tf_op jit(solution)/shard_map/all_to_all | solution.py:23
  50.3 3.4 %collective-permute-start = (bf16[1024,128]{0,1:T(8,128)(2,1)S(1)}, bf16[1024,128]{0,1:T(8,128)(2,1)}, u32[]{:S(2)}, u32[]{:S(2)}) collective-permute-start(bf16[1024,128]{0,1:T(8,128)(2,1)S(1)} %bitcast.113), channel_id=1, source_target_pairs={{0,1},{1,0},{2,3},{3,2},{4,5},{5,4},{6,7},{7,6},{8,9},{9,8},{10,11... | collective-permute-start | bytes 786440 | tf_op jit(solution)/shard_map/ppermute | solution.py:45
  53.7 2.4 %collective-permute-start.2 = (bf16[256,1024]{1,0:T(8,128)(2,1)S(1)}, bf16[256,1024]{1,0:T(8,128)(2,1)S(1)}, u32[]{:S(2)}, u32[]{:S(2)}) collective-permute-start(bf16[256,1024]{1,0:T(8,128)(2,1)S(1)} %copy-done), channel_id=1, source_target_pairs={{0,1},{1,0},{2,3},{3,2},{4,5},{5,4},{6,7},{7,6},{8,9},{9,8},{10,11... | collective-permute-start | bytes 1572872 | tf_op jit(solution)/shard_map/ppermute | solution.py:45
  56.2 3.4 %collective-permute-start.3 = (bf16[256,1024]{1,0:T(8,128)(2,1)S(1)}, bf16[256,1024]{1,0:T(8,128)(2,1)S(1)}, u32[]{:S(2)}, u32[]{:S(2)}) collective-permute-start(bf16[256,1024]{1,0:T(8,128)(2,1)S(1)} %copy-done.1), channel_id=1, source_target_pairs={{0,1},{1,0},{2,3},{3,2},{4,5},{5,4},{6,7},{7,6},{8,9},{9,8},{10,11... | collective-permute-start | bytes 1572872 | tf_op jit(solution)/shard_map/ppermute | solution.py:45
  59.7 0.1 reshape.576
  60.5 0.1 convert_reduce_fusion.2
  60.7 0.1 convolution_bitcast_fusion.1.refs_6_
  60.8 0.1 convolution_bitcast_fusion.2.refs_5_
  61.7 0.7 iota_compare_fusion.11
  62.4 1.0 broadcast_select_fusion.1
  63.5 0.9 copy.32
  64.3 2.0 copy.37
  66.4 0.9 slice.28
  67.3 0.8 copy.36
  68.1 6.7 %all-to-all-done.3 = bf16[16,32,1024]{2,1,0:T(8,128)(2,1)S(1)} async-done(((bf16[16,32,1024]{2,1,0:T(8,128)(2,1)}), bf16[16,32,1024]{2,1,0:T(8,128)(2,1)S(1)}, u32[]{:S(2)}, u32[]{:S(2)}) %all-to-all-start.3) | async-done | bytes 1048608 | tf_op jit(solution)/shard_map/all_to_all | solution.py:23
  74.8 2.7 %convolution_convert_fusion.4 = bf16[512,256]{1,0:T(8,128)(2,1)} fusion(s32[512]{0:T(512)S(1)} %get-tuple-element.469, bf16[512,1024]{1,0:T(8,128)(2,1)S(1)} %bitcast.101, bf16[1024,256]{0,1:T(8,128)(2,1)} %bitcast.106), kind=kOutput, calls=%fused_computation.65 | convolution fusion | flops 403701760 | bytes 1837056 | tf_op jit(solution)/shard_map/dot_general | solution.py:174
  77.5 2.2 %convolution_convert_fusion.7 = bf16[64,512]{1,0:T(8,128)(2,1)} fusion(s32[512]{0:T(512)S(1)} %get-tuple-element.469, bf16[512,1024]{1,0:T(8,128)(2,1)S(1)} %bitcast.102, bf16[1024,256]{0,1:T(8,128)(2,1)} %bitcast.107), kind=kOutput, calls=%fused_computation.68 | convolution fusion | flops 101122048 | bytes 1247232 | tf_op jit(solution)/shard_map/dot_general | solution.py:168
  79.7 0.3 convolution_convert_fusion.5
  80.0 0.9 constant_dynamic-slice_fusion.1
  81.0 3.7 %collective-permute-start.4 = (bf16[256,256]{1,0:T(8,128)(2,1)S(1)}, bf16[256,256]{1,0:T(8,128)(2,1)S(1)}, u32[]{:S(2)}, u32[]{:S(2)}) collective-permute-start(bf16[256,256]{1,0:T(8,128)(2,1)S(1)} %constant_dynamic-slice_fusion.1), channel_id=1, source_target_pairs={{0,1},{1,0},{2,3},{3,2},{4,5},{5,4},{6,7},{7,6},{8,9},{9,8},{10,11... | collective-permute-start | bytes 393224 | tf_op jit(solution)/shard_map/ppermute | solution.py:45
  84.7 0.8 constant_dynamic-slice_fusion.2
  85.5 2.1 %collective-permute-start.1 = (bf16[64,256]{1,0:T(8,128)(2,1)S(1)}, bf16[64,256]{1,0:T(8,128)(2,1)S(1)}, u32[]{:S(2)}, u32[]{:S(2)}) collective-permute-start(bf16[64,256]{1,0:T(8,128)(2,1)S(1)} %constant_dynamic-slice_fusion.2), channel_id=1, source_target_pairs={{0,1},{1,0},{2,3},{3,2},{4,5},{5,4},{6,7},{7,6},{8,9},{9,8},{10,11... | collective-permute-start | bytes 98312 | tf_op jit(solution)/shard_map/ppermute | solution.py:45
  87.6 3.7 %collective-permute-done.4 = bf16[256,256]{1,0:T(8,128)(2,1)S(1)} collective-permute-done((bf16[256,256]{1,0:T(8,128)(2,1)S(1)}, bf16[256,256]{1,0:T(8,128)(2,1)S(1)}, u32[]{:S(2)}, u32[]{:S(2)}) %collective-permute-start.4) | collective-permute-done | bytes 131104 | tf_op jit(solution)/shard_map/ppermute | solution.py:45
  91.3 1.6 dynamic-slice_add_fusion
  92.9 6.0 %all-to-all-start.5 = ((bf16[16,16,256]{2,1,0:T(8,128)(2,1)}), bf16[16,16,256]{2,1,0:T(8,128)(2,1)S(1)}, u32[]{:S(2)}, u32[]{:S(2)}) async-start(bf16[16,16,256]{2,1,0:T(8,128)(2,1)} %bitcast.17), calls=%async_computation.5 | async-start | bytes 262144 | tf_op jit(solution)/shard_map/all_to_all | solution.py:23
  98.9 0.8 dynamic-slice_add_fusion.1
  99.7 33.4 %all_gather.6.refs_0_ = bf16[1024,256]{1,0:T(8,128)(2,1)S(1)} all-gather(bf16[64,256]{1,0:T(8,128)(2,1)S(1)} %dynamic-slice_add_fusion.1), channel_id=1, replica_groups={{0,2,4,6,8,10,12,14,16,18,20,22,24,26,28,30},{1,3,5,7,9,11,13,15,17,19,..., dimensions={0}, use_global_device_ids=true | all-gather | bytes 557056 | tf_op jit(solution)/shard_map/all_gather | solution.py:199
  133.1 5.2 %shard_map.91 = bf16[256,1024]{1,0:T(8,128)(2,1)} custom-call(bf16[1024,256]{1,0:T(8,128)(2,1)S(1)} %all_gather.6.refs_0_, bf16[256,1024]{1,0:T(8,128)(2,1)S(1)} %copy-done, bf16[256,1024]{1,0:T(8,128)(2,1)S(1)} %collective-permute-done.2.refs_2_, bf16[256,1024]{1,0:T(8,128)(2,1)S(1)} %copy-done.1, bf16[256,1024]{1,0:T(8,128)(2,1)S(1)} %collective-permute-done.3.refs_4_, ...), custom_call_target="tpu_custom_call" | custom-call | flops 536870912 | bytes 3145728 | tf_op jit(solution)/shard_map/pallas_call | solution.py:92
  138.4 11.1 %all-to-all-start.4 = ((bf16[16,16,1024]{2,1,0:T(8,128)(2,1)}), bf16[16,16,1024]{2,1,0:T(8,128)(2,1)S(1)}, u32[]{:S(2)}, u32[]{:S(2)}) async-start(bf16[16,16,1024]{2,1,0:T(8,128)(2,1)} %bitcast.16), calls=%async_computation.4 | async-start | bytes 1048576 | tf_op jit(solution)/shard_map/all_to_all | solution.py:23
  149.5 0.1 slice_reduce_fusion
  149.7 2.6 %collective-permute-start.5 = (bf16[16,1024]{1,0:T(8,128)(2,1)S(1)}, bf16[16,1024]{1,0:T(8,128)(2,1)S(1)}, u32[]{:S(2)}, u32[]{:S(2)}) collective-permute-start(bf16[16,1024]{1,0:T(8,128)(2,1)S(1)} %constant_dynamic-slice_fusion.4), channel_id=1, source_target_pairs={{0,1},{1,0},{2,3},{3,2},{4,5},{5,4},{6,7},{7,6},{8,9},{9,8},{10,11... | collective-permute-start | bytes 98312 | tf_op jit(solution)/shard_map/ppermute | solution.py:45
  152.2 0.3 reshape.581
  152.5 0.9 fusion.27
  153.4 0.1 reshape_squeeze.3
  153.7 0.1 squeeze.9
  153.8 17.2 %all-to-all-done.4 = bf16[16,16,1024]{2,1,0:T(8,128)(2,1)S(1)} async-done(((bf16[16,16,1024]{2,1,0:T(8,128)(2,1)}), bf16[16,16,1024]{2,1,0:T(8,128)(2,1)S(1)}, u32[]{:S(2)}, u32[]{:S(2)}) %all-to-all-start.4) | async-done | bytes 524320 | tf_op jit(solution)/shard_map/all_to_all | solution.py:23
  171.2 0.1 fusion.62
  171.4 0.2 multiply_reduce_fusion
  171.6 25.7 %all-gather.2.cloned.1.call-done = bf16[1024,1024]{1,0:T(8,128)(2,1)} async-done(((bf16[32,1024]{1,0:T(8,128)(2,1)}), bf16[1024,1024]{1,0:T(8,128)(2,1)}) %all-gather.2.cloned.1.call-update) | async-done | bytes 2097168 | tf_op jit(solution)/shard_map/all_gather | solution.py:144
  197.2 2.6 %add_convert_fusion = bf16[16,1024]{1,0:T(8,128)(2,1)} fusion(bf16[16,1024]{1,0:T(8,128)(2,1)S(1)} %collective-permute-done.5, bf16[32,1024]{1,0:T(8,128)(2,1)S(1)} %get-tuple-element.342, s32[]{:T(128)S(6)} %select_n.347, bf16[1024,1024]{1,0:T(8,128)(2,1)} %all-gather.2.cloned.1.call-done, f32[16,1024]{1,0:T(8,128)S(1)} %squeeze.9, ...), kind=kOutput, calls=%fused_computation.89 | convolution fusion | flops 33734656 | bytes 2330756 | tf_op jit(solution)/shard_map/dot_general | solution.py:237
  (51 shorter events, 0.9 us)
Async XLA Ops:
  10.0 40.3 %copy-start.3 = (bf16[1024,4,32]{0,2,1:T(8,128)(2,1)S(1)}, bf16[1024,4,32]{0,2,1:T(8,128)(2,1)}, u32[]{:S(2)}) copy-start(bf16[1024,4,32]{0,2,1:T(8,128)(2,1)} %param.16) | copy-start | bytes 786436
  10.0 43.7 %copy-start = (bf16[256,1024]{1,0:T(8,128)(2,1)S(1)}, bf16[256,1024]{1,0:T(8,128)(2,1)}, u32[]{:S(2)}) copy-start(bf16[256,1024]{1,0:T(8,128)(2,1)} %refs_1_.1) | copy-start | bytes 1572868
  10.0 46.2 %copy-start.1 = (bf16[256,1024]{1,0:T(8,128)(2,1)S(1)}, bf16[256,1024]{1,0:T(8,128)(2,1)}, u32[]{:S(2)}) copy-start(bf16[256,1024]{1,0:T(8,128)(2,1)} %refs_3_.1) | copy-start | bytes 1572868
  10.1 50.6 %copy-start.5 = (f32[8,16]{1,0:T(8,128)S(1)}, f32[8,16]{1,0:T(8,128)}, u32[]{:S(2)}) copy-start(f32[8,16]{1,0:T(8,128)} %param.17) | copy-start | bytes 1540
  45.0 29.8 %all-to-all-start.3 = ((bf16[16,32,1024]{2,1,0:T(8,128)(2,1)}), bf16[16,32,1024]{2,1,0:T(8,128)(2,1)S(1)}, u32[]{:S(2)}, u32[]{:S(2)}) async-start(bf16[16,32,1024]{2,1,0:T(8,128)(2,1)} %bitcast.10), calls=%async_computation.3 | async-start | bytes 2097152 | tf_op jit(solution)/shard_map/all_to_all | solution.py:23
  50.3 146.9 %all-gather.2.cloned.1.call-start = ((), (), s32[]{:S(2)}) async-start(), calls=%async_computation.6 | async-start | bytes 2162688 | tf_op jit(solution)/shard_map/all_gather | solution.py:144
  50.3 12.1 %collective-permute-start = (bf16[1024,128]{0,1:T(8,128)(2,1)S(1)}, bf16[1024,128]{0,1:T(8,128)(2,1)}, u32[]{:S(2)}, u32[]{:S(2)}) collective-permute-start(bf16[1024,128]{0,1:T(8,128)(2,1)S(1)} %bitcast.113), channel_id=1, source_target_pairs={{0,1},{1,0},{2,3},{3,2},{4,5},{5,4},{6,7},{7,6},{8,9},{9,8},{10,11... | collective-permute-start | bytes 786440 | tf_op jit(solution)/shard_map/ppermute | solution.py:45
  53.7 79.4 %collective-permute-start.2 = (bf16[256,1024]{1,0:T(8,128)(2,1)S(1)}, bf16[256,1024]{1,0:T(8,128)(2,1)S(1)}, u32[]{:S(2)}, u32[]{:S(2)}) collective-permute-start(bf16[256,1024]{1,0:T(8,128)(2,1)S(1)} %copy-done), channel_id=1, source_target_pairs={{0,1},{1,0},{2,3},{3,2},{4,5},{5,4},{6,7},{7,6},{8,9},{9,8},{10,11... | collective-permute-start | bytes 1572872 | tf_op jit(solution)/shard_map/ppermute | solution.py:45
  56.2 76.9 %collective-permute-start.3 = (bf16[256,1024]{1,0:T(8,128)(2,1)S(1)}, bf16[256,1024]{1,0:T(8,128)(2,1)S(1)}, u32[]{:S(2)}, u32[]{:S(2)}) collective-permute-start(bf16[256,1024]{1,0:T(8,128)(2,1)S(1)} %copy-done.1), channel_id=1, source_target_pairs={{0,1},{1,0},{2,3},{3,2},{4,5},{5,4},{6,7},{7,6},{8,9},{9,8},{10,11... | collective-permute-start | bytes 1572872 | tf_op jit(solution)/shard_map/ppermute | solution.py:45
  74.8 4.9 %copy-start.4 = (pred[2,16,512]{2,1,0:T(8,128)(4,1)S(1)}, pred[2,16,512]{2,1,0:T(8,128)(4,1)}, u32[]{:S(2)}) copy-start(pred[2,16,512]{2,1,0:T(8,128)(4,1)} %iota_compare_fusion.11) | copy-start | bytes 49156
  77.5 2.5 %copy-start.2 = (bf16[1024,64]{1,0:T(8,128)(2,1)S(1)}, bf16[1024,64]{1,0:T(8,128)(2,1)}, u32[]{:S(2)}) copy-start(bf16[1024,64]{1,0:T(8,128)(2,1)} %copy.36) | copy-start | bytes 393220
  81.0 10.3 %collective-permute-start.4 = (bf16[256,256]{1,0:T(8,128)(2,1)S(1)}, bf16[256,256]{1,0:T(8,128)(2,1)S(1)}, u32[]{:S(2)}, u32[]{:S(2)}) collective-permute-start(bf16[256,256]{1,0:T(8,128)(2,1)S(1)} %constant_dynamic-slice_fusion.1), channel_id=1, source_target_pairs={{0,1},{1,0},{2,3},{3,2},{4,5},{5,4},{6,7},{7,6},{8,9},{9,8},{10,11... | collective-permute-start | bytes 393224 | tf_op jit(solution)/shard_map/ppermute | solution.py:45
  85.5 13.4 %collective-permute-start.1 = (bf16[64,256]{1,0:T(8,128)(2,1)S(1)}, bf16[64,256]{1,0:T(8,128)(2,1)S(1)}, u32[]{:S(2)}, u32[]{:S(2)}) collective-permute-start(bf16[64,256]{1,0:T(8,128)(2,1)S(1)} %constant_dynamic-slice_fusion.2), channel_id=1, source_target_pairs={{0,1},{1,0},{2,3},{3,2},{4,5},{5,4},{6,7},{7,6},{8,9},{9,8},{10,11... | collective-permute-start | bytes 98312 | tf_op jit(solution)/shard_map/ppermute | solution.py:45
  92.9 45.5 %all-to-all-start.5 = ((bf16[16,16,256]{2,1,0:T(8,128)(2,1)}), bf16[16,16,256]{2,1,0:T(8,128)(2,1)S(1)}, u32[]{:S(2)}, u32[]{:S(2)}) async-start(bf16[16,16,256]{2,1,0:T(8,128)(2,1)} %bitcast.17), calls=%async_computation.5 | async-start | bytes 262144 | tf_op jit(solution)/shard_map/all_to_all | solution.py:23
  138.4 58.9 %copy-start.6 = (f32[1024]{0:T(1024)S(1)}, f32[1024]{0:T(1024)}, u32[]{:S(2)}) copy-start(f32[1024]{0:T(1024)} %param.18) | copy-start | bytes 12292
  138.4 32.7 %all-to-all-start.4 = ((bf16[16,16,1024]{2,1,0:T(8,128)(2,1)}), bf16[16,16,1024]{2,1,0:T(8,128)(2,1)S(1)}, u32[]{:S(2)}, u32[]{:S(2)}) async-start(bf16[16,16,1024]{2,1,0:T(8,128)(2,1)} %bitcast.16), calls=%async_computation.4 | async-start | bytes 1048576 | tf_op jit(solution)/shard_map/all_to_all | solution.py:23
  149.7 21.9 %collective-permute-start.5 = (bf16[16,1024]{1,0:T(8,128)(2,1)S(1)}, bf16[16,1024]{1,0:T(8,128)(2,1)S(1)}, u32[]{:S(2)}, u32[]{:S(2)}) collective-permute-start(bf16[16,1024]{1,0:T(8,128)(2,1)S(1)} %constant_dynamic-slice_fusion.4), channel_id=1, source_target_pairs={{0,1},{1,0},{2,3},{3,2},{4,5},{5,4},{6,7},{7,6},{8,9},{9,8},{10,11... | collective-permute-start | bytes 98312 | tf_op jit(solution)/shard_map/ppermute | solution.py:45
Sparse Core Ops, SparseCore 0:
  59.8 137.4 all-gather.1

commit v2 on v1

v2 whole, which is shorter than its diff:
```python
import jax
import jax.numpy as jnp
from jax import lax
from jax.experimental import pallas as pl
from jax.experimental.pallas import tpu as pltpu
from jax.sharding import PartitionSpec as P

slot_rows = 32
near_places = 4


def groups_of(places):
    return [[2 * place + side for place in group] for side in range(2) for group in places]


def exchange(blocks, groups):
    return lax.all_to_all(
        blocks, "seq", split_axis=0, concat_axis=0, tiled=True, axis_index_groups=groups
    )


def column_groups():
    return groups_of([list(range(lax.axis_size("seq") // 2))])


def from_place(block, shift):
    count = lax.axis_size("seq")
    return lax.ppermute(block, "seq", [(i, (i + 2 * shift) % count) for i in range(count)])


def swap_pair(block):
    return lax.ppermute(block, "seq", [(i, i ^ 1) for i in range(lax.axis_size("seq"))])


def swap_core(block):
    return lax.ppermute(block, "batch", [(i, i ^ 1) for i in range(lax.axis_size("batch"))])


def from_row(block, shift):
    count = lax.axis_size("batch")
    return lax.ppermute(block, "batch", [(i, (i + 4 * shift) % count) for i in range(count)])


def gather_slots(block):
    column = lax.axis_size("seq") // 2
    far_places = column // near_places
    far = groups_of([list(range(at, column, near_places)) for at in range(near_places)])
    blocks = exchange(jnp.broadcast_to(block[None], (far_places,) + block.shape), far)
    rows = blocks.reshape(far_places * block.shape[0], block.shape[1])
    half = rows.shape[0] // 2
    return (
        rows,
        from_place(rows, 1),
        from_place(rows, -1),
        from_place(rows[:half], 2),
        from_place(rows[half:], -2),
    )


def bucket_bias(rab_table, distance):
    bucket_count = rab_table.shape[1]
    powers = 2 ** jnp.arange(bucket_count - 1, dtype=jnp.int32)
    bucket = jnp.sum((distance[:, None] >= powers[None, :]).astype(jnp.int32), axis=1)
    hits = (bucket[None, :] == jnp.arange(bucket_count, dtype=jnp.int32)[:, None]).astype(
        jnp.float32
    )
    return jnp.dot(
        rab_table, hits, precision=lax.Precision.HIGHEST, preferred_element_type=jnp.float32
    )


def silu(value):
    return value * (0.5 + 0.5 * jnp.tanh(0.5 * value))


def project_kernel(at, at_pair, rows_0, rows_1, rows_2, rows_3, rows_4, weights, *rest):
    proj_mine, proj_other, own_rows, other_rows, slots = rest
    cand_side = proj_mine.shape[0]
    own = own_rows.shape[0]
    first = 0
    for rows in (rows_0, rows_1, rows_2, rows_3, rows_4):
        count = rows.shape[0]
        slots[first : first + count, :] = silu(
            jnp.dot(rows[...], weights[...], preferred_element_type=jnp.float32)
        ).astype(jnp.bfloat16)
        first += count
    place = lax.broadcasted_iota(jnp.int32, (cand_side, first), 1)
    for side, proj in ((0, proj_mine), (1, proj_other)):
        chosen = (at[side * cand_side : (side + 1) * cand_side, :] == place).astype(jnp.float32)
        proj[...] = jnp.dot(
            chosen.astype(jnp.bfloat16), slots[...], preferred_element_type=jnp.float32
        ).astype(jnp.bfloat16)
    place = lax.broadcasted_iota(jnp.int32, (2 * own, first), 1)
    chosen = (at_pair[...] == place).astype(jnp.float32).astype(jnp.bfloat16)
    total = None
    first = 0
    for rows in (rows_0, rows_1, rows_2, rows_3, rows_4):
        count = rows.shape[0]
        part = jnp.dot(
            chosen[:, first : first + count], rows[...], preferred_element_type=jnp.float32
        )
        total = part if total is None else total + part
        first += count
    own_rows[...] = total[:own].astype(jnp.bfloat16)
    other_rows[...] = total[own:].astype(jnp.bfloat16)


def project(at, at_pair, rows, weights):
    width, columns = weights.shape
    cand_side = at.shape[0] // 2
    own = at_pair.shape[0] // 2
    slot_count = sum(piece.shape[0] for piece in rows)
    return pl.pallas_call(
        project_kernel,
        out_shape=[jax.ShapeDtypeStruct((cand_side, columns), jnp.bfloat16)] * 2
        + [jax.ShapeDtypeStruct((own, width), jnp.bfloat16)] * 2,
        scratch_shapes=[pltpu.VMEM((slot_count, columns), jnp.bfloat16)],
        compiler_params=pltpu.CompilerParams(vmem_limit_bytes=32 * 1024 * 1024),
        cost_estimate=pl.CostEstimate(
            flops=2 * slot_count * columns * (width + 2 * cand_side),
            bytes_accessed=2 * (slot_count + columns) * width,
            transcendentals=slot_count * columns,
        ),
    )(at, at_pair, *rows, weights)


def pack_kernel(feature_here, mine, arrived, w_slice, *rest):
    queries, packed = rest[-2:]
    proj = mine[...].astype(jnp.float32) + arrived[...].astype(jnp.float32)
    block = 4 * feature_here
    query = jnp.concatenate(
        [proj[:, side * block + 2 * feature_here : side * block + 3 * feature_here] for side in (0, 1)],
        axis=1,
    )
    queries[...] = query.T.astype(jnp.bfloat16)
    column, own, _ = packed.shape
    columns = 2 * block
    packed[:, :, :columns] = proj.astype(jnp.bfloat16).reshape(column, own, columns)
    lanes = w_slice.shape[1]
    for part in range(w_slice.shape[0] // own):
        packed[:, :, columns + part * lanes : columns + (part + 1) * lanes] = jnp.broadcast_to(
            w_slice[part * own : (part + 1) * own, :][None], (column, own, lanes)
        )


def pack(mine, arrived, w_slice, ready, feature_here, own):
    cand_side, columns = mine.shape
    column = cand_side // own
    packed_width = columns + w_slice.shape[0] * w_slice.shape[1] // own
    whole = pl.BlockSpec(memory_space=pltpu.VMEM)
    return pl.pallas_call(
        lambda *refs: pack_kernel(feature_here, *refs),
        in_specs=[whole] * 3 + [pl.BlockSpec(memory_space=pl.ANY)] * len(ready),
        out_specs=[whole] * 2,
        out_shape=[
            jax.ShapeDtypeStruct((2 * feature_here, cand_side), jnp.bfloat16),
            jax.ShapeDtypeStruct((column, own, packed_width), jnp.bfloat16),
        ],
        compiler_params=pltpu.CompilerParams(vmem_limit_bytes=32 * 1024 * 1024),
        cost_estimate=pl.CostEstimate(
            flops=cand_side * columns, bytes_accessed=8 * cand_side * columns, transcendentals=0
        ),
    )(mine, arrived, w_slice, *ready)


def attend_kernel(scale, *refs):
    queries, keys_a, keys_b, values_a, values_b, bias_a, bias_b, live_a, live_b = refs[:9]
    summed = refs[-3]
    head = pl.program_id(0)
    head_queries = queries[...].T
    total = None
    for keys, values, bias, live in (
        (keys_a, values_a, bias_a, live_a),
        (keys_b, values_b, bias_b, live_b),
    ):
        scores = lax.dot_general(
            head_queries, keys[...], (((1,), (1,)), ((), ())), preferred_element_type=jnp.float32
        )
        weights = silu(scores * scale + bias[pl.ds(head, 1), :])
        weights = jnp.where(live[...] > 0.0, weights, 0.0).astype(jnp.bfloat16)
        part = jnp.dot(weights, values[...], preferred_element_type=jnp.float32)
        total = part if total is None else total + part
    summed[...] = total.astype(summed.dtype)


def attend(queries, keys, values, bias, live, head_count, through):
    width, cand = queries.shape
    events = keys[0].shape[0]
    head_size = width // head_count
    event_spec = pl.BlockSpec((events, head_size), lambda h: (0, h))
    bias_spec = pl.BlockSpec((head_count, events), lambda h: (0, 0))
    live_spec = pl.BlockSpec((1, events), lambda h: (0, 0))
    held = pl.BlockSpec(memory_space=pl.ANY)
    return pl.pallas_call(
        lambda *refs: attend_kernel(head_size ** (-0.5), *refs),
        grid=(head_count,),
        in_specs=[pl.BlockSpec((head_size, cand), lambda h: (h, 0))]
        + [event_spec] * 4
        + [bias_spec] * 2
        + [live_spec] * 2
        + [held] * 2,
        out_specs=[pl.BlockSpec((cand, head_size), lambda h: (0, h)), held, held],
        out_shape=[jax.ShapeDtypeStruct((cand, width), jnp.bfloat16)]
        + [jax.ShapeDtypeStruct(array.shape, array.dtype) for array in through],
        input_output_aliases={9: 1, 10: 2},
        compiler_params=pltpu.CompilerParams(vmem_limit_bytes=32 * 1024 * 1024),
        cost_estimate=pl.CostEstimate(
            flops=8 * cand * events * width,
            bytes_accessed=8 * events * width + 4 * cand * width,
            transcendentals=2 * cand * events * head_count,
        ),
    )(queries, *keys, *values, *bias, *live, *through)


def finish_kernel(numbers, parts, self_term, gate, embedded, weights_a, weights_b, scored):
    history_sum = parts[0].astype(jnp.float32)
    for part in range(1, parts.shape[0]):
        history_sum = history_sum + parts[part].astype(jnp.float32)
    length = jnp.full((1, 1), numbers[0], jnp.int32).astype(jnp.float32)
    attended = history_sum * lax.rsqrt(length) + self_term[...]
    centre = jnp.mean(attended, axis=1, keepdims=True)
    spread = jnp.mean((attended - centre) ** 2, axis=1, keepdims=True)
    normed = (attended - centre) * lax.rsqrt(spread + 1e-05) * gate[...]
    normed = normed.astype(jnp.bfloat16)
    row_count, _, lanes = weights_a.shape
    row, core = numbers[1], numbers[2]
    for weights, owner in ((weights_a, core), (weights_b, 1 - core)):
        for shift in range(row_count):
            block = owner * row_count + lax.rem(row + row_count - shift, row_count)
            columns = pl.ds(pl.multiple_of(block * lanes, lanes), lanes)
            projected = jnp.dot(normed, weights[shift], preferred_element_type=jnp.float32)
            scored[:, columns] = (
                projected + embedded[:, columns].astype(jnp.float32)
            ).astype(scored.dtype)


def finish(numbers, parts, self_term, gate, embedded, weights_a, weights_b):
    whole = pl.BlockSpec(memory_space=pltpu.VMEM)
    rows, width = embedded.shape
    return pl.pallas_call(
        finish_kernel,
        in_specs=[pl.BlockSpec(memory_space=pltpu.SMEM)] + [whole] * 6,
        out_specs=whole,
        out_shape=jax.ShapeDtypeStruct((rows, width), jnp.bfloat16),
        compiler_params=pltpu.CompilerParams(vmem_limit_bytes=32 * 1024 * 1024),
        cost_estimate=pl.CostEstimate(
            flops=2 * rows * width * width, bytes_accessed=4 * width * width, transcendentals=0
        ),
    )(numbers, parts, self_term, gate, embedded, weights_a, weights_b)


def local(
    history_keys, history_values, lengths, item_ids, item_table, w_proj, rab, norm_gain, w_out
):
    device_count = lax.axis_size("seq")
    column = device_count // 2
    index_here = lax.axis_index("seq")
    place, side = index_here // 2, index_here % 2
    batch_here = lax.axis_index("batch")
    row, core = batch_here // 4, batch_here % 2
    row_count = lax.axis_size("batch") // 4
    events_here, width = history_keys.shape
    head_count = rab.shape[0]
    head_size = width // head_count
    scale = head_size ** (-0.5)
    table_rows = item_table.shape[0]
    cand_total = item_ids.shape[0]
    cand_here = cand_total // device_count
    cand_side = cand_total // 2
    feature_here = w_proj.shape[2]
    out_lanes = width // (2 * row_count)
    length = lengths[0]

    by_side = jnp.arange(cand_total, dtype=jnp.int32).reshape(column, 2, cand_here)
    by_side = by_side.transpose(1, 0, 2).reshape(2, cand_side)
    ids = item_ids.reshape(column, 2, cand_here).transpose(1, 0, 2).reshape(2, cand_side)
    order = jnp.where(side == 0, by_side, by_side[::-1]).reshape(cand_total)
    ids = jnp.where(side == 0, ids, ids[::-1]).reshape(cand_total)
    shard = ids // table_rows
    row_there = ids - shard * table_rows
    same = shard[:, None] == shard[None, :]
    rank = jnp.sum((same & (order[None, :] < order[:, None])).astype(jnp.int32), axis=1)
    most = jnp.max(rank) + 1

    w_mine = w_proj.reshape(width, 4 * feature_here)
    w_other = swap_pair(w_mine)
    w_pair = jnp.concatenate(
        [jnp.where(side == 0, w_mine, w_other), jnp.where(side == 0, w_other, w_mine)], axis=1
    )
    keys = (history_keys, swap_pair(history_keys))
    values = (history_values, swap_pair(history_values))
    w_slice = lax.dynamic_slice_in_dim(w_out, (core * row_count + row) * out_lanes, out_lanes, 1)

    def lookup(first_rank):
        slot = rank - first_rank
        slots_here = jnp.arange(slot_rows, dtype=jnp.int32)
        taken = (shard == index_here)[:, None] & (slot[:, None] == slots_here[None, :])
        slot_row = jnp.sum(jnp.where(taken, row_there[:, None], 0), axis=0)
        picks = (
            slot_row[:, None] == jnp.arange(table_rows, dtype=jnp.int32)[None, :]
        ).astype(jnp.bfloat16)
        packed = jnp.dot(picks, item_table, preferred_element_type=jnp.float32)
        rows = gather_slots(packed.astype(jnp.bfloat16))
        inside = (shard % 2 == side) & (slot >= 0) & (slot < slot_rows)
        source = shard // 2
        ahead = (source - place) % near_places
        piece = jnp.where(ahead == 0, 0, jnp.where(ahead == near_places - 1, 1, ahead + 1))
        block = piece * (column // near_places) + source // near_places
        at = jnp.where(inside, block * slot_rows + slot, -1)
        at_pair = lax.dynamic_slice_in_dim(
            at.reshape(2, cand_side), place * cand_here, cand_here, 1
        )
        return tuple(
            project(at.reshape(cand_total, 1), at_pair.reshape(2 * cand_here, 1), rows, w_pair)
        )

    def another(state):
        first_rank, found = state
        more = lookup(first_rank)
        return first_rank + slot_rows, tuple(a + b for a, b in zip(found, more))

    _, (proj_mine, proj_other, own_rows, other_rows) = lax.while_loop(
        lambda state: state[0] < most, another, (jnp.int32(slot_rows), lookup(jnp.int32(0)))
    )
    side_queries, packed = pack(
        proj_mine, swap_pair(proj_other), w_slice, (keys[1], values[1]), feature_here, cand_here
    )
    received = exchange(packed, column_groups())
    all_queries = lax.all_gather(
        side_queries, "seq", axis=0, tiled=True, axis_index_groups=column_groups()
    )

    def bias_of(index):
        positions = index * events_here + jnp.arange(events_here, dtype=jnp.int32)
        return (
            bucket_bias(rab, length - positions),
            (positions < length).astype(jnp.float32)[None, :],
        )

    bias, live = zip(bias_of(index_here), bias_of(index_here + 1 - 2 * side))
    summed, received, other_rows = attend(
        all_queries, keys, values, bias, live, head_count, (received, other_rows)
    )
    parts = exchange(summed.reshape(column, cand_here, width), column_groups())
    embedded = own_rows + swap_pair(other_rows)

    own_proj = (
        received[:, :, : 8 * feature_here]
        .reshape(column, cand_here, 2, 4, feature_here)
        .transpose(3, 1, 0, 2, 4)
        .reshape(4, cand_here, width)
        .astype(jnp.float32)
    )
    gate_u, own_v, own_queries, own_k = own_proj[0], own_proj[1], own_proj[2], own_proj[3]
    self_scores = jnp.sum((own_queries * own_k).reshape(cand_here, head_count, head_size), axis=2)
    self_scores = self_scores * scale + rab[:, 0][None, :]
    self_term = jax.nn.silu(self_scores)[:, :, None] * own_v.reshape(
        cand_here, head_count, head_size
    )
    self_term = self_term.reshape(cand_here, width)
    gate = norm_gain[None, :] * gate_u

    w_here = (
        received[:, :, 8 * feature_here :]
        .reshape(column, cand_here, -1, out_lanes)
        .transpose(0, 2, 1, 3)
        .reshape(column, 1, -1, out_lanes)
    )
    w_rows = jnp.stack(
        [w_here] + [from_row(w_here, shift) for shift in range(1, row_count)], axis=0
    )
    w_far = swap_pair(w_rows)
    w_rows = jnp.concatenate(
        [jnp.where(side == 0, w_rows, w_far), jnp.where(side == 0, w_far, w_rows)], axis=2
    ).reshape(row_count, width, out_lanes)
    w_core = swap_core(w_rows)
    numbers = jnp.stack([length, row, core])
    return finish(numbers, parts, self_term, gate, embedded, w_rows, w_core)


def solution(mesh):
    return jax.shard_map(
        local,
        mesh=mesh,
        in_specs=(
            P(("batch", "seq"), None),
            P(("batch", "seq"), None),
            P("batch"),
            P("batch"),
            P("seq", None),
            P(None, None, "seq"),
            P(),
            P(),
            P("seq", None),
        ),
        out_specs=P(("batch", "seq"), None),
        check_vma=False,
    )
```

time: 208 us -> 188 us (0.904)
  the two profiles are of different devices: /device:TPU:16 before, /device:TPU:6 now
where the time goes in v2:
time: 188 us; the launch traced here: 187 us
  starting transfers between devices  76.7 us (41%)
  waiting for transfers between devices  43.2 us (23%)
  blocking collectives  37 us (20%)
  local copies, waits for them, and re-layouts  11.7 us (6%)
  Pallas kernels  10.3 us (5%)
  other arithmetic  5.37 us (3%)
    all_gather x1, blocking collectives, local(): lax.all_gather(side_queries, 'seq', axis=0, tiled=True, axis_index_groups...  37 us
    all_to_all x3, starting transfers between devices, exchange(): lax.all_to_all(blocks, 'seq', split_axis=0, concat_axis=0, tiled=True, ax...  31.1 us
    all_to_all x3, waiting for transfers between devices, exchange(): lax.all_to_all(blocks, 'seq', split_axis=0, concat_axis=0, tiled=True, ax...  20.9 us
    ppermute x6, starting transfers between devices, swap_pair(): lax.ppermute(block, 'seq', [(i, i ^ 1) for i in range(lax.axis_size('seq'...  17.5 us
    ppermute x6, waiting for transfers between devices, swap_pair(): lax.ppermute(block, 'seq', [(i, i ^ 1) for i in range(lax.axis_size('seq'...  16.1 us
    ppermute x4, starting transfers between devices, from_place(): lax.ppermute(block, 'seq', [(i, (i + 2 * shift) % count) for i in range(c...  15.8 us
    ppermute x3, starting transfers between devices, from_row(): lax.ppermute(block, 'batch', [(i, (i + 4 * shift) % count) for i in range...  10.3 us
    pallas_call x1, Pallas kernels, attend(): pl.pallas_call(lambda *refs: attend_kernel(head_size ** (-0.5), *refs), g...  5.26 us
  transfers between devices with their start and end apart: 17, of which 9 were waited for; matrix products, arithmetic and copies ran while one was open for 7% of the time, Pallas kernels for 1%

profile of v2, /device:TPU:6, one launch (start us, length us, event | category | flops | bytes accessed | tf_op | source)
XLA Modules:
  0.0 186.6 jit_solution(12843941652576992480)
XLA Ops:
  0.0 1.2 copy.131
  1.2 2.7 %collective-permute-start.8 = (bf16[1024,128]{1,0:T(8,128)(2,1)S(1)}, bf16[1024,128]{1,0:T(8,128)(2,1)S(1)}, u32[]{:S(2)}, u32[]{:S(2)}) collective-permute-start(bf16[1024,128]{1,0:T(8,128)(2,1)S(1)} %copy.131), channel_id=1, source_target_pairs={{0,1},{1,0},{2,3},{3,2},{4,5},{5,4},{6,7},{7,6},{8,9},{9,8},{10,11... | collective-permute-start | bytes 786440 | tf_op jit(solution)/shard_map/ppermute | solution.py:32
  4.0 0.8 reshape.803
  4.9 0.6 fusion.59
  6.0 0.3 convert_reduce_fusion
  7.0 0.7 broadcast_in_dim.71
  7.8 15.1 %all-to-all-start.1 = ((bf16[4,32,1024]{2,1,0:T(8,128)(2,1)}), bf16[4,32,1024]{2,1,0:T(8,128)(2,1)S(1)}, u32[]{:S(2)}, u32[]{:S(2)}) async-start(bf16[4,32,1024]{2,1,0:T(8,128)(2,1)} %broadcast_in_dim.71), calls=%async_computation.1 | async-start | bytes 524288 | tf_op jit(solution)/shard_map/all_to_all | solution.py:17
  22.9 1.5 fusion.57
  24.5 0.6 rem.372
  25.1 0.6 reshape.840
  25.8 0.7 reduce_max.9
  27.1 13.3 %all-to-all-done.1 = bf16[4,32,1024]{2,1,0:T(8,128)(2,1)S(1)} async-done(((bf16[4,32,1024]{2,1,0:T(8,128)(2,1)}), bf16[4,32,1024]{2,1,0:T(8,128)(2,1)S(1)}, u32[]{:S(2)}, u32[]{:S(2)}) %all-to-all-start.1) | async-done | bytes 262176 | tf_op jit(solution)/shard_map/all_to_all | solution.py:17
  40.4 5.9 %collective-permute-start.4 = (bf16[128,1024]{1,0:T(8,128)(2,1)S(1)}, bf16[128,1024]{1,0:T(8,128)(2,1)S(1)}, u32[]{:S(2)}, u32[]{:S(2)}) collective-permute-start(bf16[128,1024]{1,0:T(8,128)(2,1)S(1)} %bitcast.98), channel_id=1, source_target_pairs={{0,2},{1,3},{2,4},{3,5},{4,6},{5,7},{6,8},{7,9},{8,10},{9,11},{10,... | collective-permute-start | bytes 786440 | tf_op jit(solution)/shard_map/ppermute | solution.py:28
  46.4 1.9 %collective-permute-start.5 = (bf16[128,1024]{1,0:T(8,128)(2,1)S(1)}, bf16[128,1024]{1,0:T(8,128)(2,1)S(1)}, u32[]{:S(2)}, u32[]{:S(2)}) collective-permute-start(bf16[128,1024]{1,0:T(8,128)(2,1)S(1)} %bitcast.99), channel_id=1, source_target_pairs={{0,30},{1,31},{2,0},{3,1},{4,2},{5,3},{6,4},{7,5},{8,6},{9,7},{10,... | collective-permute-start | bytes 786440 | tf_op jit(solution)/shard_map/ppermute | solution.py:28
  48.3 4.5 %collective-permute-start.6 = (bf16[64,1024]{1,0:T(8,128)(2,1)S(1)}, bf16[64,1024]{1,0:T(8,128)(2,1)S(1)}, u32[]{:S(2)}, u32[]{:S(2)}) collective-permute-start(bf16[64,1024]{1,0:T(8,128)(2,1)S(1)} %bitcast.122), channel_id=1, source_target_pairs={{0,4},{1,5},{2,6},{3,7},{4,8},{5,9},{6,10},{7,11},{8,12},{9,13},{1... | collective-permute-start | bytes 393224 | tf_op jit(solution)/shard_map/ppermute | solution.py:28
  52.8 3.5 %collective-permute-start.7 = (bf16[64,1024]{1,0:T(8,128)(2,1)S(1)}, bf16[64,1024]{1,0:T(8,128)(2,1)S(1)}, u32[]{:S(2)}, u32[]{:S(2)}) collective-permute-start(bf16[64,1024]{1,0:T(8,128)(2,1)S(1)} %bitcast.121), channel_id=1, source_target_pairs={{0,28},{1,29},{2,30},{3,31},{4,0},{5,1},{6,2},{7,3},{8,4},{9,5},{1... | collective-permute-start | bytes 393224 | tf_op jit(solution)/shard_map/ppermute | solution.py:28
  56.4 1.0 copy-done.1
  57.4 3.1 %collective-permute-start.10 = (bf16[256,1024]{1,0:T(8,128)(2,1)S(1)}, bf16[256,1024]{1,0:T(8,128)(2,1)S(1)}, u32[]{:S(2)}, u32[]{:S(2)}) collective-permute-start(bf16[256,1024]{1,0:T(8,128)(2,1)S(1)} %copy-done.1), channel_id=1, source_target_pairs={{0,1},{1,0},{2,3},{3,2},{4,5},{5,4},{6,7},{7,6},{8,9},{9,8},{10,11... | collective-permute-start | bytes 1572872 | tf_op jit(solution)/shard_map/ppermute | solution.py:32
  60.5 1.1 collective-permute-done.7.rows_4
  61.6 1.5 shard_map.91
  63.1 1.0 copy-done.2
  64.2 3.1 %collective-permute-start.11 = (bf16[256,1024]{1,0:T(8,128)(2,1)S(1)}, bf16[256,1024]{1,0:T(8,128)(2,1)S(1)}, u32[]{:S(2)}, u32[]{:S(2)}) collective-permute-start(bf16[256,1024]{1,0:T(8,128)(2,1)S(1)} %copy-done.2), channel_id=1, source_target_pairs={{0,1},{1,0},{2,3},{3,2},{4,5},{5,4},{6,7},{7,6},{8,9},{9,8},{10,11... | collective-permute-start | bytes 1572872 | tf_op jit(solution)/shard_map/ppermute | solution.py:32
  68.0 2.7 %collective-permute-start.9 = (bf16[256,256]{1,0:T(8,128)(2,1)}, bf16[256,256]{1,0:T(8,128)(2,1)S(1)}, u32[]{:S(2)}, u32[]{:S(2)}) collective-permute-start(bf16[256,256]{1,0:T(8,128)(2,1)} %get-tuple-element.385), channel_id=1, source_target_pairs={{0,1},{1,0},{2,3},{3,2},{4,5},{5,4},{6,7},{7,6},{8,9},{9,8},{10,11... | collective-permute-start | bytes 393224 | tf_op jit(solution)/shard_map/ppermute | solution.py:32
  70.8 3.4 %collective-permute-done.10.refs_3_.refs_2_ = bf16[256,1024]{1,0:T(8,128)(2,1)S(1)} collective-permute-done((bf16[256,1024]{1,0:T(8,128)(2,1)S(1)}, bf16[256,1024]{1,0:T(8,128)(2,1)S(1)}, u32[]{:S(2)}, u32[]{:S(2)}) %collective-permute-start.10) | collective-permute-done | bytes 524320 | tf_op jit(solution)/shard_map/ppermute | solution.py:32
  74.2 9.0 %collective-permute-done.11.refs_4_ = bf16[256,1024]{1,0:T(8,128)(2,1)S(1)} collective-permute-done((bf16[256,1024]{1,0:T(8,128)(2,1)S(1)}, bf16[256,1024]{1,0:T(8,128)(2,1)S(1)}, u32[]{:S(2)}, u32[]{:S(2)}) %collective-permute-start.11) | collective-permute-done | bytes 524320 | tf_op jit(solution)/shard_map/ppermute | solution.py:32
  83.2 1.4 collective-permute-done.9.refs_1_
  84.6 1.7 shard_map.92
  86.3 5.3 %all-to-all-start.2 = ((bf16[16,16,512]{2,1,0:T(8,128)(2,1)}), bf16[16,16,512]{2,1,0:T(8,128)(2,1)S(1)}, u32[]{:S(2)}, u32[]{:S(2)}) async-start(bf16[16,16,512]{2,1,0:T(8,128)(2,1)} %get-tuple-element.387), calls=%async_computation.2 | async-start | bytes 524288 | tf_op jit(solution)/shard_map/all_to_all | solution.py:17
  91.7 0.6 copy-done.20
  92.5 37.0 %all_gather.3.refs_0_ = bf16[1024,256]{1,0:T(8,128)(2,1)S(1)} all-gather(bf16[64,256]{1,0:T(8,128)(2,1)S(1)} %get-tuple-element.386), channel_id=1, replica_groups={{0,2,4,6,8,10,12,14,16,18,20,22,24,26,28,30},{1,3,5,7,9,11,13,15,17,19,..., dimensions={0}, use_global_device_ids=true | all-gather | bytes 557056 | tf_op jit(solution)/shard_map/all_gather | solution.py:329
  129.6 5.3 %shard_map.93 = (bf16[256,1024]{1,0:T(8,128)(2,1)}, bf16[16,16,512]{2,1,0:T(8,128)(2,1)S(1)}, bf16[16,1024]{1,0:T(8,128)(2,1)S(1)}) custom-call(bf16[1024,256]{1,0:T(8,128)(2,1)S(1)} %all_gather.3.refs_0_, bf16[256,1024]{1,0:T(8,128)(2,1)S(1)} %copy-done.1, ...), custom_call_target="tpu_custom_call", output_to_operand_aliasing={{1}: (9, {}), {2}: (10, {})} | custom-call | flops 536870912 | bytes 3145728 | tf_op jit(solution)/shard_map/pallas_call | solution.py:194
  134.9 4.9 %collective-permute-start.15 = (bf16[16,1,32,128]{3,2,0,1:T(8,128)(2,1)S(1)}, bf16[16,1,32,128]{3,2,0,1:T(8,128)(2,1)S(1)}, u32[]{:S(2)}, u32[]{:S(2)}) collective-permute-start(bf16[16,1,32,128]{3,2,0,1:T(8,128)(2,1)S(1)} %bitcast.104), channel_id=1, source_target_pairs={{0,384},{32,416},{64,448},{96,480},{128,0},{160,32},{192,64},{224,... | collective-permute-start | bytes 393224 | tf_op jit(solution)/shard_map/ppermute | solution.py:41
  139.9 2.5 %collective-permute-start.14 = (bf16[16,1,32,128]{3,2,0,1:T(8,128)(2,1)S(1)}, bf16[16,1,32,128]{3,2,0,1:T(8,128)(2,1)S(1)}, u32[]{:S(2)}, u32[]{:S(2)}) collective-permute-start(bf16[16,1,32,128]{3,2,0,1:T(8,128)(2,1)S(1)} %bitcast.105), channel_id=1, source_target_pairs={{0,256},{32,288},{64,320},{96,352},{128,384},{160,416},{192,448},{... | collective-permute-start | bytes 393224 | tf_op jit(solution)/shard_map/ppermute | solution.py:41
  142.4 2.9 %collective-permute-start.13 = (bf16[16,1,32,128]{3,2,0,1:T(8,128)(2,1)S(1)}, bf16[16,1,32,128]{3,2,0,1:T(8,128)(2,1)S(1)}, u32[]{:S(2)}, u32[]{:S(2)}) collective-permute-start(bf16[16,1,32,128]{3,2,0,1:T(8,128)(2,1)S(1)} %bitcast.106), channel_id=1, source_target_pairs={{0,128},{32,160},{64,192},{96,224},{128,256},{160,288},{192,320},{... | collective-permute-start | bytes 393224 | tf_op jit(solution)/shard_map/ppermute | solution.py:41
  145.3 2.9 %collective-permute-done.14 = bf16[16,1,32,128]{3,2,0,1:T(8,128)(2,1)S(1)} collective-permute-done((bf16[16,1,32,128]{3,2,0,1:T(8,128)(2,1)S(1)}, bf16[16,1,32,128]{3,2,0,1:T(8,128)(2,1)S(1)}, u32[]{:S(2)}, u32[]{:S(2)}) %collective-permute-start.14) | collective-permute-done | bytes 131104 | tf_op jit(solution)/shard_map/ppermute | solution.py:41
  148.2 2.3 %collective-permute-done.13 = bf16[16,1,32,128]{3,2,0,1:T(8,128)(2,1)S(1)} collective-permute-done((bf16[16,1,32,128]{3,2,0,1:T(8,128)(2,1)S(1)}, bf16[16,1,32,128]{3,2,0,1:T(8,128)(2,1)S(1)}, u32[]{:S(2)}, u32[]{:S(2)}) %collective-permute-start.13) | collective-permute-done | bytes 131104 | tf_op jit(solution)/shard_map/ppermute | solution.py:41
  150.5 3.1 %collective-permute-start.16 = (bf16[4,16,1,32,128]{4,3,2,1,0:T(8,128)(2,1)S(1)}, bf16[4,16,1,32,128]{4,3,2,1,0:T(8,128)(2,1)S(1)}, u32[]{:S(2)}, u32[]{:S(2)}) collective-permute-start(bf16[4,16,1,32,128]{4,3,2,1,0:T(8,128)(2,1)S(1)} %pad_maximum_fusion.2), channel_id=1, source_target_pairs={{0,1},{1,0},{2,3},{3,2},{4,5},{5,4},{6,7},{7,6},{8,9},{9,8},{10,11... | collective-permute-start | bytes 1572872 | tf_op jit(solution)/shard_map/ppermute | solution.py:32
  153.7 10.7 %all-to-all-start.3 = ((bf16[16,16,1024]{2,1,0:T(8,128)(2,1)}), bf16[16,16,1024]{2,1,0:T(8,128)(2,1)S(1)}, u32[]{:S(2)}, u32[]{:S(2)}) async-start(bf16[16,16,1024]{2,1,0:T(8,128)(2,1)} %bitcast.16), calls=%async_computation.3 | async-start | bytes 1048576 | tf_op jit(solution)/shard_map/all_to_all | solution.py:17
  164.6 1.9 %collective-permute-start.17 = (bf16[4,1024,128]{2,1,0:T(8,128)(2,1)S(1)}, bf16[4,1024,128]{2,1,0:T(8,128)(2,1)S(1)}, u32[]{:S(2)}, u32[]{:S(2)}) collective-permute-start(bf16[4,1024,128]{2,1,0:T(8,128)(2,1)S(1)} %bitcast.96), channel_id=1, source_target_pairs={{0,32},{32,0},{64,96},{96,64},{128,160},{160,128},{192,224},{224,1... | collective-permute-start | bytes 3145736 | tf_op jit(solution)/shard_map/ppermute | solution.py:36
  166.7 1.5 reshape.821
  168.2 1.8 copy.151
  170.0 0.6 fusion.61
  170.5 0.3 reshape_squeeze.3
  171.5 2.7 %collective-permute-start.12 = (bf16[16,1024]{1,0:T(8,128)(2,1)S(1)}, bf16[16,1024]{1,0:T(8,128)(2,1)S(1)}, u32[]{:S(2)}, u32[]{:S(2)}) collective-permute-start(bf16[16,1024]{1,0:T(8,128)(2,1)S(1)} %get-tuple-element.392), channel_id=1, source_target_pairs={{0,1},{1,0},{2,3},{3,2},{4,5},{5,4},{6,7},{7,6},{8,9},{9,8},{10,11... | collective-permute-start | bytes 98312 | tf_op jit(solution)/shard_map/ppermute | solution.py:32
  174.3 0.7 copy-done.21
  175.0 2.3 %collective-permute-done.12 = bf16[16,1024]{1,0:T(8,128)(2,1)S(1)} collective-permute-done((bf16[16,1024]{1,0:T(8,128)(2,1)S(1)}, bf16[16,1024]{1,0:T(8,128)(2,1)S(1)}, u32[]{:S(2)}, u32[]{:S(2)}) %collective-permute-start.12) | collective-permute-done | bytes 32800 | tf_op jit(solution)/shard_map/ppermute | solution.py:32
  177.3 7.6 %all-to-all-done.3.parts = bf16[16,16,1024]{2,1,0:T(8,128)(2,1)S(1)} async-done(((bf16[16,16,1024]{2,1,0:T(8,128)(2,1)}), bf16[16,16,1024]{2,1,0:T(8,128)(2,1)S(1)}, u32[]{:S(2)}, u32[]{:S(2)}) %all-to-all-start.3) | async-done | bytes 524320 | tf_op jit(solution)/shard_map/all_to_all | solution.py:17
  184.9 1.8 shard_map.94
  (73 shorter events, 3.2 us)
Async XLA Ops:
  0.0 70.8 %copy-start = (bf16[32,1024]{1,0:T(8,128)(2,1)S(1)}, bf16[32,1024]{1,0:T(8,128)(2,1)}, u32[]{:S(2)}) copy-start(bf16[32,1024]{1,0:T(8,128)(2,1)} %param.19) | copy-start | bytes 196612
  0.0 6.7 %copy-start.3 = (bf16[512,1024]{1,0:T(8,128)(2,1)S(1)}, bf16[512,1024]{1,0:T(8,128)(2,1)}, u32[]{:S(2)}) copy-start(bf16[512,1024]{1,0:T(8,128)(2,1)} %param.15) | copy-start | bytes 3145732
  1.2 55.1 %collective-permute-start.8 = (bf16[1024,128]{1,0:T(8,128)(2,1)S(1)}, bf16[1024,128]{1,0:T(8,128)(2,1)S(1)}, u32[]{:S(2)}, u32[]{:S(2)}) collective-permute-start(bf16[1024,128]{1,0:T(8,128)(2,1)S(1)} %copy.131), channel_id=1, source_target_pairs={{0,1},{1,0},{2,3},{3,2},{4,5},{5,4},{6,7},{7,6},{8,9},{9,8},{10,11... | collective-permute-start | bytes 786440 | tf_op jit(solution)/shard_map/ppermute | solution.py:32
  7.8 32.7 %all-to-all-start.1 = ((bf16[4,32,1024]{2,1,0:T(8,128)(2,1)}), bf16[4,32,1024]{2,1,0:T(8,128)(2,1)S(1)}, u32[]{:S(2)}, u32[]{:S(2)}) async-start(bf16[4,32,1024]{2,1,0:T(8,128)(2,1)} %broadcast_in_dim.71), calls=%async_computation.1 | async-start | bytes 524288 | tf_op jit(solution)/shard_map/all_to_all | solution.py:17
  40.4 21.1 %collective-permute-start.4 = (bf16[128,1024]{1,0:T(8,128)(2,1)S(1)}, bf16[128,1024]{1,0:T(8,128)(2,1)S(1)}, u32[]{:S(2)}, u32[]{:S(2)}) collective-permute-start(bf16[128,1024]{1,0:T(8,128)(2,1)S(1)} %bitcast.98), channel_id=1, source_target_pairs={{0,2},{1,3},{2,4},{3,5},{4,6},{5,7},{6,8},{7,9},{8,10},{9,11},{10,... | collective-permute-start | bytes 786440 | tf_op jit(solution)/shard_map/ppermute | solution.py:28
  46.4 15.2 %collective-permute-start.5 = (bf16[128,1024]{1,0:T(8,128)(2,1)S(1)}, bf16[128,1024]{1,0:T(8,128)(2,1)S(1)}, u32[]{:S(2)}, u32[]{:S(2)}) collective-permute-start(bf16[128,1024]{1,0:T(8,128)(2,1)S(1)} %bitcast.99), channel_id=1, source_target_pairs={{0,30},{1,31},{2,0},{3,1},{4,2},{5,3},{6,4},{7,5},{8,6},{9,7},{10,... | collective-permute-start | bytes 786440 | tf_op jit(solution)/shard_map/ppermute | solution.py:28
  48.3 12.2 %collective-permute-start.6 = (bf16[64,1024]{1,0:T(8,128)(2,1)S(1)}, bf16[64,1024]{1,0:T(8,128)(2,1)S(1)}, u32[]{:S(2)}, u32[]{:S(2)}) collective-permute-start(bf16[64,1024]{1,0:T(8,128)(2,1)S(1)} %bitcast.122), channel_id=1, source_target_pairs={{0,4},{1,5},{2,6},{3,7},{4,8},{5,9},{6,10},{7,11},{8,12},{9,13},{1... | collective-permute-start | bytes 393224 | tf_op jit(solution)/shard_map/ppermute | solution.py:28
  52.8 8.8 %collective-permute-start.7 = (bf16[64,1024]{1,0:T(8,128)(2,1)S(1)}, bf16[64,1024]{1,0:T(8,128)(2,1)S(1)}, u32[]{:S(2)}, u32[]{:S(2)}) collective-permute-start(bf16[64,1024]{1,0:T(8,128)(2,1)S(1)} %bitcast.121), channel_id=1, source_target_pairs={{0,28},{1,29},{2,30},{3,31},{4,0},{5,1},{6,2},{7,3},{8,4},{9,5},{1... | collective-permute-start | bytes 393224 | tf_op jit(solution)/shard_map/ppermute | solution.py:28
  56.4 1.0 copy-start.1
  57.4 5.7 %copy-start.4 = (bf16[1024,256]{1,0:T(8,128)(2,1)}, bf16[1024,256]{1,0:T(8,128)(2,1)S(1)}, u32[]{:S(2)}) copy-start(bf16[1024,256]{1,0:T(8,128)(2,1)S(1)} %pad_maximum_fusion.1.weights) | copy-start | bytes 1572868
  57.4 16.7 %collective-permute-start.10 = (bf16[256,1024]{1,0:T(8,128)(2,1)S(1)}, bf16[256,1024]{1,0:T(8,128)(2,1)S(1)}, u32[]{:S(2)}, u32[]{:S(2)}) collective-permute-start(bf16[256,1024]{1,0:T(8,128)(2,1)S(1)} %copy-done.1), channel_id=1, source_target_pairs={{0,1},{1,0},{2,3},{3,2},{4,5},{5,4},{6,7},{7,6},{8,9},{9,8},{10,11... | collective-permute-start | bytes 1572872 | tf_op jit(solution)/shard_map/ppermute | solution.py:32
  63.1 1.0 copy-start.2
  64.2 19.0 %collective-permute-start.11 = (bf16[256,1024]{1,0:T(8,128)(2,1)S(1)}, bf16[256,1024]{1,0:T(8,128)(2,1)S(1)}, u32[]{:S(2)}, u32[]{:S(2)}) collective-permute-start(bf16[256,1024]{1,0:T(8,128)(2,1)S(1)} %copy-done.2), channel_id=1, source_target_pairs={{0,1},{1,0},{2,3},{3,2},{4,5},{5,4},{6,7},{7,6},{8,9},{9,8},{10,11... | collective-permute-start | bytes 1572872 | tf_op jit(solution)/shard_map/ppermute | solution.py:32
  68.0 16.6 %collective-permute-start.9 = (bf16[256,256]{1,0:T(8,128)(2,1)}, bf16[256,256]{1,0:T(8,128)(2,1)S(1)}, u32[]{:S(2)}, u32[]{:S(2)}) collective-permute-start(bf16[256,256]{1,0:T(8,128)(2,1)} %get-tuple-element.385), channel_id=1, source_target_pairs={{0,1},{1,0},{2,3},{3,2},{4,5},{5,4},{6,7},{7,6},{8,9},{9,8},{10,11... | collective-permute-start | bytes 393224 | tf_op jit(solution)/shard_map/ppermute | solution.py:32
  86.3 43.3 %all-to-all-start.2 = ((bf16[16,16,512]{2,1,0:T(8,128)(2,1)}), bf16[16,16,512]{2,1,0:T(8,128)(2,1)S(1)}, u32[]{:S(2)}, u32[]{:S(2)}) async-start(bf16[16,16,512]{2,1,0:T(8,128)(2,1)} %get-tuple-element.387), calls=%async_computation.2 | async-start | bytes 524288 | tf_op jit(solution)/shard_map/all_to_all | solution.py:17
  91.6 0.7 copy-start.20
  134.9 10.4 %collective-permute-start.15 = (bf16[16,1,32,128]{3,2,0,1:T(8,128)(2,1)S(1)}, bf16[16,1,32,128]{3,2,0,1:T(8,128)(2,1)S(1)}, u32[]{:S(2)}, u32[]{:S(2)}) collective-permute-start(bf16[16,1,32,128]{3,2,0,1:T(8,128)(2,1)S(1)} %bitcast.104), channel_id=1, source_target_pairs={{0,384},{32,416},{64,448},{96,480},{128,0},{160,32},{192,64},{224,... | collective-permute-start | bytes 393224 | tf_op jit(solution)/shard_map/ppermute | solution.py:41
  139.9 8.4 %collective-permute-start.14 = (bf16[16,1,32,128]{3,2,0,1:T(8,128)(2,1)S(1)}, bf16[16,1,32,128]{3,2,0,1:T(8,128)(2,1)S(1)}, u32[]{:S(2)}, u32[]{:S(2)}) collective-permute-start(bf16[16,1,32,128]{3,2,0,1:T(8,128)(2,1)S(1)} %bitcast.105), channel_id=1, source_target_pairs={{0,256},{32,288},{64,320},{96,352},{128,384},{160,416},{192,448},{... | collective-permute-start | bytes 393224 | tf_op jit(solution)/shard_map/ppermute | solution.py:41
  142.4 8.1 %collective-permute-start.13 = (bf16[16,1,32,128]{3,2,0,1:T(8,128)(2,1)S(1)}, bf16[16,1,32,128]{3,2,0,1:T(8,128)(2,1)S(1)}, u32[]{:S(2)}, u32[]{:S(2)}) collective-permute-start(bf16[16,1,32,128]{3,2,0,1:T(8,128)(2,1)S(1)} %bitcast.106), channel_id=1, source_target_pairs={{0,128},{32,160},{64,192},{96,224},{128,256},{160,288},{192,320},{... | collective-permute-start | bytes 393224 | tf_op jit(solution)/shard_map/ppermute | solution.py:41
  150.5 13.9 %collective-permute-start.16 = (bf16[4,16,1,32,128]{4,3,2,1,0:T(8,128)(2,1)S(1)}, bf16[4,16,1,32,128]{4,3,2,1,0:T(8,128)(2,1)S(1)}, u32[]{:S(2)}, u32[]{:S(2)}) collective-permute-start(bf16[4,16,1,32,128]{4,3,2,1,0:T(8,128)(2,1)S(1)} %pad_maximum_fusion.2), channel_id=1, source_target_pairs={{0,1},{1,0},{2,3},{3,2},{4,5},{5,4},{6,7},{7,6},{8,9},{9,8},{10,11... | collective-permute-start | bytes 1572872 | tf_op jit(solution)/shard_map/ppermute | solution.py:32
  153.7 31.2 %all-to-all-start.3 = ((bf16[16,16,1024]{2,1,0:T(8,128)(2,1)}), bf16[16,16,1024]{2,1,0:T(8,128)(2,1)S(1)}, u32[]{:S(2)}, u32[]{:S(2)}) async-start(bf16[16,16,1024]{2,1,0:T(8,128)(2,1)} %bitcast.16), calls=%async_computation.3 | async-start | bytes 1048576 | tf_op jit(solution)/shard_map/all_to_all | solution.py:17
  164.6 12.7 %collective-permute-start.17 = (bf16[4,1024,128]{2,1,0:T(8,128)(2,1)S(1)}, bf16[4,1024,128]{2,1,0:T(8,128)(2,1)S(1)}, u32[]{:S(2)}, u32[]{:S(2)}) collective-permute-start(bf16[4,1024,128]{2,1,0:T(8,128)(2,1)S(1)} %bitcast.96), channel_id=1, source_target_pairs={{0,32},{32,0},{64,96},{96,64},{128,160},{160,128},{192,224},{224,1... | collective-permute-start | bytes 3145736 | tf_op jit(solution)/shard_map/ppermute | solution.py:36
  171.5 5.8 %collective-permute-start.12 = (bf16[16,1024]{1,0:T(8,128)(2,1)S(1)}, bf16[16,1024]{1,0:T(8,128)(2,1)S(1)}, u32[]{:S(2)}, u32[]{:S(2)}) collective-permute-start(bf16[16,1024]{1,0:T(8,128)(2,1)S(1)} %get-tuple-element.392), channel_id=1, source_target_pairs={{0,1},{1,0},{2,3},{3,2},{4,5},{5,4},{6,7},{7,6},{8,9},{9,8},{10,11... | collective-permute-start | bytes 98312 | tf_op jit(solution)/shard_map/ppermute | solution.py:32
  174.3 0.7 copy-start.21

commit v3 on v2

--- a/solution.py
+++ b/solution.py
@@ -32,13 +32,11 @@
     return lax.ppermute(block, "seq", [(i, i ^ 1) for i in range(lax.axis_size("seq"))])
 
 
-def swap_core(block):
-    return lax.ppermute(block, "batch", [(i, i ^ 1) for i in range(lax.axis_size("batch"))])
-
-
-def from_row(block, shift):
+def from_replica(block, rows, cores):
     count = lax.axis_size("batch")
-    return lax.ppermute(block, "batch", [(i, (i + 4 * shift) % count) for i in range(count)])
+    return lax.ppermute(
+        block, "batch", [(i, ((i + 4 * rows) % count) ^ cores) for i in range(count)]
+    )
 
 
 def gather_slots(block):
@@ -71,6 +69,49 @@
 
 def silu(value):
     return value * (0.5 + 0.5 * jnp.tanh(0.5 * value))
+
+
+def pick_kernel(numbers, ids, table, packed):
+    rows, count = table.shape[0], ids.shape[1]
+    there = ids[...] - numbers[0] * rows
+    here = (there >= 0) & (there < rows)
+    before = lax.broadcasted_iota(jnp.int32, (count, count), 0) < lax.broadcasted_iota(
+        jnp.int32, (count, count), 1
+    )
+    marks = jnp.broadcast_to(here.astype(jnp.float32), (8, count)).astype(jnp.bfloat16)
+    rank = jnp.dot(
+        marks,
+        before.astype(jnp.float32).astype(jnp.bfloat16),
+        preferred_element_type=jnp.float32,
+    )[:1].astype(jnp.int32)
+    slot = jnp.where(here, rank - numbers[1], -1)
+    taken = slot == lax.broadcasted_iota(jnp.int32, (packed.shape[0], count), 0)
+    wanted = there == lax.broadcasted_iota(jnp.int32, (rows, count), 0)
+    picks = lax.dot_general(
+        taken.astype(jnp.float32).astype(jnp.bfloat16),
+        wanted.astype(jnp.float32).astype(jnp.bfloat16),
+        (((1,), (1,)), ((), ())),
+        preferred_element_type=jnp.float32,
+    ).astype(jnp.bfloat16)
+    packed[...] = jnp.dot(picks, table[...], preferred_element_type=jnp.float32).astype(
+        jnp.bfloat16
+    )
+
+
+def pick(numbers, ids, table):
+    whole = pl.BlockSpec(memory_space=pltpu.VMEM)
+    return pl.pallas_call(
+        pick_kernel,
+        in_specs=[pl.BlockSpec(memory_space=pltpu.SMEM), whole, whole],
+        out_specs=whole,
+        out_shape=jax.ShapeDtypeStruct((slot_rows, table.shape[1]), jnp.bfloat16),
+        compiler_params=pltpu.CompilerParams(vmem_limit_bytes=32 * 1024 * 1024),
+        cost_estimate=pl.CostEstimate(
+            flops=2 * slot_rows * table.shape[0] * table.shape[1],
+            bytes_accessed=2 * table.shape[0] * table.shape[1],
+            transcendentals=0,
+        ),
+    )(numbers, ids.reshape(1, -1), table)
 
 
 def project_kernel(at, at_pair, rows_0, rows_1, rows_2, rows_3, rows_4, weights, *rest):
@@ -212,7 +253,8 @@
     )(queries, *keys, *values, *bias, *live, *through)
 
 
-def finish_kernel(numbers, parts, self_term, gate, embedded, weights_a, weights_b, scored):
+def finish_kernel(numbers, parts, self_term, gate, embedded, *rest):
+    weights, scored = rest[:-1], rest[-1]
     history_sum = parts[0].astype(jnp.float32)
     for part in range(1, parts.shape[0]):
         history_sum = history_sum + parts[part].astype(jnp.float32)
@@ -222,31 +264,32 @@
     spread = jnp.mean((attended - centre) ** 2, axis=1, keepdims=True)
     normed = (attended - centre) * lax.rsqrt(spread + 1e-05) * gate[...]
     normed = normed.astype(jnp.bfloat16)
-    row_count, _, lanes = weights_a.shape
+    lanes = weights[0].shape[1]
+    row_count = len(weights) // 2
     row, core = numbers[1], numbers[2]
-    for weights, owner in ((weights_a, core), (weights_b, 1 - core)):
-        for shift in range(row_count):
-            block = owner * row_count + lax.rem(row + row_count - shift, row_count)
-            columns = pl.ds(pl.multiple_of(block * lanes, lanes), lanes)
-            projected = jnp.dot(normed, weights[shift], preferred_element_type=jnp.float32)
-            scored[:, columns] = (
-                projected + embedded[:, columns].astype(jnp.float32)
-            ).astype(scored.dtype)
-
-
-def finish(numbers, parts, self_term, gate, embedded, weights_a, weights_b):
+    for index, columns_of in enumerate(weights):
+        owner = core if index < row_count else 1 - core
+        block = owner * row_count + lax.rem(row + row_count - index % row_count, row_count)
+        columns = pl.ds(pl.multiple_of(block * lanes, lanes), lanes)
+        projected = jnp.dot(normed, columns_of[...], preferred_element_type=jnp.float32)
+        scored[:, columns] = (projected + embedded[:, columns].astype(jnp.float32)).astype(
+            scored.dtype
+        )
+
+
+def finish(numbers, parts, self_term, gate, embedded, weights):
     whole = pl.BlockSpec(memory_space=pltpu.VMEM)
     rows, width = embedded.shape
     return pl.pallas_call(
         finish_kernel,
-        in_specs=[pl.BlockSpec(memory_space=pltpu.SMEM)] + [whole] * 6,
+        in_specs=[pl.BlockSpec(memory_space=pltpu.SMEM)] + [whole] * (4 + len(weights)),
         out_specs=whole,
         out_shape=jax.ShapeDtypeStruct((rows, width), jnp.bfloat16),
         compiler_params=pltpu.CompilerParams(vmem_limit_bytes=32 * 1024 * 1024),
         cost_estimate=pl.CostEstimate(
             flops=2 * rows * width * width, bytes_accessed=4 * width * width, transcendentals=0
         ),
-    )(numbers, parts, self_term, gate, embedded, weights_a, weights_b)
+    )(numbers, parts, self_term, gate, embedded, *weights)
 
 
 def local(
@@ -282,25 +325,16 @@
     rank = jnp.sum((same & (order[None, :] < order[:, None])).astype(jnp.int32), axis=1)
     most = jnp.max(rank) + 1
 
-    w_mine = w_proj.reshape(width, 4 * feature_here)
-    w_other = swap_pair(w_mine)
-    w_pair = jnp.concatenate(
-        [jnp.where(side == 0, w_mine, w_other), jnp.where(side == 0, w_other, w_mine)], axis=1
-    )
-    keys = (history_keys, swap_pair(history_keys))
-    values = (history_values, swap_pair(history_values))
     w_slice = lax.dynamic_slice_in_dim(w_out, (core * row_count + row) * out_lanes, out_lanes, 1)
-
-    def lookup(first_rank):
+    slice_rows = w_slice.shape[0]
+
+    def lookup(first_rank, send):
+        packed = pick(jnp.stack([index_here, first_rank]), item_ids, item_table)
+        packed, send = lax.optimization_barrier((packed, send))
+        return gather_slots(packed), [swap_pair(block) for block in send]
+
+    def place_of(first_rank):
         slot = rank - first_rank
-        slots_here = jnp.arange(slot_rows, dtype=jnp.int32)
-        taken = (shard == index_here)[:, None] & (slot[:, None] == slots_here[None, :])
-        slot_row = jnp.sum(jnp.where(taken, row_there[:, None], 0), axis=0)
-        picks = (
-            slot_row[:, None] == jnp.arange(table_rows, dtype=jnp.int32)[None, :]
-        ).astype(jnp.bfloat16)
-        packed = jnp.dot(picks, item_table, preferred_element_type=jnp.float32)
-        rows = gather_slots(packed.astype(jnp.bfloat16))
         inside = (shard % 2 == side) & (slot >= 0) & (slot < slot_rows)
         source = shard // 2
         ahead = (source - place) % near_places
@@ -310,20 +344,35 @@
         at_pair = lax.dynamic_slice_in_dim(
             at.reshape(2, cand_side), place * cand_here, cand_here, 1
         )
-        return tuple(
-            project(at.reshape(cand_total, 1), at_pair.reshape(2 * cand_here, 1), rows, w_pair)
-        )
+        return at.reshape(cand_total, 1), at_pair.reshape(2 * cand_here, 1)
+
+    w_mine = w_proj.reshape(width, 4 * feature_here)
+    w_send = jnp.concatenate([w_mine, w_slice.reshape(-1, 4 * feature_here)])
+    rows, (w_other, keys_other, values_other) = lookup(
+        jnp.int32(0), (w_send, history_keys, history_values)
+    )
+    slice_other = w_other[width:].reshape(w_slice.shape)
+    w_other = w_other[:width]
+    keys, values = (history_keys, keys_other), (history_values, values_other)
+    w_pair = jnp.concatenate(
+        [jnp.where(side == 0, w_mine, w_other), jnp.where(side == 0, w_other, w_mine)], axis=1
+    )
+    slices = jnp.concatenate(
+        [jnp.where(side == 0, w_slice, slice_other), jnp.where(side == 0, slice_other, w_slice)]
+    )
+    found = tuple(project(*place_of(jnp.int32(0)), rows, w_pair))
 
     def another(state):
         first_rank, found = state
-        more = lookup(first_rank)
+        rows, _ = lookup(first_rank, ())
+        more = project(*place_of(first_rank), rows, w_pair)
         return first_rank + slot_rows, tuple(a + b for a, b in zip(found, more))
 
     _, (proj_mine, proj_other, own_rows, other_rows) = lax.while_loop(
-        lambda state: state[0] < most, another, (jnp.int32(slot_rows), lookup(jnp.int32(0)))
+        lambda state: state[0] < most, another, (jnp.int32(slot_rows), found)
     )
     side_queries, packed = pack(
-        proj_mine, swap_pair(proj_other), w_slice, (keys[1], values[1]), feature_here, cand_here
+        proj_mine, swap_pair(proj_other), slices, (keys_other,), feature_here, cand_here
     )
     received = exchange(packed, column_groups())
     all_queries = lax.all_gather(
@@ -362,20 +411,17 @@
 
     w_here = (
         received[:, :, 8 * feature_here :]
-        .reshape(column, cand_here, -1, out_lanes)
+        .reshape(column, cand_here, 2 * slice_rows // cand_here, out_lanes)
         .transpose(0, 2, 1, 3)
-        .reshape(column, 1, -1, out_lanes)
-    )
-    w_rows = jnp.stack(
-        [w_here] + [from_row(w_here, shift) for shift in range(1, row_count)], axis=0
-    )
-    w_far = swap_pair(w_rows)
-    w_rows = jnp.concatenate(
-        [jnp.where(side == 0, w_rows, w_far), jnp.where(side == 0, w_far, w_rows)], axis=2
-    ).reshape(row_count, width, out_lanes)
-    w_core = swap_core(w_rows)
+        .reshape(width, out_lanes)
+    )
+    weights = [
+        from_replica(w_here, rows_before, other) if rows_before or other else w_here
+        for other in range(2)
+        for rows_before in range(row_count)
+    ]
     numbers = jnp.stack([length, row, core])
-    return finish(numbers, parts, self_term, gate, embedded, w_rows, w_core)
+    return finish(numbers, parts, self_term, gate, embedded, weights)
 
 
 def solution(mesh):

time: 188 us -> 190 us (1.011)
  the two profiles are of different devices: /device:TPU:6 before, /device:TPU:1 now
where the time goes in v3:
time: 190 us; the launch traced here: 189 us
  starting transfers between devices  92.8 us (49%)
  blocking collectives  35.5 us (19%)
  waiting for transfers between devices  28.7 us (15%)
  local copies, waits for them, and re-layouts  11.5 us (6%)
  Pallas kernels  10.7 us (6%)
  other arithmetic  7.14 us (4%)
    all_gather x1, blocking collectives, local(): lax.all_gather(side_queries, 'seq', axis=0, tiled=True, axis_index_groups...  35.5 us
    all_to_all x3, starting transfers between devices, exchange(): lax.all_to_all(blocks, 'seq', split_axis=0, concat_axis=0, tiled=True, ax...  31.8 us
    ppermute x7, starting transfers between devices, from_replica(): lax.ppermute(block, 'batch', [(i, (i + 4 * rows) % count ^ cores) for i i...  29.8 us
    ppermute x4, starting transfers between devices, from_place(): lax.ppermute(block, 'seq', [(i, (i + 2 * shift) % count) for i in range(c...  18.3 us
    ppermute x5, starting transfers between devices, swap_pair(): lax.ppermute(block, 'seq', [(i, i ^ 1) for i in range(lax.axis_size('seq'...  13 us
    ppermute x5, waiting for transfers between devices, swap_pair(): lax.ppermute(block, 'seq', [(i, i ^ 1) for i in range(lax.axis_size('seq'...  9.63 us
    all_to_all x3, waiting for transfers between devices, exchange(): lax.all_to_all(blocks, 'seq', split_axis=0, concat_axis=0, tiled=True, ax...  9.49 us
    ppermute x7, waiting for transfers between devices, from_replica(): lax.ppermute(block, 'batch', [(i, (i + 4 * rows) % count ^ cores) for i i...  9 us
  transfers between devices with their start and end apart: 19, of which 7 were waited for; matrix products, arithmetic and copies ran while one was open for 7% of the time, Pallas kernels for 1%

profile of v3, /device:TPU:1, one launch (start us, length us, event | category | flops | bytes accessed | tf_op | source)
XLA Modules:
  0.0 188.5 jit_solution(14797052235659703116)
XLA Ops:
  0.0 1.2 copy.115
  1.3 0.7 constant_dynamic-slice_fusion.17
  2.0 0.6 copy-done.16
  2.7 1.2 shard_map.91
  3.8 3.9 %collective-permute-start.8 = (bf16[1056,128]{1,0:T(8,128)(2,1)S(1)}, bf16[1056,128]{1,0:T(8,128)(2,1)S(1)}, u32[]{:S(2)}, u32[]{:S(2)}) collective-permute-start(bf16[1056,128]{1,0:T(8,128)(2,1)S(1)} %pad_maximum_fusion.1), channel_id=1, source_target_pairs={{0,1},{1,0},{2,3},{3,2},{4,5},{5,4},{6,7},{7,6},{8,9},{9,8},{10,11... | collective-permute-start | bytes 811016 | tf_op jit(solution)/shard_map/ppermute | solution.py:32
  8.1 0.6 fusion.55
  9.2 0.9 convert_reduce_fusion
  10.1 0.7 reduce_sum.49
  10.8 0.8 copy.112
  11.7 0.7 broadcast_in_dim.29
  12.4 14.8 %all-to-all-start.1 = ((bf16[4,32,1024]{2,1,0:T(8,128)(2,1)}), bf16[4,32,1024]{2,1,0:T(8,128)(2,1)S(1)}, u32[]{:S(2)}, u32[]{:S(2)}) async-start(bf16[4,32,1024]{2,1,0:T(8,128)(2,1)} %broadcast_in_dim.29), calls=%async_computation.1 | async-start | bytes 524288 | tf_op jit(solution)/shard_map/all_to_all | solution.py:17
  27.2 1.5 fusion.53
  29.0 1.3 reduce_max.9
  31.0 9.5 %all-to-all-done.1 = bf16[4,32,1024]{2,1,0:T(8,128)(2,1)S(1)} async-done(((bf16[4,32,1024]{2,1,0:T(8,128)(2,1)}), bf16[4,32,1024]{2,1,0:T(8,128)(2,1)S(1)}, u32[]{:S(2)}, u32[]{:S(2)}) %all-to-all-start.1) | async-done | bytes 262176 | tf_op jit(solution)/shard_map/all_to_all | solution.py:17
  40.4 9.0 %collective-permute-start.4 = (bf16[128,1024]{1,0:T(8,128)(2,1)S(1)}, bf16[128,1024]{1,0:T(8,128)(2,1)S(1)}, u32[]{:S(2)}, u32[]{:S(2)}) collective-permute-start(bf16[128,1024]{1,0:T(8,128)(2,1)S(1)} %bitcast.102), channel_id=1, source_target_pairs={{0,2},{1,3},{2,4},{3,5},{4,6},{5,7},{6,8},{7,9},{8,10},{9,11},{10,... | collective-permute-start | bytes 786440 | tf_op jit(solution)/shard_map/ppermute | solution.py:28
  49.4 1.9 %collective-permute-start.5 = (bf16[128,1024]{1,0:T(8,128)(2,1)S(1)}, bf16[128,1024]{1,0:T(8,128)(2,1)S(1)}, u32[]{:S(2)}, u32[]{:S(2)}) collective-permute-start(bf16[128,1024]{1,0:T(8,128)(2,1)S(1)} %bitcast.103), channel_id=1, source_target_pairs={{0,30},{1,31},{2,0},{3,1},{4,2},{5,3},{6,4},{7,5},{8,6},{9,7},{10,... | collective-permute-start | bytes 786440 | tf_op jit(solution)/shard_map/ppermute | solution.py:28
  51.4 3.8 %collective-permute-start.6 = (bf16[64,1024]{1,0:T(8,128)(2,1)S(1)}, bf16[64,1024]{1,0:T(8,128)(2,1)S(1)}, u32[]{:S(2)}, u32[]{:S(2)}) collective-permute-start(bf16[64,1024]{1,0:T(8,128)(2,1)S(1)} %bitcast.121), channel_id=1, source_target_pairs={{0,4},{1,5},{2,6},{3,7},{4,8},{5,9},{6,10},{7,11},{8,12},{9,13},{1... | collective-permute-start | bytes 393224 | tf_op jit(solution)/shard_map/ppermute | solution.py:28
  55.2 3.6 %collective-permute-start.7 = (bf16[64,1024]{1,0:T(8,128)(2,1)S(1)}, bf16[64,1024]{1,0:T(8,128)(2,1)S(1)}, u32[]{:S(2)}, u32[]{:S(2)}) collective-permute-start(bf16[64,1024]{1,0:T(8,128)(2,1)S(1)} %bitcast.120), channel_id=1, source_target_pairs={{0,28},{1,29},{2,30},{3,31},{4,0},{5,1},{6,2},{7,3},{8,4},{9,5},{1... | collective-permute-start | bytes 393224 | tf_op jit(solution)/shard_map/ppermute | solution.py:28
  58.9 0.6 copy-done.13
  59.6 1.0 copy-done
  60.6 2.2 %collective-permute-start.10 = (bf16[256,1024]{1,0:T(8,128)(2,1)S(1)}, bf16[256,1024]{1,0:T(8,128)(2,1)S(1)}, u32[]{:S(2)}, u32[]{:S(2)}) collective-permute-start(bf16[256,1024]{1,0:T(8,128)(2,1)S(1)} %copy-done), channel_id=1, source_target_pairs={{0,1},{1,0},{2,3},{3,2},{4,5},{5,4},{6,7},{7,6},{8,9},{9,8},{10,11... | collective-permute-start | bytes 1572872 | tf_op jit(solution)/shard_map/ppermute | solution.py:32
  63.3 1.7 shard_map.92
  65.0 2.6 %collective-permute-start.9 = (bf16[256,256]{1,0:T(8,128)(2,1)}, bf16[256,256]{1,0:T(8,128)(2,1)S(1)}, u32[]{:S(2)}, u32[]{:S(2)}) collective-permute-start(bf16[256,256]{1,0:T(8,128)(2,1)} %get-tuple-element.832), channel_id=1, source_target_pairs={{0,1},{1,0},{2,3},{3,2},{4,5},{5,4},{6,7},{7,6},{8,9},{9,8},{10,11... | collective-permute-start | bytes 393224 | tf_op jit(solution)/shard_map/ppermute | solution.py:32
  67.6 0.7 broadcast_select_fusion.3
  68.3 4.5 %collective-permute-done.10.refs_3_.refs_2_ = bf16[256,1024]{1,0:T(8,128)(2,1)S(1)} collective-permute-done((bf16[256,1024]{1,0:T(8,128)(2,1)S(1)}, bf16[256,1024]{1,0:T(8,128)(2,1)S(1)}, u32[]{:S(2)}, u32[]{:S(2)}) %collective-permute-start.10) | collective-permute-done | bytes 524320 | tf_op jit(solution)/shard_map/ppermute | solution.py:32
  72.7 2.8 %collective-permute-done.9.refs_1_ = bf16[256,256]{1,0:T(8,128)(2,1)S(1)} collective-permute-done((bf16[256,256]{1,0:T(8,128)(2,1)}, bf16[256,256]{1,0:T(8,128)(2,1)S(1)}, u32[]{:S(2)}, u32[]{:S(2)}) %collective-permute-start.9) | collective-permute-done | bytes 131104 | tf_op jit(solution)/shard_map/ppermute | solution.py:32
  75.5 0.9 shard_map.93
  76.4 6.1 %all-to-all-start.2 = ((bf16[16,16,768]{2,1,0:T(8,128)(2,1)}), bf16[16,16,768]{2,1,0:T(8,128)(2,1)S(1)}, u32[]{:S(2)}, u32[]{:S(2)}) async-start(bf16[16,16,768]{2,1,0:T(8,128)(2,1)} %get-tuple-element.394), calls=%async_computation.2 | async-start | bytes 786432 | tf_op jit(solution)/shard_map/all_to_all | solution.py:17
  82.5 2.2 %collective-permute-start.11 = (bf16[256,1024]{1,0:T(8,128)(2,1)S(1)}, bf16[256,1024]{1,0:T(8,128)(2,1)S(1)}, u32[]{:S(2)}, u32[]{:S(2)}) collective-permute-start(bf16[256,1024]{1,0:T(8,128)(2,1)S(1)} %copy-done.1), channel_id=1, source_target_pairs={{0,1},{1,0},{2,3},{3,2},{4,5},{5,4},{6,7},{7,6},{8,9},{9,8},{10,11... | collective-permute-start | bytes 1572872 | tf_op jit(solution)/shard_map/ppermute | solution.py:32
  85.5 0.6 copy-done.23
  86.3 35.5 %all_gather.3.refs_0_ = bf16[1024,256]{1,0:T(8,128)(2,1)S(1)} all-gather(bf16[64,256]{1,0:T(8,128)(2,1)S(1)} %get-tuple-element.392), channel_id=1, replica_groups={{0,2,4,6,8,10,12,14,16,18,20,22,24,26,28,30},{1,3,5,7,9,11,13,15,17,19,..., dimensions={0}, use_global_device_ids=true | all-gather | bytes 557056 | tf_op jit(solution)/shard_map/all_gather | solution.py:378
  121.8 5.2 %shard_map.94 = (bf16[256,1024]{1,0:T(8,128)(2,1)}, bf16[16,16,768]{2,1,0:T(8,128)(2,1)S(1)}, bf16[16,1024]{1,0:T(8,128)(2,1)S(1)}) custom-call(bf16[1024,256]{1,0:T(8,128)(2,1)S(1)} %all_gather.3.refs_0_, bf16[256,1024]{1,0:T(8,128)(2,1)S(1)} %copy-done, ...), custom_call_target="tpu_custom_call", output_to_operand_aliasing={{1}: (9, {}), {2}: (10, {})} | custom-call | flops 536870912 | bytes 3145728 | tf_op jit(solution)/shard_map/pallas_call | solution.py:235
  127.0 10.9 %all-to-all-start.3 = ((bf16[16,16,1024]{2,1,0:T(8,128)(2,1)}), bf16[16,16,1024]{2,1,0:T(8,128)(2,1)S(1)}, u32[]{:S(2)}, u32[]{:S(2)}) async-start(bf16[16,16,1024]{2,1,0:T(8,128)(2,1)} %bitcast.21), calls=%async_computation.3 | async-start | bytes 1048576 | tf_op jit(solution)/shard_map/all_to_all | solution.py:17
  138.3 3.2 %collective-permute-start.13 = (bf16[1024,128]{1,0:T(8,128)(2,1)S(1)}, bf16[1024,128]{1,0:T(8,128)(2,1)S(1)}, u32[]{:S(2)}, u32[]{:S(2)}) collective-permute-start(bf16[1024,128]{1,0:T(8,128)(2,1)S(1)} %bitcast.105), channel_id=1, source_target_pairs={{0,128},{32,160},{64,192},{96,224},{128,256},{160,288},{192,320},{... | collective-permute-start | bytes 786440 | tf_op jit(solution)/shard_map/ppermute | solution.py:37
  141.5 4.5 %collective-permute-start.14 = (bf16[1024,128]{1,0:T(8,128)(2,1)S(1)}, bf16[1024,128]{1,0:T(8,128)(2,1)S(1)}, u32[]{:S(2)}, u32[]{:S(2)}) collective-permute-start(bf16[1024,128]{1,0:T(8,128)(2,1)S(1)} %bitcast.106), channel_id=1, source_target_pairs={{0,256},{32,288},{64,320},{96,352},{128,384},{160,416},{192,448},{... | collective-permute-start | bytes 786440 | tf_op jit(solution)/shard_map/ppermute | solution.py:37
  146.0 3.0 %collective-permute-start.15 = (bf16[1024,128]{1,0:T(8,128)(2,1)S(1)}, bf16[1024,128]{1,0:T(8,128)(2,1)S(1)}, u32[]{:S(2)}, u32[]{:S(2)}) collective-permute-start(bf16[1024,128]{1,0:T(8,128)(2,1)S(1)} %bitcast.107), channel_id=1, source_target_pairs={{0,384},{32,416},{64,448},{96,480},{128,0},{160,32},{192,64},{224,... | collective-permute-start | bytes 786440 | tf_op jit(solution)/shard_map/ppermute | solution.py:37
  149.0 9.9 %collective-permute-start.16 = (bf16[1024,128]{1,0:T(8,128)(2,1)S(1)}, bf16[1024,128]{1,0:T(8,128)(2,1)S(1)}, u32[]{:S(2)}, u32[]{:S(2)}) collective-permute-start(bf16[1024,128]{1,0:T(8,128)(2,1)S(1)} %bitcast.108), channel_id=1, source_target_pairs={{0,32},{32,0},{64,96},{96,64},{128,160},{160,128},{192,224},{224,1... | collective-permute-start | bytes 786440 | tf_op jit(solution)/shard_map/ppermute | solution.py:37
  158.9 0.7 slice_convert_fusion
  159.6 1.4 reshape.789
  162.5 2.2 %collective-permute-start.12 = (bf16[16,1024]{1,0:T(8,128)(2,1)S(1)}, bf16[16,1024]{1,0:T(8,128)(2,1)S(1)}, u32[]{:S(2)}, u32[]{:S(2)}) collective-permute-start(bf16[16,1024]{1,0:T(8,128)(2,1)S(1)} %get-tuple-element.399), channel_id=1, source_target_pairs={{0,1},{1,0},{2,3},{3,2},{4,5},{5,4},{6,7},{7,6},{8,9},{9,8},{10,11... | collective-permute-start | bytes 98312 | tf_op jit(solution)/shard_map/ppermute | solution.py:32
  164.8 2.4 %collective-permute-done.12 = bf16[16,1024]{1,0:T(8,128)(2,1)S(1)} collective-permute-done((bf16[16,1024]{1,0:T(8,128)(2,1)S(1)}, bf16[16,1024]{1,0:T(8,128)(2,1)S(1)}, u32[]{:S(2)}, u32[]{:S(2)}) %collective-permute-start.12) | collective-permute-done | bytes 32800 | tf_op jit(solution)/shard_map/ppermute | solution.py:32
  167.2 3.3 %collective-permute-start.17 = (bf16[1024,128]{1,0:T(8,128)(2,1)S(1)}, bf16[1024,128]{1,0:T(8,128)(2,1)S(1)}, u32[]{:S(2)}, u32[]{:S(2)}) collective-permute-start(bf16[1024,128]{1,0:T(8,128)(2,1)S(1)} %bitcast.109), channel_id=1, source_target_pairs={{0,160},{32,128},{64,224},{96,192},{128,288},{160,256},{192,352},{... | collective-permute-start | bytes 786440 | tf_op jit(solution)/shard_map/ppermute | solution.py:37
  170.5 2.0 %collective-permute-start.18 = (bf16[1024,128]{1,0:T(8,128)(2,1)S(1)}, bf16[1024,128]{1,0:T(8,128)(2,1)S(1)}, u32[]{:S(2)}, u32[]{:S(2)}) collective-permute-start(bf16[1024,128]{1,0:T(8,128)(2,1)S(1)} %bitcast.110), channel_id=1, source_target_pairs={{0,288},{32,256},{64,352},{96,320},{128,416},{160,384},{192,480},{... | collective-permute-start | bytes 786440 | tf_op jit(solution)/shard_map/ppermute | solution.py:37
  172.5 3.9 %collective-permute-start.19 = (bf16[1024,128]{1,0:T(8,128)(2,1)S(1)}, bf16[1024,128]{1,0:T(8,128)(2,1)S(1)}, u32[]{:S(2)}, u32[]{:S(2)}) collective-permute-start(bf16[1024,128]{1,0:T(8,128)(2,1)S(1)} %bitcast.111), channel_id=1, source_target_pairs={{0,416},{32,384},{64,480},{96,448},{128,32},{160,0},{192,96},{224,... | collective-permute-start | bytes 786440 | tf_op jit(solution)/shard_map/ppermute | solution.py:37
  177.0 0.7 copy-done.12
  177.7 6.6 %collective-permute-done.17.rest_5_ = bf16[1024,128]{1,0:T(8,128)(2,1)S(1)} collective-permute-done((bf16[1024,128]{1,0:T(8,128)(2,1)S(1)}, bf16[1024,128]{1,0:T(8,128)(2,1)S(1)}, u32[]{:S(2)}, u32[]{:S(2)}) %collective-permute-start.17) | collective-permute-done | bytes 262176 | tf_op jit(solution)/shard_map/ppermute | solution.py:37
  184.4 2.4 %collective-permute-done.19.rest_7_ = bf16[1024,128]{1,0:T(8,128)(2,1)S(1)} collective-permute-done((bf16[1024,128]{1,0:T(8,128)(2,1)S(1)}, bf16[1024,128]{1,0:T(8,128)(2,1)S(1)}, u32[]{:S(2)}, u32[]{:S(2)}) %collective-permute-start.19) | collective-permute-done | bytes 262176 | tf_op jit(solution)/shard_map/ppermute | solution.py:37
  186.7 1.8 shard_map.95
  (79 shorter events, 4.5 us)
Async XLA Ops:
  0.0 2.0 %copy-start.2 = (bf16[512,1024]{1,0:T(8,128)(2,1)S(1)}, bf16[512,1024]{1,0:T(8,128)(2,1)}, u32[]{:S(2)}) copy-start(bf16[512,1024]{1,0:T(8,128)(2,1)} %table.1) | copy-start | bytes 3145732
  2.0 0.7 copy-start.16
  3.8 54.9 %collective-permute-start.8 = (bf16[1056,128]{1,0:T(8,128)(2,1)S(1)}, bf16[1056,128]{1,0:T(8,128)(2,1)S(1)}, u32[]{:S(2)}, u32[]{:S(2)}) collective-permute-start(bf16[1056,128]{1,0:T(8,128)(2,1)S(1)} %pad_maximum_fusion.1), channel_id=1, source_target_pairs={{0,1},{1,0},{2,3},{3,2},{4,5},{5,4},{6,7},{7,6},{8,9},{9,8},{10,11... | collective-permute-start | bytes 811016 | tf_op jit(solution)/shard_map/ppermute | solution.py:32
  12.4 28.0 %all-to-all-start.1 = ((bf16[4,32,1024]{2,1,0:T(8,128)(2,1)}), bf16[4,32,1024]{2,1,0:T(8,128)(2,1)S(1)}, u32[]{:S(2)}, u32[]{:S(2)}) async-start(bf16[4,32,1024]{2,1,0:T(8,128)(2,1)} %broadcast_in_dim.29), calls=%async_computation.1 | async-start | bytes 524288 | tf_op jit(solution)/shard_map/all_to_all | solution.py:17
  40.4 22.8 %collective-permute-start.4 = (bf16[128,1024]{1,0:T(8,128)(2,1)S(1)}, bf16[128,1024]{1,0:T(8,128)(2,1)S(1)}, u32[]{:S(2)}, u32[]{:S(2)}) collective-permute-start(bf16[128,1024]{1,0:T(8,128)(2,1)S(1)} %bitcast.102), channel_id=1, source_target_pairs={{0,2},{1,3},{2,4},{3,5},{4,6},{5,7},{6,8},{7,9},{8,10},{9,11},{10,... | collective-permute-start | bytes 786440 | tf_op jit(solution)/shard_map/ppermute | solution.py:28
  49.4 13.9 %collective-permute-start.5 = (bf16[128,1024]{1,0:T(8,128)(2,1)S(1)}, bf16[128,1024]{1,0:T(8,128)(2,1)S(1)}, u32[]{:S(2)}, u32[]{:S(2)}) collective-permute-start(bf16[128,1024]{1,0:T(8,128)(2,1)S(1)} %bitcast.103), channel_id=1, source_target_pairs={{0,30},{1,31},{2,0},{3,1},{4,2},{5,3},{6,4},{7,5},{8,6},{9,7},{10,... | collective-permute-start | bytes 786440 | tf_op jit(solution)/shard_map/ppermute | solution.py:28
  51.4 11.3 %collective-permute-start.6 = (bf16[64,1024]{1,0:T(8,128)(2,1)S(1)}, bf16[64,1024]{1,0:T(8,128)(2,1)S(1)}, u32[]{:S(2)}, u32[]{:S(2)}) collective-permute-start(bf16[64,1024]{1,0:T(8,128)(2,1)S(1)} %bitcast.121), channel_id=1, source_target_pairs={{0,4},{1,5},{2,6},{3,7},{4,8},{5,9},{6,10},{7,11},{8,12},{9,13},{1... | collective-permute-start | bytes 393224 | tf_op jit(solution)/shard_map/ppermute | solution.py:28
  55.2 8.1 %collective-permute-start.7 = (bf16[64,1024]{1,0:T(8,128)(2,1)S(1)}, bf16[64,1024]{1,0:T(8,128)(2,1)S(1)}, u32[]{:S(2)}, u32[]{:S(2)}) collective-permute-start(bf16[64,1024]{1,0:T(8,128)(2,1)S(1)} %bitcast.120), channel_id=1, source_target_pairs={{0,28},{1,29},{2,30},{3,31},{4,0},{5,1},{6,2},{7,3},{8,4},{9,5},{1... | collective-permute-start | bytes 393224 | tf_op jit(solution)/shard_map/ppermute | solution.py:28
  58.8 0.7 copy-start.13
  59.5 1.0 copy-start
  60.6 12.2 %collective-permute-start.10 = (bf16[256,1024]{1,0:T(8,128)(2,1)S(1)}, bf16[256,1024]{1,0:T(8,128)(2,1)S(1)}, u32[]{:S(2)}, u32[]{:S(2)}) collective-permute-start(bf16[256,1024]{1,0:T(8,128)(2,1)S(1)} %copy-done), channel_id=1, source_target_pairs={{0,1},{1,0},{2,3},{3,2},{4,5},{5,4},{6,7},{7,6},{8,9},{9,8},{10,11... | collective-permute-start | bytes 1572872 | tf_op jit(solution)/shard_map/ppermute | solution.py:32
  65.0 10.6 %collective-permute-start.9 = (bf16[256,256]{1,0:T(8,128)(2,1)}, bf16[256,256]{1,0:T(8,128)(2,1)S(1)}, u32[]{:S(2)}, u32[]{:S(2)}) collective-permute-start(bf16[256,256]{1,0:T(8,128)(2,1)} %get-tuple-element.832), channel_id=1, source_target_pairs={{0,1},{1,0},{2,3},{3,2},{4,5},{5,4},{6,7},{7,6},{8,9},{9,8},{10,11... | collective-permute-start | bytes 393224 | tf_op jit(solution)/shard_map/ppermute | solution.py:32
  76.4 6.1 %copy-start.1 = (bf16[256,1024]{1,0:T(8,128)(2,1)S(1)}, bf16[256,1024]{1,0:T(8,128)(2,1)}, u32[]{:S(2)}) copy-start(bf16[256,1024]{1,0:T(8,128)(2,1)} %refs_3_.1) | copy-start | bytes 1572868
  76.4 45.4 %all-to-all-start.2 = ((bf16[16,16,768]{2,1,0:T(8,128)(2,1)}), bf16[16,16,768]{2,1,0:T(8,128)(2,1)S(1)}, u32[]{:S(2)}, u32[]{:S(2)}) async-start(bf16[16,16,768]{2,1,0:T(8,128)(2,1)} %get-tuple-element.394), calls=%async_computation.2 | async-start | bytes 786432 | tf_op jit(solution)/shard_map/all_to_all | solution.py:17
  82.5 39.3 %collective-permute-start.11 = (bf16[256,1024]{1,0:T(8,128)(2,1)S(1)}, bf16[256,1024]{1,0:T(8,128)(2,1)S(1)}, u32[]{:S(2)}, u32[]{:S(2)}) collective-permute-start(bf16[256,1024]{1,0:T(8,128)(2,1)S(1)} %copy-done.1), channel_id=1, source_target_pairs={{0,1},{1,0},{2,3},{3,2},{4,5},{5,4},{6,7},{7,6},{8,9},{9,8},{10,11... | collective-permute-start | bytes 1572872 | tf_op jit(solution)/shard_map/ppermute | solution.py:32
  85.4 0.7 copy-start.23
  86.3 35.5 %copy-start.9 = (bf16[16,1024]{1,0:T(8,128)(2,1)S(1)}, bf16[16,1024]{1,0:T(8,128)(2,1)}, u32[]{:S(2)}) copy-start(bf16[16,1024]{1,0:T(8,128)(2,1)} %get-tuple-element.834) | copy-start | bytes 98308
  127.0 59.7 %all-to-all-start.3 = ((bf16[16,16,1024]{2,1,0:T(8,128)(2,1)}), bf16[16,16,1024]{2,1,0:T(8,128)(2,1)S(1)}, u32[]{:S(2)}, u32[]{:S(2)}) async-start(bf16[16,16,1024]{2,1,0:T(8,128)(2,1)} %bitcast.21), calls=%async_computation.3 | async-start | bytes 1048576 | tf_op jit(solution)/shard_map/all_to_all | solution.py:17
  138.3 32.3 %collective-permute-start.13 = (bf16[1024,128]{1,0:T(8,128)(2,1)S(1)}, bf16[1024,128]{1,0:T(8,128)(2,1)S(1)}, u32[]{:S(2)}, u32[]{:S(2)}) collective-permute-start(bf16[1024,128]{1,0:T(8,128)(2,1)S(1)} %bitcast.105), channel_id=1, source_target_pairs={{0,128},{32,160},{64,192},{96,224},{128,256},{160,288},{192,320},{... | collective-permute-start | bytes 786440 | tf_op jit(solution)/shard_map/ppermute | solution.py:37
  141.5 31.0 %collective-permute-start.14 = (bf16[1024,128]{1,0:T(8,128)(2,1)S(1)}, bf16[1024,128]{1,0:T(8,128)(2,1)S(1)}, u32[]{:S(2)}, u32[]{:S(2)}) collective-permute-start(bf16[1024,128]{1,0:T(8,128)(2,1)S(1)} %bitcast.106), channel_id=1, source_target_pairs={{0,256},{32,288},{64,320},{96,352},{128,384},{160,416},{192,448},{... | collective-permute-start | bytes 786440 | tf_op jit(solution)/shard_map/ppermute | solution.py:37
  146.0 31.7 %collective-permute-start.15 = (bf16[1024,128]{1,0:T(8,128)(2,1)S(1)}, bf16[1024,128]{1,0:T(8,128)(2,1)S(1)}, u32[]{:S(2)}, u32[]{:S(2)}) collective-permute-start(bf16[1024,128]{1,0:T(8,128)(2,1)S(1)} %bitcast.107), channel_id=1, source_target_pairs={{0,384},{32,416},{64,448},{96,480},{128,0},{160,32},{192,64},{224,... | collective-permute-start | bytes 786440 | tf_op jit(solution)/shard_map/ppermute | solution.py:37
  149.0 28.7 %collective-permute-start.16 = (bf16[1024,128]{1,0:T(8,128)(2,1)S(1)}, bf16[1024,128]{1,0:T(8,128)(2,1)S(1)}, u32[]{:S(2)}, u32[]{:S(2)}) collective-permute-start(bf16[1024,128]{1,0:T(8,128)(2,1)S(1)} %bitcast.108), channel_id=1, source_target_pairs={{0,32},{32,0},{64,96},{96,64},{128,160},{160,128},{192,224},{224,1... | collective-permute-start | bytes 786440 | tf_op jit(solution)/shard_map/ppermute | solution.py:37
  162.2 2.5 %copy-start.24 = (f32[1024]{0:T(1024)S(1)}, f32[1024]{0:T(1024)}, u32[]{:S(2)}) copy-start(f32[1024]{0:T(1024)} %param.18) | copy-start | bytes 12292
  162.5 4.7 %collective-permute-start.12 = (bf16[16,1024]{1,0:T(8,128)(2,1)S(1)}, bf16[16,1024]{1,0:T(8,128)(2,1)S(1)}, u32[]{:S(2)}, u32[]{:S(2)}) collective-permute-start(bf16[16,1024]{1,0:T(8,128)(2,1)S(1)} %get-tuple-element.399), channel_id=1, source_target_pairs={{0,1},{1,0},{2,3},{3,2},{4,5},{5,4},{6,7},{7,6},{8,9},{9,8},{10,11... | collective-permute-start | bytes 98312 | tf_op jit(solution)/shard_map/ppermute | solution.py:32
  167.2 17.2 %collective-permute-start.17 = (bf16[1024,128]{1,0:T(8,128)(2,1)S(1)}, bf16[1024,128]{1,0:T(8,128)(2,1)S(1)}, u32[]{:S(2)}, u32[]{:S(2)}) collective-permute-start(bf16[1024,128]{1,0:T(8,128)(2,1)S(1)} %bitcast.109), channel_id=1, source_target_pairs={{0,160},{32,128},{64,224},{96,192},{128,288},{160,256},{192,352},{... | collective-permute-start | bytes 786440 | tf_op jit(solution)/shard_map/ppermute | solution.py:37
  170.5 13.9 %collective-permute-start.18 = (bf16[1024,128]{1,0:T(8,128)(2,1)S(1)}, bf16[1024,128]{1,0:T(8,128)(2,1)S(1)}, u32[]{:S(2)}, u32[]{:S(2)}) collective-permute-start(bf16[1024,128]{1,0:T(8,128)(2,1)S(1)} %bitcast.110), channel_id=1, source_target_pairs={{0,288},{32,256},{64,352},{96,320},{128,416},{160,384},{192,480},{... | collective-permute-start | bytes 786440 | tf_op jit(solution)/shard_map/ppermute | solution.py:37
  172.5 14.2 %collective-permute-start.19 = (bf16[1024,128]{1,0:T(8,128)(2,1)S(1)}, bf16[1024,128]{1,0:T(8,128)(2,1)S(1)}, u32[]{:S(2)}, u32[]{:S(2)}) collective-permute-start(bf16[1024,128]{1,0:T(8,128)(2,1)S(1)} %bitcast.111), channel_id=1, source_target_pairs={{0,416},{32,384},{64,480},{96,448},{128,32},{160,0},{192,96},{224,... | collective-permute-start | bytes 786440 | tf_op jit(solution)/shard_map/ppermute | solution.py:37
  176.9 0.8 copy-start.12

commit v4 on v3

--- a/solution.py
+++ b/solution.py
@@ -32,11 +32,13 @@
     return lax.ppermute(block, "seq", [(i, i ^ 1) for i in range(lax.axis_size("seq"))])
 
 
-def from_replica(block, rows, cores):
+def swap_core(block):
+    return lax.ppermute(block, "batch", [(i, i ^ 1) for i in range(lax.axis_size("batch"))])
+
+
+def from_row(block, shift):
     count = lax.axis_size("batch")
-    return lax.ppermute(
-        block, "batch", [(i, ((i + 4 * rows) % count) ^ cores) for i in range(count)]
-    )
+    return lax.ppermute(block, "batch", [(i, (i + 4 * shift) % count) for i in range(count)])
 
 
 def gather_slots(block):
@@ -71,40 +73,85 @@
     return value * (0.5 + 0.5 * jnp.tanh(0.5 * value))
 
 
-def pick_kernel(numbers, ids, table, packed):
+def marked(condition):
+    return condition.astype(jnp.float32).astype(jnp.bfloat16)
+
+
+def pick_kernel(numbers, ids, table, packed, slots, pair_slots, most):
     rows, count = table.shape[0], ids.shape[1]
-    there = ids[...] - numbers[0] * rows
-    here = (there >= 0) & (there < rows)
+    index, first_rank, devices = numbers[0], numbers[1], most.shape[0]
+    place, side = index // 2, lax.rem(index, 2)
+    slot_count = packed.shape[0]
+    shard_lanes = ids[...] // rows
+    shards = lax.broadcasted_iota(jnp.int32, (most.shape[0], count), 0)
+    member = shards == shard_lanes
     before = lax.broadcasted_iota(jnp.int32, (count, count), 0) < lax.broadcasted_iota(
         jnp.int32, (count, count), 1
     )
-    marks = jnp.broadcast_to(here.astype(jnp.float32), (8, count)).astype(jnp.bfloat16)
-    rank = jnp.dot(
-        marks,
-        before.astype(jnp.float32).astype(jnp.bfloat16),
-        preferred_element_type=jnp.float32,
-    )[:1].astype(jnp.int32)
-    slot = jnp.where(here, rank - numbers[1], -1)
-    taken = slot == lax.broadcasted_iota(jnp.int32, (packed.shape[0], count), 0)
+    ranks = jnp.dot(marked(member), marked(before), preferred_element_type=jnp.float32)
+    rank = jnp.sum(jnp.where(member, ranks, 0.0), axis=0, keepdims=True)
+    counts = jnp.sum(member.astype(jnp.float32), axis=1, keepdims=True)
+    most[...] = jnp.broadcast_to(
+        jnp.max(counts, axis=0, keepdims=True), most.shape
+    ).astype(jnp.int32)
+    slot = rank.astype(jnp.int32) - first_rank
+    there = ids[...] - index * rows
+    own_slot = jnp.where((there >= 0) & (there < rows), slot, -1)
+    taken = own_slot == lax.broadcasted_iota(jnp.int32, (slot_count, count), 0)
     wanted = there == lax.broadcasted_iota(jnp.int32, (rows, count), 0)
     picks = lax.dot_general(
-        taken.astype(jnp.float32).astype(jnp.bfloat16),
-        wanted.astype(jnp.float32).astype(jnp.bfloat16),
-        (((1,), (1,)), ((), ())),
-        preferred_element_type=jnp.float32,
+        marked(taken), marked(wanted), (((1,), (1,)), ((), ())), preferred_element_type=jnp.float32
     ).astype(jnp.bfloat16)
     packed[...] = jnp.dot(picks, table[...], preferred_element_type=jnp.float32).astype(
         jnp.bfloat16
     )
-
-
-def pick(numbers, ids, table):
+    source = shard_lanes // 2
+    inside = (shard_lanes - 2 * source == side) & (slot >= 0) & (slot < slot_count)
+    ahead = lax.rem(source - place + devices, near_places)
+    piece = jnp.where(ahead == 0, 0, jnp.where(ahead == near_places - 1, 1, ahead + 1))
+    block = piece * (devices // 2 // near_places) + source // near_places
+    facts = jnp.concatenate(
+        [
+            jnp.broadcast_to(jnp.where(inside, fact, -1).astype(jnp.float32), (8, count))
+            for fact in (block, slot)
+        ],
+        axis=0,
+    ).astype(jnp.bfloat16)
+
+    def spread(chosen, out):
+        both = lax.dot_general(
+            marked(chosen), facts, (((1,), (1,)), ((), ())), preferred_element_type=jnp.float32
+        )
+        block_at, slot_at = both[:, :1].astype(jnp.int32), both[:, 8:9].astype(jnp.int32)
+        out[...] = jnp.where(block_at < 0, -1, block_at * slot_count + slot_at)
+
+    own = count // devices
+    at = lax.broadcasted_iota(jnp.int32, (count, count), 0)
+    half = at // (count // 2)
+    inner = at - half * (count // 2)
+    owner_side = jnp.where(half == 0, side, 1 - side)
+    original = (inner // own) * (2 * own) + owner_side * own + lax.rem(inner, own)
+    spread(original == lax.broadcasted_iota(jnp.int32, (count, count), 1), slots)
+    at = lax.broadcasted_iota(jnp.int32, (2 * own, count), 0)
+    half = at // own
+    owner_side = jnp.where(half == 0, side, 1 - side)
+    original = place * (2 * own) + owner_side * own + at - half * own
+    spread(original == lax.broadcasted_iota(jnp.int32, (2 * own, count), 1), pair_slots)
+
+
+def pick(numbers, ids, table, devices):
     whole = pl.BlockSpec(memory_space=pltpu.VMEM)
+    count = ids.shape[0]
     return pl.pallas_call(
         pick_kernel,
         in_specs=[pl.BlockSpec(memory_space=pltpu.SMEM), whole, whole],
-        out_specs=whole,
-        out_shape=jax.ShapeDtypeStruct((slot_rows, table.shape[1]), jnp.bfloat16),
+        out_specs=[whole] * 4,
+        out_shape=[
+            jax.ShapeDtypeStruct((slot_rows, table.shape[1]), jnp.bfloat16),
+            jax.ShapeDtypeStruct((count, 1), jnp.int32),
+            jax.ShapeDtypeStruct((2 * count // devices, 1), jnp.int32),
+            jax.ShapeDtypeStruct((devices, 128), jnp.int32),
+        ],
         compiler_params=pltpu.CompilerParams(vmem_limit_bytes=32 * 1024 * 1024),
         cost_estimate=pl.CostEstimate(
             flops=2 * slot_rows * table.shape[0] * table.shape[1],
@@ -115,20 +162,25 @@
 
 
 def project_kernel(at, at_pair, rows_0, rows_1, rows_2, rows_3, rows_4, weights, *rest):
-    proj_mine, proj_other, own_rows, other_rows, slots = rest
-    cand_side = proj_mine.shape[0]
-    own = own_rows.shape[0]
+    proj_mine, proj_other, own_rows, slots = rest
+    cand_side, columns = proj_mine.shape
+    own, width = own_rows.shape
     first = 0
     for rows in (rows_0, rows_1, rows_2, rows_3, rows_4):
         count = rows.shape[0]
         slots[first : first + count, :] = silu(
-            jnp.dot(rows[...], weights[...], preferred_element_type=jnp.float32)
+            lax.dot_general(
+                rows[...],
+                weights[...],
+                (((1,), (1,)), ((), ())),
+                preferred_element_type=jnp.float32,
+            )
         ).astype(jnp.bfloat16)
         first += count
     place = lax.broadcasted_iota(jnp.int32, (cand_side, first), 1)
     for side, proj in ((0, proj_mine), (1, proj_other)):
         chosen = (at[side * cand_side : (side + 1) * cand_side, :] == place).astype(jnp.float32)
-        proj[...] = jnp.dot(
+        proj[:cand_side, :] = jnp.dot(
             chosen.astype(jnp.bfloat16), slots[...], preferred_element_type=jnp.float32
         ).astype(jnp.bfloat16)
     place = lax.broadcasted_iota(jnp.int32, (2 * own, first), 1)
@@ -143,18 +195,24 @@
         total = part if total is None else total + part
         first += count
     own_rows[...] = total[:own].astype(jnp.bfloat16)
-    other_rows[...] = total[own:].astype(jnp.bfloat16)
+    for part in range(width // columns):
+        proj_other[cand_side + part * own : cand_side + (part + 1) * own, :] = total[
+            own:, part * columns : (part + 1) * columns
+        ].astype(jnp.bfloat16)
 
 
 def project(at, at_pair, rows, weights):
-    width, columns = weights.shape
+    columns, width = weights.shape
     cand_side = at.shape[0] // 2
     own = at_pair.shape[0] // 2
     slot_count = sum(piece.shape[0] for piece in rows)
     return pl.pallas_call(
         project_kernel,
-        out_shape=[jax.ShapeDtypeStruct((cand_side, columns), jnp.bfloat16)] * 2
-        + [jax.ShapeDtypeStruct((own, width), jnp.bfloat16)] * 2,
+        out_shape=[
+            jax.ShapeDtypeStruct((cand_side, columns), jnp.bfloat16),
+            jax.ShapeDtypeStruct((cand_side + own * width // columns, columns), jnp.bfloat16),
+            jax.ShapeDtypeStruct((own, width), jnp.bfloat16),
+        ],
         scratch_shapes=[pltpu.VMEM((slot_count, columns), jnp.bfloat16)],
         compiler_params=pltpu.CompilerParams(vmem_limit_bytes=32 * 1024 * 1024),
         cost_estimate=pl.CostEstimate(
@@ -165,9 +223,17 @@
     )(at, at_pair, *rows, weights)
 
 
-def pack_kernel(feature_here, mine, arrived, w_slice, *rest):
-    queries, packed = rest[-2:]
-    proj = mine[...].astype(jnp.float32) + arrived[...].astype(jnp.float32)
+def pack_kernel(feature_here, mine, arrived, own_rows, w_slice, *rest):
+    queries, packed, embedded = rest[-3:]
+    cand_side, columns = mine.shape
+    own = own_rows.shape[0]
+    proj = mine[...].astype(jnp.float32) + arrived[:cand_side, :].astype(jnp.float32)
+    for part in range(own_rows.shape[1] // columns):
+        lanes = slice(part * columns, (part + 1) * columns)
+        other = arrived[cand_side + part * own : cand_side + (part + 1) * own, :]
+        embedded[:, lanes] = (
+            own_rows[:, lanes].astype(jnp.float32) + other.astype(jnp.float32)
+        ).astype(jnp.bfloat16)
     block = 4 * feature_here
     query = jnp.concatenate(
         [proj[:, side * block + 2 * feature_here : side * block + 3 * feature_here] for side in (0, 1)],
@@ -184,29 +250,31 @@
         )
 
 
-def pack(mine, arrived, w_slice, ready, feature_here, own):
+def pack(mine, arrived, own_rows, w_slice, ready, feature_here):
     cand_side, columns = mine.shape
+    own = own_rows.shape[0]
     column = cand_side // own
     packed_width = columns + w_slice.shape[0] * w_slice.shape[1] // own
     whole = pl.BlockSpec(memory_space=pltpu.VMEM)
     return pl.pallas_call(
         lambda *refs: pack_kernel(feature_here, *refs),
-        in_specs=[whole] * 3 + [pl.BlockSpec(memory_space=pl.ANY)] * len(ready),
-        out_specs=[whole] * 2,
+        in_specs=[whole] * 4 + [pl.BlockSpec(memory_space=pl.ANY)] * len(ready),
+        out_specs=[whole] * 3,
         out_shape=[
             jax.ShapeDtypeStruct((2 * feature_here, cand_side), jnp.bfloat16),
             jax.ShapeDtypeStruct((column, own, packed_width), jnp.bfloat16),
+            jax.ShapeDtypeStruct(own_rows.shape, jnp.bfloat16),
         ],
         compiler_params=pltpu.CompilerParams(vmem_limit_bytes=32 * 1024 * 1024),
         cost_estimate=pl.CostEstimate(
             flops=cand_side * columns, bytes_accessed=8 * cand_side * columns, transcendentals=0
         ),
-    )(mine, arrived, w_slice, *ready)
+    )(mine, arrived, own_rows, w_slice, *ready)
 
 
 def attend_kernel(scale, *refs):
     queries, keys_a, keys_b, values_a, values_b, bias_a, bias_b, live_a, live_b = refs[:9]
-    summed = refs[-3]
+    summed = refs[-2]
     head = pl.program_id(0)
     head_queries = queries[...].T
     total = None
@@ -239,18 +307,20 @@
         + [event_spec] * 4
         + [bias_spec] * 2
         + [live_spec] * 2
-        + [held] * 2,
-        out_specs=[pl.BlockSpec((cand, head_size), lambda h: (0, h)), held, held],
-        out_shape=[jax.ShapeDtypeStruct((cand, width), jnp.bfloat16)]
-        + [jax.ShapeDtypeStruct(array.shape, array.dtype) for array in through],
-        input_output_aliases={9: 1, 10: 2},
+        + [held],
+        out_specs=[pl.BlockSpec((cand, head_size), lambda h: (0, h)), held],
+        out_shape=[
+            jax.ShapeDtypeStruct((cand, width), jnp.bfloat16),
+            jax.ShapeDtypeStruct(through.shape, through.dtype),
+        ],
+        input_output_aliases={9: 1},
         compiler_params=pltpu.CompilerParams(vmem_limit_bytes=32 * 1024 * 1024),
         cost_estimate=pl.CostEstimate(
             flops=8 * cand * events * width,
             bytes_accessed=8 * events * width + 4 * cand * width,
             transcendentals=2 * cand * events * head_count,
         ),
-    )(queries, *keys, *values, *bias, *live, *through)
+    )(queries, *keys, *values, *bias, *live, through)
 
 
 def finish_kernel(numbers, parts, self_term, gate, embedded, *rest):
@@ -314,65 +384,43 @@
     out_lanes = width // (2 * row_count)
     length = lengths[0]
 
-    by_side = jnp.arange(cand_total, dtype=jnp.int32).reshape(column, 2, cand_here)
-    by_side = by_side.transpose(1, 0, 2).reshape(2, cand_side)
-    ids = item_ids.reshape(column, 2, cand_here).transpose(1, 0, 2).reshape(2, cand_side)
-    order = jnp.where(side == 0, by_side, by_side[::-1]).reshape(cand_total)
-    ids = jnp.where(side == 0, ids, ids[::-1]).reshape(cand_total)
-    shard = ids // table_rows
-    row_there = ids - shard * table_rows
-    same = shard[:, None] == shard[None, :]
-    rank = jnp.sum((same & (order[None, :] < order[:, None])).astype(jnp.int32), axis=1)
-    most = jnp.max(rank) + 1
-
     w_slice = lax.dynamic_slice_in_dim(w_out, (core * row_count + row) * out_lanes, out_lanes, 1)
     slice_rows = w_slice.shape[0]
 
     def lookup(first_rank, send):
-        packed = pick(jnp.stack([index_here, first_rank]), item_ids, item_table)
+        numbers = jnp.stack([index_here, first_rank])
+        packed, slots, pair_slots, most = pick(numbers, item_ids, item_table, device_count)
         packed, send = lax.optimization_barrier((packed, send))
-        return gather_slots(packed), [swap_pair(block) for block in send]
-
-    def place_of(first_rank):
-        slot = rank - first_rank
-        inside = (shard % 2 == side) & (slot >= 0) & (slot < slot_rows)
-        source = shard // 2
-        ahead = (source - place) % near_places
-        piece = jnp.where(ahead == 0, 0, jnp.where(ahead == near_places - 1, 1, ahead + 1))
-        block = piece * (column // near_places) + source // near_places
-        at = jnp.where(inside, block * slot_rows + slot, -1)
-        at_pair = lax.dynamic_slice_in_dim(
-            at.reshape(2, cand_side), place * cand_here, cand_here, 1
-        )
-        return at.reshape(cand_total, 1), at_pair.reshape(2 * cand_here, 1)
-
-    w_mine = w_proj.reshape(width, 4 * feature_here)
-    w_send = jnp.concatenate([w_mine, w_slice.reshape(-1, 4 * feature_here)])
-    rows, (w_other, keys_other, values_other) = lookup(
+        rows = gather_slots(packed)
+        return rows, slots, pair_slots, most[0, 0], [swap_pair(block) for block in send]
+
+    w_mine = w_proj.transpose(1, 2, 0).reshape(4 * feature_here, width)
+    w_send = jnp.concatenate([w_mine, w_slice.reshape(-1, width)])
+    rows, slots, pair_slots, most, (w_other, keys_other, values_other) = lookup(
         jnp.int32(0), (w_send, history_keys, history_values)
     )
-    slice_other = w_other[width:].reshape(w_slice.shape)
-    w_other = w_other[:width]
+    slice_other = w_other[4 * feature_here :].reshape(w_slice.shape)
+    w_other = w_other[: 4 * feature_here]
     keys, values = (history_keys, keys_other), (history_values, values_other)
     w_pair = jnp.concatenate(
-        [jnp.where(side == 0, w_mine, w_other), jnp.where(side == 0, w_other, w_mine)], axis=1
+        [jnp.where(side == 0, w_mine, w_other), jnp.where(side == 0, w_other, w_mine)]
     )
     slices = jnp.concatenate(
         [jnp.where(side == 0, w_slice, slice_other), jnp.where(side == 0, slice_other, w_slice)]
     )
-    found = tuple(project(*place_of(jnp.int32(0)), rows, w_pair))
+    found = tuple(project(slots, pair_slots, rows, w_pair))
 
     def another(state):
         first_rank, found = state
-        rows, _ = lookup(first_rank, ())
-        more = project(*place_of(first_rank), rows, w_pair)
+        rows, slots, pair_slots, _, _ = lookup(first_rank, ())
+        more = project(slots, pair_slots, rows, w_pair)
         return first_rank + slot_rows, tuple(a + b for a, b in zip(found, more))
 
-    _, (proj_mine, proj_other, own_rows, other_rows) = lax.while_loop(
+    _, (proj_mine, proj_other, own_rows) = lax.while_loop(
         lambda state: state[0] < most, another, (jnp.int32(slot_rows), found)
     )
-    side_queries, packed = pack(
-        proj_mine, swap_pair(proj_other), slices, (keys_other,), feature_here, cand_here
+    side_queries, packed, embedded = pack(
+        proj_mine, swap_pair(proj_other), own_rows, slices, (keys_other,), feature_here
     )
     received = exchange(packed, column_groups())
     all_queries = lax.all_gather(
@@ -387,11 +435,8 @@
         )
 
     bias, live = zip(bias_of(index_here), bias_of(index_here + 1 - 2 * side))
-    summed, received, other_rows = attend(
-        all_queries, keys, values, bias, live, head_count, (received, other_rows)
-    )
+    summed, received = attend(all_queries, keys, values, bias, live, head_count, received)
     parts = exchange(summed.reshape(column, cand_here, width), column_groups())
-    embedded = own_rows + swap_pair(other_rows)
 
     own_proj = (
         received[:, :, : 8 * feature_here]
@@ -415,11 +460,8 @@
         .transpose(0, 2, 1, 3)
         .reshape(width, out_lanes)
     )
-    weights = [
-        from_replica(w_here, rows_before, other) if rows_before or other else w_here
-        for other in range(2)
-        for rows_before in range(row_count)
-    ]
+    weights = [w_here] + [from_row(w_here, shift) for shift in range(1, row_count)]
+    weights = [*weights, *swap_core(jnp.stack(weights))]
     numbers = jnp.stack([length, row, core])
     return finish(numbers, parts, self_term, gate, embedded, weights)
 

time: 190 us -> 168 us (0.88)
  starting transfers between devices: 92.8 us -> 82.7 us
  waiting for transfers between devices: 28.7 us -> 23 us
  local copies, waits for them, and re-layouts: 11.5 us -> 7.63 us
  other arithmetic: 7.14 us -> 3.9 us
  Pallas kernels: 10.7 us -> 13.1 us
    ppermute x7 -> x4, starting transfers between devices: 29.8 us -> 19.7 us  [the longest x1 10.2 us: swap_core(): lax.ppermute(block, 'batch', [(i, i ^ 1) for i in range(lax.axis_size('ba...]
    ppermute x5 -> x4, waiting for transfers between devices: 9.63 us -> 5.75 us  [swap_pair(): lax.ppermute(block, 'seq', [(i, i ^ 1) for i in range(lax.axis_size('seq'...]
    unnamed x22 -> x16, local copies, waits for them, and re-layouts: 3.77 us -> 1.6 us
    ppermute x7 -> x4, waiting for transfers between devices: 9 us -> 6.86 us  [the longest x3 6.86 us: from_row(): lax.ppermute(block, 'batch', [(i, (i + 4 * shift) % count) for i in range...]
    sign x2 -> x0, other arithmetic: 2.13 us -> none  [place_of(): source = shard // 2]
    ppermute x5 -> x4, starting transfers between devices: 13 us -> 12.6 us  [swap_pair(): lax.ppermute(block, 'seq', [(i, i ^ 1) for i in range(lax.axis_size('seq'...]
  transfers between devices with their start and end apart: 19 -> 15, of which waited for: 7 -> 6; matrix products, arithmetic and copies ran while one was open for 7% -> 5% of each run, Pallas kernels for 1% -> 1%
where the time goes in v4:
time: 168 us; the launch traced here: 167 us
  starting transfers between devices  82.7 us (49%)
  blocking collectives  34.6 us (21%)
  waiting for transfers between devices  23 us (14%)
  Pallas kernels  13.1 us (8%)
  local copies, waits for them, and re-layouts  7.63 us (5%)
  other arithmetic  3.9 us (2%)
    all_gather x1, blocking collectives, local(): lax.all_gather(side_queries, 'seq', axis=0, tiled=True, axis_index_groups...  34.6 us
    all_to_all x3, starting transfers between devices, exchange(): lax.all_to_all(blocks, 'seq', split_axis=0, concat_axis=0, tiled=True, ax...  32.6 us
    ppermute x4, starting transfers between devices, from_place(): lax.ppermute(block, 'seq', [(i, (i + 2 * shift) % count) for i in range(c...  17.8 us
    ppermute x4, starting transfers between devices, swap_pair(): lax.ppermute(block, 'seq', [(i, i ^ 1) for i in range(lax.axis_size('seq'...  12.6 us
    all_to_all x3, waiting for transfers between devices, exchange(): lax.all_to_all(blocks, 'seq', split_axis=0, concat_axis=0, tiled=True, ax...  10.2 us
    ppermute x1, starting transfers between devices, swap_core(): lax.ppermute(block, 'batch', [(i, i ^ 1) for i in range(lax.axis_size('ba...  10.2 us
    ppermute x3, starting transfers between devices, from_row(): lax.ppermute(block, 'batch', [(i, (i + 4 * shift) % count) for i in range...  9.5 us
    ppermute x3, waiting for transfers between devices, from_row(): lax.ppermute(block, 'batch', [(i, (i + 4 * shift) % count) for i in range...  6.86 us
  transfers between devices with their start and end apart: 15, of which 6 were waited for; matrix products, arithmetic and copies ran while one was open for 5% of the time, Pallas kernels for 1%

profile of v4, /device:TPU:1, one launch (start us, length us, event | category | flops | bytes accessed | tf_op | source)
XLA Modules:
  0.0 166.8 jit_solution(1539512974886898124)
XLA Ops:
  0.0 0.7 constant_dynamic-slice_fusion
  0.8 1.0 pad_maximum_fusion.2
  1.8 2.3 %shard_map.91 = (bf16[32,1024]{1,0:T(8,128)(2,1)S(1)}, s32[512,1]{1,0:T(8,128)S(1)}, s32[32,1]{1,0:T(8,128)S(1)}, s32[32,128]{1,0:T(8,128)S(1)}) custom-call(s32[2]{0:T(128)S(1)} %pad_add_fusion.2.numbers, s32[1,512]{1,0:T(1,128)S(1)} %bitcast.88, bf16[512,1024]{1,0:T(8,128)(2,1)} %table.1), custom_call_target="tpu_custom_call" | custom-call | flops 33554432 | bytes 1048576 | tf_op jit(solution)/shard_map/pallas_call | solution.py:145
  4.1 0.7 broadcast_in_dim.12
  4.8 15.6 %all-to-all-start.1 = ((bf16[4,32,1024]{2,1,0:T(8,128)(2,1)}), bf16[4,32,1024]{2,1,0:T(8,128)(2,1)S(1)}, u32[]{:S(2)}, u32[]{:S(2)}) async-start(bf16[4,32,1024]{2,1,0:T(8,128)(2,1)} %broadcast_in_dim.12), calls=%async_computation.1 | async-start | bytes 524288 | tf_op jit(solution)/shard_map/all_to_all | solution.py:17
  20.4 3.1 %collective-permute-start.8 = (bf16[132,1024]{1,0:T(8,128)(2,1)S(1)}, bf16[132,1024]{1,0:T(8,128)(2,1)S(1)}, u32[]{:S(2)}, u32[]{:S(2)}) collective-permute-start(bf16[132,1024]{1,0:T(8,128)(2,1)S(1)} %pad_maximum_fusion.2), channel_id=1, source_target_pairs={{0,1},{1,0},{2,3},{3,2},{4,5},{5,4},{6,7},{7,6},{8,9},{9,8},{10,11... | collective-permute-start | bytes 811016 | tf_op jit(solution)/shard_map/ppermute | solution.py:32
  23.5 0.5 slice.63
  24.1 10.1 %all-to-all-done.1 = bf16[4,32,1024]{2,1,0:T(8,128)(2,1)S(1)} async-done(((bf16[4,32,1024]{2,1,0:T(8,128)(2,1)}), bf16[4,32,1024]{2,1,0:T(8,128)(2,1)S(1)}, u32[]{:S(2)}, u32[]{:S(2)}) %all-to-all-start.1) | async-done | bytes 262176 | tf_op jit(solution)/shard_map/all_to_all | solution.py:17
  34.2 4.3 %collective-permute-start.5 = (bf16[128,1024]{1,0:T(8,128)(2,1)S(1)}, bf16[128,1024]{1,0:T(8,128)(2,1)S(1)}, u32[]{:S(2)}, u32[]{:S(2)}) collective-permute-start(bf16[128,1024]{1,0:T(8,128)(2,1)S(1)} %bitcast.74), channel_id=1, source_target_pairs={{0,30},{1,31},{2,0},{3,1},{4,2},{5,3},{6,4},{7,5},{8,6},{9,7},{10,... | collective-permute-start | bytes 786440 | tf_op jit(solution)/shard_map/ppermute | solution.py:28
  38.5 6.1 %collective-permute-start.4 = (bf16[128,1024]{1,0:T(8,128)(2,1)S(1)}, bf16[128,1024]{1,0:T(8,128)(2,1)S(1)}, u32[]{:S(2)}, u32[]{:S(2)}) collective-permute-start(bf16[128,1024]{1,0:T(8,128)(2,1)S(1)} %bitcast.75), channel_id=1, source_target_pairs={{0,2},{1,3},{2,4},{3,5},{4,6},{5,7},{6,8},{7,9},{8,10},{9,11},{10,... | collective-permute-start | bytes 786440 | tf_op jit(solution)/shard_map/ppermute | solution.py:28
  44.7 0.7 fusion.7
  45.4 3.7 %collective-permute-start.6 = (bf16[64,1024]{1,0:T(8,128)(2,1)}, bf16[64,1024]{1,0:T(8,128)(2,1)S(1)}, u32[]{:S(2)}, u32[]{:S(2)}) collective-permute-start(bf16[64,1024]{1,0:T(8,128)(2,1)} %bitcast.13), channel_id=1, source_target_pairs={{0,4},{1,5},{2,6},{3,7},{4,8},{5,9},{6,10},{7,11},{8,12},{9,13},{1... | collective-permute-start | bytes 393224 | tf_op jit(solution)/shard_map/ppermute | solution.py:28
  49.2 3.6 %collective-permute-start.7 = (bf16[64,1024]{1,0:T(8,128)(2,1)}, bf16[64,1024]{1,0:T(8,128)(2,1)S(1)}, u32[]{:S(2)}, u32[]{:S(2)}) collective-permute-start(bf16[64,1024]{1,0:T(8,128)(2,1)} %bitcast.14), channel_id=1, source_target_pairs={{0,28},{1,29},{2,30},{3,31},{4,0},{5,1},{6,2},{7,3},{8,4},{9,5},{1... | collective-permute-start | bytes 393224 | tf_op jit(solution)/shard_map/ppermute | solution.py:28
  53.0 1.0 copy-done
  54.0 3.2 %collective-permute-start.10 = (bf16[256,1024]{1,0:T(8,128)(2,1)S(1)}, bf16[256,1024]{1,0:T(8,128)(2,1)S(1)}, u32[]{:S(2)}, u32[]{:S(2)}) collective-permute-start(bf16[256,1024]{1,0:T(8,128)(2,1)S(1)} %copy-done), channel_id=1, source_target_pairs={{0,1},{1,0},{2,3},{3,2},{4,5},{5,4},{6,7},{7,6},{8,9},{9,8},{10,11... | collective-permute-start | bytes 1572872 | tf_op jit(solution)/shard_map/ppermute | solution.py:32
  57.2 0.2 collective-permute-done.7.rows_4
  57.5 2.1 %shard_map.92 = (bf16[256,256]{1,0:T(8,128)(2,1)}, bf16[320,256]{1,0:T(8,128)(2,1)}, bf16[16,1024]{1,0:T(8,128)(2,1)S(1)}) custom-call(s32[512,1]{1,0:T(8,128)S(1)} %get-tuple-element.77.at, s32[32,1]{1,0:T(8,128)S(1)} %get-tuple-element.78.at_pair, bf16[128,1024]{1,0:T(8,128)(2,1)S(1)} %bitcast.76, bf16[128,1024]{1,0:T(8,128)(2,1)S(1)} %collective-permute-done.4.rows_1, ...), custom_call_target="tpu_custom_call" | custom-call | flops 402653184 | bytes 1572864 | tf_op jit(solution)/shard_map/pallas_call | solution.py:209
  59.5 0.6 while.14
  60.2 3.1 %collective-permute-start.9 = (bf16[320,256]{1,0:T(8,128)(2,1)}, bf16[320,256]{1,0:T(8,128)(2,1)S(1)}, u32[]{:S(2)}, u32[]{:S(2)}) collective-permute-start(bf16[320,256]{1,0:T(8,128)(2,1)} %get-tuple-element.87), channel_id=1, source_target_pairs={{0,1},{1,0},{2,3},{3,2},{4,5},{5,4},{6,7},{7,6},{8,9},{9,8},{10,11... | collective-permute-start | bytes 491528 | tf_op jit(solution)/shard_map/ppermute | solution.py:32
  63.3 0.7 broadcast_select_fusion.3
  64.0 2.2 %collective-permute-done.10.refs_4_.refs_2_ = bf16[256,1024]{1,0:T(8,128)(2,1)S(1)} collective-permute-done((bf16[256,1024]{1,0:T(8,128)(2,1)S(1)}, bf16[256,1024]{1,0:T(8,128)(2,1)S(1)}, u32[]{:S(2)}, u32[]{:S(2)}) %collective-permute-start.10) | collective-permute-done | bytes 524320 | tf_op jit(solution)/shard_map/ppermute | solution.py:32
  66.3 3.5 %collective-permute-done.9.refs_1_ = bf16[320,256]{1,0:T(8,128)(2,1)S(1)} collective-permute-done((bf16[320,256]{1,0:T(8,128)(2,1)}, bf16[320,256]{1,0:T(8,128)(2,1)S(1)}, u32[]{:S(2)}, u32[]{:S(2)}) %collective-permute-start.9) | collective-permute-done | bytes 163872 | tf_op jit(solution)/shard_map/ppermute | solution.py:32
  69.8 1.8 %shard_map.93 = (bf16[64,256]{1,0:T(8,128)(2,1)S(1)}, bf16[16,16,768]{2,1,0:T(8,128)(2,1)}, bf16[16,1024]{1,0:T(8,128)(2,1)S(1)}) custom-call(bf16[256,256]{1,0:T(8,128)(2,1)} %get-tuple-element.86.refs_0_, bf16[320,256]{1,0:T(8,128)(2,1)S(1)} %collective-permute-done.9.refs_1_, bf16[16,1024]{1,0:T(8,128)(2,1)S(1)} %get-tuple-element.88.refs_2_, ...), custom_call_target="tpu_custom_call" | custom-call | flops 65536 | bytes 524288 | tf_op jit(solution)/shard_map/pallas_call | solution.py:259
  71.6 6.1 %all-to-all-start.2 = ((bf16[16,16,768]{2,1,0:T(8,128)(2,1)}), bf16[16,16,768]{2,1,0:T(8,128)(2,1)S(1)}, u32[]{:S(2)}, u32[]{:S(2)}) async-start(bf16[16,16,768]{2,1,0:T(8,128)(2,1)} %get-tuple-element.92), calls=%async_computation.2 | async-start | bytes 786432 | tf_op jit(solution)/shard_map/all_to_all | solution.py:17
  77.7 3.1 %collective-permute-start.11 = (bf16[256,1024]{1,0:T(8,128)(2,1)S(1)}, bf16[256,1024]{1,0:T(8,128)(2,1)S(1)}, u32[]{:S(2)}, u32[]{:S(2)}) collective-permute-start(bf16[256,1024]{1,0:T(8,128)(2,1)S(1)} %copy-done.1), channel_id=1, source_target_pairs={{0,1},{1,0},{2,3},{3,2},{4,5},{5,4},{6,7},{7,6},{8,9},{9,8},{10,11... | collective-permute-start | bytes 1572872 | tf_op jit(solution)/shard_map/ppermute | solution.py:32
  81.5 0.1 convert_reduce_fusion
  81.6 0.6 copy-done.10
  82.2 0.1 convolution_bitcast_fusion.refs_6_
  82.3 0.1 convolution_bitcast_fusion.1.refs_5_
  82.4 34.6 %all_gather.3.refs_0_ = bf16[1024,256]{1,0:T(8,128)(2,1)S(1)} all-gather(bf16[64,256]{1,0:T(8,128)(2,1)S(1)} %get-tuple-element.90), channel_id=1, replica_groups={{0,2,4,6,8,10,12,14,16,18,20,22,24,26,28,30},{1,3,5,7,9,11,13,15,17,19,..., dimensions={0}, use_global_device_ids=true | all-gather | bytes 557056 | tf_op jit(solution)/shard_map/all_gather | solution.py:426
  117.0 5.2 %shard_map.94 = (bf16[256,1024]{1,0:T(8,128)(2,1)}, bf16[16,16,768]{2,1,0:T(8,128)(2,1)S(1)}) custom-call(bf16[1024,256]{1,0:T(8,128)(2,1)S(1)} %all_gather.3.refs_0_, bf16[256,1024]{1,0:T(8,128)(2,1)S(1)} %copy-done, bf16[256,1024]{1,0:T(8,128)(2,1)S(1)} %collective-permute-done.10.refs_4_.refs_2_, ...), custom_call_target="tpu_custom_call", output_to_operand_aliasing={{1}: (9, {})} | custom-call | flops 536870912 | bytes 3145728 | tf_op jit(solution)/shard_map/pallas_call | solution.py:303
  122.3 10.9 %all-to-all-start.3 = ((bf16[16,16,1024]{2,1,0:T(8,128)(2,1)}), bf16[16,16,1024]{2,1,0:T(8,128)(2,1)S(1)}, u32[]{:S(2)}, u32[]{:S(2)}) async-start(bf16[16,16,1024]{2,1,0:T(8,128)(2,1)} %bitcast.20), calls=%async_computation.3 | async-start | bytes 1048576 | tf_op jit(solution)/shard_map/all_to_all | solution.py:17
  133.3 4.7 %collective-permute-start.14 = (bf16[1024,128]{1,0:T(8,128)(2,1)S(1)}, bf16[1024,128]{1,0:T(8,128)(2,1)S(1)}, u32[]{:S(2)}, u32[]{:S(2)}) collective-permute-start(bf16[1024,128]{1,0:T(8,128)(2,1)S(1)} %bitcast.77), channel_id=1, source_target_pairs={{0,384},{32,416},{64,448},{96,480},{128,0},{160,32},{192,64},{224,... | collective-permute-start | bytes 786440 | tf_op jit(solution)/shard_map/ppermute | solution.py:41
  137.9 2.2 %collective-permute-start.13 = (bf16[1024,128]{1,0:T(8,128)(2,1)S(1)}, bf16[1024,128]{1,0:T(8,128)(2,1)S(1)}, u32[]{:S(2)}, u32[]{:S(2)}) collective-permute-start(bf16[1024,128]{1,0:T(8,128)(2,1)S(1)} %bitcast.78), channel_id=1, source_target_pairs={{0,256},{32,288},{64,320},{96,352},{128,384},{160,416},{192,448},{... | collective-permute-start | bytes 786440 | tf_op jit(solution)/shard_map/ppermute | solution.py:41
  140.2 2.6 %collective-permute-start.12 = (bf16[1024,128]{1,0:T(8,128)(2,1)S(1)}, bf16[1024,128]{1,0:T(8,128)(2,1)S(1)}, u32[]{:S(2)}, u32[]{:S(2)}) collective-permute-start(bf16[1024,128]{1,0:T(8,128)(2,1)S(1)} %bitcast.79), channel_id=1, source_target_pairs={{0,128},{32,160},{64,192},{96,224},{128,256},{160,288},{192,320},{... | collective-permute-start | bytes 786440 | tf_op jit(solution)/shard_map/ppermute | solution.py:41
  142.8 3.8 %collective-permute-done.13.rest_2_ = bf16[1024,128]{1,0:T(8,128)(2,1)S(1)} collective-permute-done((bf16[1024,128]{1,0:T(8,128)(2,1)S(1)}, bf16[1024,128]{1,0:T(8,128)(2,1)S(1)}, u32[]{:S(2)}, u32[]{:S(2)}) %collective-permute-start.13) | collective-permute-done | bytes 262176 | tf_op jit(solution)/shard_map/ppermute | solution.py:41
  146.6 3.0 %collective-permute-done.12.rest_1_ = bf16[1024,128]{1,0:T(8,128)(2,1)S(1)} collective-permute-done((bf16[1024,128]{1,0:T(8,128)(2,1)S(1)}, bf16[1024,128]{1,0:T(8,128)(2,1)S(1)}, u32[]{:S(2)}, u32[]{:S(2)}) %collective-permute-start.12) | collective-permute-done | bytes 262176 | tf_op jit(solution)/shard_map/ppermute | solution.py:41
  149.6 1.1 pad_maximum_fusion
  150.8 10.2 %collective-permute-start.15 = (bf16[4,1024,128]{2,1,0:T(8,128)(2,1)}, bf16[4,1024,128]{2,1,0:T(8,128)(2,1)}, u32[]{:S(2)}, u32[]{:S(2)}) collective-permute-start(bf16[4,1024,128]{2,1,0:T(8,128)(2,1)} %pad_maximum_fusion), channel_id=1, source_target_pairs={{0,32},{32,0},{64,96},{96,64},{128,160},{160,128},{192,224},{224,1... | collective-permute-start | bytes 3145736 | tf_op jit(solution)/shard_map/ppermute | solution.py:36
  160.9 0.1 pad_add_fusion.1.numbers
  161.0 0.1 slice_reduce_fusion
  161.1 0.5 reshape.157
  161.6 0.5 copy.28
  162.2 0.6 fusion.6
  162.7 0.3 squeeze.13
  163.3 0.3 reshape_squeeze.3
  163.8 1.3 slice_bitcast_fusion
  165.1 1.8 %shard_map.95 = bf16[16,1024]{1,0:T(8,128)(2,1)} custom-call(s32[3]{0:T(128)S(1)} %pad_add_fusion.1.numbers, bf16[16,16,1024]{2,1,0:T(8,128)(2,1)S(1)} %all-to-all-done.3.parts, f32[16,1024]{1,0:T(8,128)S(1)} %get-tuple-element.131.self_term, f32[16,1024]{1,0:T(8,128)S(1)} %get-tuple-element.132.gate, bf16[16,1024]{1,0:T(8,128)(2,1)S(1)} %get-tuple-element.95.embedded, ...), custom_call_target="tpu_custom_call" | custom-call | flops 33554432 | bytes 4194304 | tf_op jit(solution)/shard_map/pallas_call | solution.py:353
  (43 shorter events, 0.7 us)
Async XLA Ops:
  0.8 1.0 copy-start.9
  4.8 29.4 %all-to-all-start.1 = ((bf16[4,32,1024]{2,1,0:T(8,128)(2,1)}), bf16[4,32,1024]{2,1,0:T(8,128)(2,1)S(1)}, u32[]{:S(2)}, u32[]{:S(2)}) async-start(bf16[4,32,1024]{2,1,0:T(8,128)(2,1)} %broadcast_in_dim.12), calls=%async_computation.1 | async-start | bytes 524288 | tf_op jit(solution)/shard_map/all_to_all | solution.py:17
  20.4 32.4 %collective-permute-start.8 = (bf16[132,1024]{1,0:T(8,128)(2,1)S(1)}, bf16[132,1024]{1,0:T(8,128)(2,1)S(1)}, u32[]{:S(2)}, u32[]{:S(2)}) collective-permute-start(bf16[132,1024]{1,0:T(8,128)(2,1)S(1)} %pad_maximum_fusion.2), channel_id=1, source_target_pairs={{0,1},{1,0},{2,3},{3,2},{4,5},{5,4},{6,7},{7,6},{8,9},{9,8},{10,11... | collective-permute-start | bytes 811016 | tf_op jit(solution)/shard_map/ppermute | solution.py:32
  34.2 18.6 %copy-start.8 = (bf16[1024,4,32]{0,2,1:T(8,128)(2,1)S(1)}, bf16[1024,4,32]{0,2,1:T(8,128)(2,1)}, u32[]{:S(2)}) copy-start(bf16[1024,4,32]{0,2,1:T(8,128)(2,1)} %param.16) | copy-start | bytes 786436
  34.2 23.3 %collective-permute-start.5 = (bf16[128,1024]{1,0:T(8,128)(2,1)S(1)}, bf16[128,1024]{1,0:T(8,128)(2,1)S(1)}, u32[]{:S(2)}, u32[]{:S(2)}) collective-permute-start(bf16[128,1024]{1,0:T(8,128)(2,1)S(1)} %bitcast.74), channel_id=1, source_target_pairs={{0,30},{1,31},{2,0},{3,1},{4,2},{5,3},{6,4},{7,5},{8,6},{9,7},{10,... | collective-permute-start | bytes 786440 | tf_op jit(solution)/shard_map/ppermute | solution.py:28
  38.5 18.9 %collective-permute-start.4 = (bf16[128,1024]{1,0:T(8,128)(2,1)S(1)}, bf16[128,1024]{1,0:T(8,128)(2,1)S(1)}, u32[]{:S(2)}, u32[]{:S(2)}) collective-permute-start(bf16[128,1024]{1,0:T(8,128)(2,1)S(1)} %bitcast.75), channel_id=1, source_target_pairs={{0,2},{1,3},{2,4},{3,5},{4,6},{5,7},{6,8},{7,9},{8,10},{9,11},{10,... | collective-permute-start | bytes 786440 | tf_op jit(solution)/shard_map/ppermute | solution.py:28
  45.4 11.8 %collective-permute-start.6 = (bf16[64,1024]{1,0:T(8,128)(2,1)}, bf16[64,1024]{1,0:T(8,128)(2,1)S(1)}, u32[]{:S(2)}, u32[]{:S(2)}) collective-permute-start(bf16[64,1024]{1,0:T(8,128)(2,1)} %bitcast.13), channel_id=1, source_target_pairs={{0,4},{1,5},{2,6},{3,7},{4,8},{5,9},{6,10},{7,11},{8,12},{9,13},{1... | collective-permute-start | bytes 393224 | tf_op jit(solution)/shard_map/ppermute | solution.py:28
  49.2 8.3 %collective-permute-start.7 = (bf16[64,1024]{1,0:T(8,128)(2,1)}, bf16[64,1024]{1,0:T(8,128)(2,1)S(1)}, u32[]{:S(2)}, u32[]{:S(2)}) collective-permute-start(bf16[64,1024]{1,0:T(8,128)(2,1)} %bitcast.14), channel_id=1, source_target_pairs={{0,28},{1,29},{2,30},{3,31},{4,0},{5,1},{6,2},{7,3},{8,4},{9,5},{1... | collective-permute-start | bytes 393224 | tf_op jit(solution)/shard_map/ppermute | solution.py:28
  52.9 1.0 copy-start
  54.0 5.6 %copy-start.3 = (bf16[256,1024]{1,0:T(8,128)(2,1)}, bf16[256,1024]{1,0:T(8,128)(2,1)S(1)}, u32[]{:S(2)}) copy-start(bf16[256,1024]{1,0:T(8,128)(2,1)S(1)} %pad_maximum_fusion.1.weights) | copy-start | bytes 1572868
  54.0 5.6 %copy-start.2 = (bf16[512,1024]{1,0:T(8,128)(2,1)S(1)}, bf16[512,1024]{1,0:T(8,128)(2,1)}, u32[]{:S(2)}) copy-start(bf16[512,1024]{1,0:T(8,128)(2,1)} %table.1) | copy-start | bytes 3145732
  54.0 12.3 %collective-permute-start.10 = (bf16[256,1024]{1,0:T(8,128)(2,1)S(1)}, bf16[256,1024]{1,0:T(8,128)(2,1)S(1)}, u32[]{:S(2)}, u32[]{:S(2)}) collective-permute-start(bf16[256,1024]{1,0:T(8,128)(2,1)S(1)} %copy-done), channel_id=1, source_target_pairs={{0,1},{1,0},{2,3},{3,2},{4,5},{5,4},{6,7},{7,6},{8,9},{9,8},{10,11... | collective-permute-start | bytes 1572872 | tf_op jit(solution)/shard_map/ppermute | solution.py:32
  60.2 9.6 %collective-permute-start.9 = (bf16[320,256]{1,0:T(8,128)(2,1)}, bf16[320,256]{1,0:T(8,128)(2,1)S(1)}, u32[]{:S(2)}, u32[]{:S(2)}) collective-permute-start(bf16[320,256]{1,0:T(8,128)(2,1)} %get-tuple-element.87), channel_id=1, source_target_pairs={{0,1},{1,0},{2,3},{3,2},{4,5},{5,4},{6,7},{7,6},{8,9},{9,8},{10,11... | collective-permute-start | bytes 491528 | tf_op jit(solution)/shard_map/ppermute | solution.py:32
  71.6 6.1 %copy-start.1 = (bf16[256,1024]{1,0:T(8,128)(2,1)S(1)}, bf16[256,1024]{1,0:T(8,128)(2,1)}, u32[]{:S(2)}) copy-start(bf16[256,1024]{1,0:T(8,128)(2,1)} %refs_3_.1) | copy-start | bytes 1572868
  71.6 45.5 %all-to-all-start.2 = ((bf16[16,16,768]{2,1,0:T(8,128)(2,1)}), bf16[16,16,768]{2,1,0:T(8,128)(2,1)S(1)}, u32[]{:S(2)}, u32[]{:S(2)}) async-start(bf16[16,16,768]{2,1,0:T(8,128)(2,1)} %get-tuple-element.92), calls=%async_computation.2 | async-start | bytes 786432 | tf_op jit(solution)/shard_map/all_to_all | solution.py:17
  77.7 39.3 %collective-permute-start.11 = (bf16[256,1024]{1,0:T(8,128)(2,1)S(1)}, bf16[256,1024]{1,0:T(8,128)(2,1)S(1)}, u32[]{:S(2)}, u32[]{:S(2)}) collective-permute-start(bf16[256,1024]{1,0:T(8,128)(2,1)S(1)} %copy-done.1), channel_id=1, source_target_pairs={{0,1},{1,0},{2,3},{3,2},{4,5},{5,4},{6,7},{7,6},{8,9},{9,8},{10,11... | collective-permute-start | bytes 1572872 | tf_op jit(solution)/shard_map/ppermute | solution.py:32
  81.5 0.7 copy-start.10
  122.3 42.8 %all-to-all-start.3 = ((bf16[16,16,1024]{2,1,0:T(8,128)(2,1)}), bf16[16,16,1024]{2,1,0:T(8,128)(2,1)S(1)}, u32[]{:S(2)}, u32[]{:S(2)}) async-start(bf16[16,16,1024]{2,1,0:T(8,128)(2,1)} %bitcast.20), calls=%async_computation.3 | async-start | bytes 1048576 | tf_op jit(solution)/shard_map/all_to_all | solution.py:17
  133.3 9.5 %collective-permute-start.14 = (bf16[1024,128]{1,0:T(8,128)(2,1)S(1)}, bf16[1024,128]{1,0:T(8,128)(2,1)S(1)}, u32[]{:S(2)}, u32[]{:S(2)}) collective-permute-start(bf16[1024,128]{1,0:T(8,128)(2,1)S(1)} %bitcast.77), channel_id=1, source_target_pairs={{0,384},{32,416},{64,448},{96,480},{128,0},{160,32},{192,64},{224,... | collective-permute-start | bytes 786440 | tf_op jit(solution)/shard_map/ppermute | solution.py:41
  137.9 8.7 %collective-permute-start.13 = (bf16[1024,128]{1,0:T(8,128)(2,1)S(1)}, bf16[1024,128]{1,0:T(8,128)(2,1)S(1)}, u32[]{:S(2)}, u32[]{:S(2)}) collective-permute-start(bf16[1024,128]{1,0:T(8,128)(2,1)S(1)} %bitcast.78), channel_id=1, source_target_pairs={{0,256},{32,288},{64,320},{96,352},{128,384},{160,416},{192,448},{... | collective-permute-start | bytes 786440 | tf_op jit(solution)/shard_map/ppermute | solution.py:41
  140.2 9.5 %collective-permute-start.12 = (bf16[1024,128]{1,0:T(8,128)(2,1)S(1)}, bf16[1024,128]{1,0:T(8,128)(2,1)S(1)}, u32[]{:S(2)}, u32[]{:S(2)}) collective-permute-start(bf16[1024,128]{1,0:T(8,128)(2,1)S(1)} %bitcast.79), channel_id=1, source_target_pairs={{0,128},{32,160},{64,192},{96,224},{128,256},{160,288},{192,320},{... | collective-permute-start | bytes 786440 | tf_op jit(solution)/shard_map/ppermute | solution.py:41
  150.8 13.0 %collective-permute-start.15 = (bf16[4,1024,128]{2,1,0:T(8,128)(2,1)}, bf16[4,1024,128]{2,1,0:T(8,128)(2,1)}, u32[]{:S(2)}, u32[]{:S(2)}) collective-permute-start(bf16[4,1024,128]{2,1,0:T(8,128)(2,1)} %pad_maximum_fusion), channel_id=1, source_target_pairs={{0,32},{32,0},{64,96},{96,64},{128,160},{160,128},{192,224},{224,1... | collective-permute-start | bytes 3145736 | tf_op jit(solution)/shard_map/ppermute | solution.py:36
  162.7 1.0 copy-start.11

commit v5 on v4

--- a/solution.py
+++ b/solution.py
@@ -41,12 +41,11 @@
     return lax.ppermute(block, "batch", [(i, (i + 4 * shift) % count) for i in range(count)])
 
 
-def gather_slots(block):
+def gather_slots(blocks):
     column = lax.axis_size("seq") // 2
-    far_places = column // near_places
     far = groups_of([list(range(at, column, near_places)) for at in range(near_places)])
-    blocks = exchange(jnp.broadcast_to(block[None], (far_places,) + block.shape), far)
-    rows = blocks.reshape(far_places * block.shape[0], block.shape[1])
+    blocks = exchange(blocks, far)
+    rows = blocks.reshape(blocks.shape[0] * blocks.shape[1], blocks.shape[2])
     half = rows.shape[0] // 2
     return (
         rows,
@@ -70,43 +69,72 @@
 
 
 def silu(value):
-    return value * (0.5 + 0.5 * jnp.tanh(0.5 * value))
+    return half_silu(0.5 * value)
+
+
+def half_silu(half):
+    return half + half * jnp.tanh(half)
 
 
 def marked(condition):
     return condition.astype(jnp.float32).astype(jnp.bfloat16)
 
 
-def pick_kernel(numbers, ids, table, packed, slots, pair_slots, most):
+def earlier(count):
+    return lax.broadcasted_iota(jnp.int32, (count, count), 0) < lax.broadcasted_iota(
+        jnp.int32, (count, count), 1
+    )
+
+
+def pick_kernel(numbers, ids, table, packed):
     rows, count = table.shape[0], ids.shape[1]
-    index, first_rank, devices = numbers[0], numbers[1], most.shape[0]
-    place, side = index // 2, lax.rem(index, 2)
-    slot_count = packed.shape[0]
-    shard_lanes = ids[...] // rows
-    shards = lax.broadcasted_iota(jnp.int32, (most.shape[0], count), 0)
-    member = shards == shard_lanes
-    before = lax.broadcasted_iota(jnp.int32, (count, count), 0) < lax.broadcasted_iota(
-        jnp.int32, (count, count), 1
-    )
-    ranks = jnp.dot(marked(member), marked(before), preferred_element_type=jnp.float32)
-    rank = jnp.sum(jnp.where(member, ranks, 0.0), axis=0, keepdims=True)
-    counts = jnp.sum(member.astype(jnp.float32), axis=1, keepdims=True)
-    most[...] = jnp.broadcast_to(
-        jnp.max(counts, axis=0, keepdims=True), most.shape
-    ).astype(jnp.int32)
-    slot = rank.astype(jnp.int32) - first_rank
-    there = ids[...] - index * rows
-    own_slot = jnp.where((there >= 0) & (there < rows), slot, -1)
-    taken = own_slot == lax.broadcasted_iota(jnp.int32, (slot_count, count), 0)
+    copies, slot_count, _ = packed.shape
+    there = ids[...] - numbers[0] * rows
+    here = (there >= 0) & (there < rows)
+    marks = jnp.broadcast_to(here.astype(jnp.float32), (8, count)).astype(jnp.bfloat16)
+    rank = jnp.dot(marks, marked(earlier(count)), preferred_element_type=jnp.float32)[:1]
+    slot = jnp.where(here, rank.astype(jnp.int32) - numbers[1], -1)
+    taken = slot == lax.broadcasted_iota(jnp.int32, (slot_count, count), 0)
     wanted = there == lax.broadcasted_iota(jnp.int32, (rows, count), 0)
     picks = lax.dot_general(
         marked(taken), marked(wanted), (((1,), (1,)), ((), ())), preferred_element_type=jnp.float32
     ).astype(jnp.bfloat16)
-    packed[...] = jnp.dot(picks, table[...], preferred_element_type=jnp.float32).astype(
-        jnp.bfloat16
-    )
-    source = shard_lanes // 2
-    inside = (shard_lanes - 2 * source == side) & (slot >= 0) & (slot < slot_count)
+    found = jnp.dot(picks, table[...], preferred_element_type=jnp.float32).astype(jnp.bfloat16)
+    for copy in range(copies):
+        packed[copy] = found
+
+
+def pick(numbers, ids, table, copies):
+    whole = pl.BlockSpec(memory_space=pltpu.VMEM)
+    return pl.pallas_call(
+        pick_kernel,
+        in_specs=[pl.BlockSpec(memory_space=pltpu.SMEM), whole, whole],
+        out_specs=whole,
+        out_shape=jax.ShapeDtypeStruct((copies, slot_rows, table.shape[1]), jnp.bfloat16),
+        compiler_params=pltpu.CompilerParams(vmem_limit_bytes=32 * 1024 * 1024),
+        cost_estimate=pl.CostEstimate(
+            flops=2 * slot_rows * table.shape[0] * table.shape[1],
+            bytes_accessed=2 * table.shape[0] * table.shape[1],
+            transcendentals=0,
+        ),
+    )(numbers, ids.reshape(1, -1), table)
+
+
+def locate_kernel(table_rows, numbers, ids, slots, pair_slots, most):
+    count, devices = ids.shape[1], most.shape[0]
+    index = numbers[0]
+    place, side = index // 2, lax.rem(index, 2)
+    shard = ids[...] // table_rows
+    member = lax.broadcasted_iota(jnp.int32, (devices, count), 0) == shard
+    ranks = jnp.dot(marked(member), marked(earlier(count)), preferred_element_type=jnp.float32)
+    rank = jnp.sum(jnp.where(member, ranks, 0.0), axis=0, keepdims=True)
+    counts = jnp.sum(member.astype(jnp.float32), axis=1, keepdims=True)
+    most[...] = jnp.broadcast_to(jnp.max(counts, axis=0, keepdims=True), most.shape).astype(
+        jnp.int32
+    )
+    slot = rank.astype(jnp.int32) - numbers[1]
+    source = shard // 2
+    inside = (shard - 2 * source == side) & (slot >= 0) & (slot < slot_rows)
     ahead = lax.rem(source - place + devices, near_places)
     piece = jnp.where(ahead == 0, 0, jnp.where(ahead == near_places - 1, 1, ahead + 1))
     block = piece * (devices // 2 // near_places) + source // near_places
@@ -123,7 +151,7 @@
             marked(chosen), facts, (((1,), (1,)), ((), ())), preferred_element_type=jnp.float32
         )
         block_at, slot_at = both[:, :1].astype(jnp.int32), both[:, 8:9].astype(jnp.int32)
-        out[...] = jnp.where(block_at < 0, -1, block_at * slot_count + slot_at)
+        out[...] = jnp.where(block_at < 0, -1, block_at * slot_rows + slot_at)
 
     own = count // devices
     at = lax.broadcasted_iota(jnp.int32, (count, count), 0)
@@ -139,30 +167,27 @@
     spread(original == lax.broadcasted_iota(jnp.int32, (2 * own, count), 1), pair_slots)
 
 
-def pick(numbers, ids, table, devices):
+def locate(numbers, ids, table_rows, devices):
     whole = pl.BlockSpec(memory_space=pltpu.VMEM)
     count = ids.shape[0]
     return pl.pallas_call(
-        pick_kernel,
-        in_specs=[pl.BlockSpec(memory_space=pltpu.SMEM), whole, whole],
-        out_specs=[whole] * 4,
+        lambda *refs: locate_kernel(table_rows, *refs),
+        in_specs=[pl.BlockSpec(memory_space=pltpu.SMEM), whole],
+        out_specs=[whole] * 3,
         out_shape=[
-            jax.ShapeDtypeStruct((slot_rows, table.shape[1]), jnp.bfloat16),
             jax.ShapeDtypeStruct((count, 1), jnp.int32),
             jax.ShapeDtypeStruct((2 * count // devices, 1), jnp.int32),
             jax.ShapeDtypeStruct((devices, 128), jnp.int32),
         ],
         compiler_params=pltpu.CompilerParams(vmem_limit_bytes=32 * 1024 * 1024),
         cost_estimate=pl.CostEstimate(
-            flops=2 * slot_rows * table.shape[0] * table.shape[1],
-            bytes_accessed=2 * table.shape[0] * table.shape[1],
-            transcendentals=0,
-        ),
-    )(numbers, ids.reshape(1, -1), table)
+            flops=2 * count * count * devices, bytes_accessed=8 * count, transcendentals=0
+        ),
+    )(numbers, ids.reshape(1, -1))
 
 
 def project_kernel(at, at_pair, rows_0, rows_1, rows_2, rows_3, rows_4, weights, *rest):
-    proj_mine, proj_other, own_rows, slots = rest
+    proj_mine, proj_other, own_rows, slots = rest[-4:]
     cand_side, columns = proj_mine.shape
     own, width = own_rows.shape
     first = 0
@@ -201,13 +226,16 @@
         ].astype(jnp.bfloat16)
 
 
-def project(at, at_pair, rows, weights):
+def project(at, at_pair, rows, weights, ready):
     columns, width = weights.shape
     cand_side = at.shape[0] // 2
     own = at_pair.shape[0] // 2
     slot_count = sum(piece.shape[0] for piece in rows)
+    whole = pl.BlockSpec(memory_space=pltpu.VMEM)
     return pl.pallas_call(
         project_kernel,
+        in_specs=[whole] * (3 + len(rows)) + [pl.BlockSpec(memory_space=pl.ANY)] * len(ready),
+        out_specs=[whole] * 3,
         out_shape=[
             jax.ShapeDtypeStruct((cand_side, columns), jnp.bfloat16),
             jax.ShapeDtypeStruct((cand_side + own * width // columns, columns), jnp.bfloat16),
@@ -220,7 +248,7 @@
             bytes_accessed=2 * (slot_count + columns) * width,
             transcendentals=slot_count * columns,
         ),
-    )(at, at_pair, *rows, weights)
+    )(at, at_pair, *rows, weights, *ready)
 
 
 def pack_kernel(feature_here, mine, arrived, own_rows, w_slice, *rest):
@@ -235,11 +263,7 @@
             own_rows[:, lanes].astype(jnp.float32) + other.astype(jnp.float32)
         ).astype(jnp.bfloat16)
     block = 4 * feature_here
-    query = jnp.concatenate(
-        [proj[:, side * block + 2 * feature_here : side * block + 3 * feature_here] for side in (0, 1)],
-        axis=1,
-    )
-    queries[...] = query.T.astype(jnp.bfloat16)
+    queries[...] = proj[:, block : block + 2 * feature_here].T.astype(jnp.bfloat16)
     column, own, _ = packed.shape
     columns = 2 * block
     packed[:, :, :columns] = proj.astype(jnp.bfloat16).reshape(column, own, columns)
@@ -250,7 +274,7 @@
         )
 
 
-def pack(mine, arrived, own_rows, w_slice, ready, feature_here):
+def pack(mine, arrived, own_rows, w_slice, feature_here):
     cand_side, columns = mine.shape
     own = own_rows.shape[0]
     column = cand_side // own
@@ -258,7 +282,7 @@
     whole = pl.BlockSpec(memory_space=pltpu.VMEM)
     return pl.pallas_call(
         lambda *refs: pack_kernel(feature_here, *refs),
-        in_specs=[whole] * 4 + [pl.BlockSpec(memory_space=pl.ANY)] * len(ready),
+        in_specs=[whole] * 4,
         out_specs=[whole] * 3,
         out_shape=[
             jax.ShapeDtypeStruct((2 * feature_here, cand_side), jnp.bfloat16),
@@ -269,46 +293,59 @@
         cost_estimate=pl.CostEstimate(
             flops=cand_side * columns, bytes_accessed=8 * cand_side * columns, transcendentals=0
         ),
-    )(mine, arrived, own_rows, w_slice, *ready)
-
-
-def attend_kernel(scale, *refs):
+    )(mine, arrived, own_rows, w_slice)
+
+
+def attend_kernel(scale, heads, *refs):
     queries, keys_a, keys_b, values_a, values_b, bias_a, bias_b, live_a, live_b = refs[:9]
     summed = refs[-2]
-    head = pl.program_id(0)
-    head_queries = queries[...].T
-    total = None
-    for keys, values, bias, live in (
-        (keys_a, values_a, bias_a, live_a),
-        (keys_b, values_b, bias_b, live_b),
-    ):
-        scores = lax.dot_general(
-            head_queries, keys[...], (((1,), (1,)), ((), ())), preferred_element_type=jnp.float32
-        )
-        weights = silu(scores * scale + bias[pl.ds(head, 1), :])
-        weights = jnp.where(live[...] > 0.0, weights, 0.0).astype(jnp.bfloat16)
-        part = jnp.dot(weights, values[...], preferred_element_type=jnp.float32)
-        total = part if total is None else total + part
-    summed[...] = total.astype(summed.dtype)
-
-
-def attend(queries, keys, values, bias, live, head_count, through):
+    first_head = pl.program_id(0) * heads
+    head_size = keys_a.shape[1] // heads
+    for head in range(heads):
+        lanes = slice(head * head_size, (head + 1) * head_size)
+        head_queries = queries[lanes, :].T
+        total = None
+        for keys, values, bias, live in (
+            (keys_a, values_a, bias_a, live_a),
+            (keys_b, values_b, bias_b, live_b),
+        ):
+            scores = lax.dot_general(
+                head_queries,
+                keys[:, lanes],
+                (((1,), (1,)), ((), ())),
+                preferred_element_type=jnp.float32,
+            )
+            half_bias = 0.5 * bias[pl.ds(first_head + head, 1), :]
+            weights = half_silu(scores * (0.5 * scale) + half_bias)
+            weights = jnp.where(live[...] > 0.0, weights, 0.0).astype(jnp.bfloat16)
+            part = jnp.dot(weights, values[:, lanes], preferred_element_type=jnp.float32)
+            total = part if total is None else total + part
+        summed[:, lanes] = total.astype(summed.dtype)
+
+
+def attend(queries, keys, values, keys_other, values_other, bias, live, head_count, through):
     width, cand = queries.shape
-    events = keys[0].shape[0]
+    events = keys.shape[0]
     head_size = width // head_count
-    event_spec = pl.BlockSpec((events, head_size), lambda h: (0, h))
+    heads = 4
+    lanes = heads * head_size
     bias_spec = pl.BlockSpec((head_count, events), lambda h: (0, 0))
     live_spec = pl.BlockSpec((1, events), lambda h: (0, 0))
     held = pl.BlockSpec(memory_space=pl.ANY)
     return pl.pallas_call(
-        lambda *refs: attend_kernel(head_size ** (-0.5), *refs),
-        grid=(head_count,),
-        in_specs=[pl.BlockSpec((head_size, cand), lambda h: (h, 0))]
-        + [event_spec] * 4
+        lambda *refs: attend_kernel(head_size ** (-0.5), heads, *refs),
+        grid=(head_count // heads,),
+        in_specs=[
+            pl.BlockSpec((lanes, cand), lambda h: (h, 0)),
+            pl.BlockSpec((events, lanes), lambda h: (0, h)),
+            pl.BlockSpec((events, lanes), lambda h: (0, h)),
+            pl.BlockSpec((events, lanes), lambda h: (0, h)),
+            pl.BlockSpec((events, lanes), lambda h: (0, h)),
+        ]
         + [bias_spec] * 2
         + [live_spec] * 2
         + [held],
-        out_specs=[pl.BlockSpec((cand, head_size), lambda h: (0, h)), held],
+        out_specs=[pl.BlockSpec((cand, lanes), lambda h: (0, h)), held],
         out_shape=[
             jax.ShapeDtypeStruct((cand, width), jnp.bfloat16),
             jax.ShapeDtypeStruct(through.shape, through.dtype),
@@ -320,7 +357,47 @@
             bytes_accessed=8 * events * width + 4 * cand * width,
             transcendentals=2 * cand * events * head_count,
         ),
-    )(queries, *keys, *values, *bias, *live, through)
+    )(queries, keys, keys_other, values, values_other, *bias, *live, through)
+
+
+def own_kernel(scale, rab, received, gain, self_term, gate):
+    own, width = self_term.shape
+    column = received.shape[0]
+    lanes = width // column
+    gate_u, own_v, own_queries, own_k = (
+        jnp.concatenate(
+            [
+                received[place, :, part * lanes : (part + 1) * lanes].astype(jnp.float32)
+                for place in range(column)
+            ],
+            axis=1,
+        )
+        for part in range(4)
+    )
+    gate[...] = gate_u * gain[...]
+    products = own_queries * own_k
+    head_count = rab.shape[0]
+    head_size = width // head_count
+    for head in range(head_count):
+        head_lanes = slice(head * head_size, (head + 1) * head_size)
+        score = jnp.sum(products[:, head_lanes], axis=1, keepdims=True) * scale + rab[head, 0]
+        self_term[:, head_lanes] = silu(score) * own_v[:, head_lanes]
+
+
+def own_parts(received, rab, gain, own):
+    width = gain.shape[0]
+    whole = pl.BlockSpec(memory_space=pltpu.VMEM)
+    scale = (width // rab.shape[0]) ** (-0.5)
+    return pl.pallas_call(
+        lambda *refs: own_kernel(scale, *refs),
+        in_specs=[pl.BlockSpec(memory_space=pltpu.SMEM), whole, whole],
+        out_specs=[whole] * 2,
+        out_shape=[jax.ShapeDtypeStruct((own, width), jnp.float32)] * 2,
+        compiler_params=pltpu.CompilerParams(vmem_limit_bytes=32 * 1024 * 1024),
+        cost_estimate=pl.CostEstimate(
+            flops=8 * own * width, bytes_accessed=32 * own * width, transcendentals=own
+        ),
+    )(rab, received, gain.reshape(1, -1))
 
 
 def finish_kernel(numbers, parts, self_term, gate, embedded, *rest):
@@ -374,8 +451,6 @@
     row_count = lax.axis_size("batch") // 4
     events_here, width = history_keys.shape
     head_count = rab.shape[0]
-    head_size = width // head_count
-    scale = head_size ** (-0.5)
     table_rows = item_table.shape[0]
     cand_total = item_ids.shape[0]
     cand_here = cand_total // device_count
@@ -387,40 +462,50 @@
     w_slice = lax.dynamic_slice_in_dim(w_out, (core * row_count + row) * out_lanes, out_lanes, 1)
     slice_rows = w_slice.shape[0]
 
-    def lookup(first_rank, send):
-        numbers = jnp.stack([index_here, first_rank])
-        packed, slots, pair_slots, most = pick(numbers, item_ids, item_table, device_count)
-        packed, send = lax.optimization_barrier((packed, send))
-        rows = gather_slots(packed)
-        return rows, slots, pair_slots, most[0, 0], [swap_pair(block) for block in send]
-
+    far_places = column // near_places
     w_mine = w_proj.transpose(1, 2, 0).reshape(4 * feature_here, width)
-    w_send = jnp.concatenate([w_mine, w_slice.reshape(-1, width)])
-    rows, slots, pair_slots, most, (w_other, keys_other, values_other) = lookup(
-        jnp.int32(0), (w_send, history_keys, history_values)
-    )
+
+    def numbers_at(first_rank):
+        return jnp.stack([index_here, first_rank])
+
+    picked = pick(numbers_at(jnp.int32(0)), item_ids, item_table, far_places)
+    picked, w_sent, *sent = lax.optimization_barrier(
+        (picked, w_mine, history_values, history_keys, w_slice)
+    )
+    values_sent, keys_sent, slice_sent = sent
+    rows = gather_slots(picked)
+    w_other = swap_pair(jnp.concatenate([w_sent, slice_sent.reshape(-1, width)]))
     slice_other = w_other[4 * feature_here :].reshape(w_slice.shape)
     w_other = w_other[: 4 * feature_here]
-    keys, values = (history_keys, keys_other), (history_values, values_other)
-    w_pair = jnp.concatenate(
-        [jnp.where(side == 0, w_mine, w_other), jnp.where(side == 0, w_other, w_mine)]
-    )
+    keys_other, values_other = swap_pair(keys_sent), swap_pair(values_sent)
+    w_pair = jnp.stack(
+        [
+            jnp.where(side == 0, w_mine, w_other).reshape(4, feature_here, width),
+            jnp.where(side == 0, w_other, w_mine).reshape(4, feature_here, width),
+        ],
+        axis=1,
+    ).reshape(8 * feature_here, width)
     slices = jnp.concatenate(
         [jnp.where(side == 0, w_slice, slice_other), jnp.where(side == 0, slice_other, w_slice)]
     )
-    found = tuple(project(slots, pair_slots, rows, w_pair))
+    slots, pair_slots, most = locate(
+        numbers_at(jnp.int32(0)), item_ids, table_rows, device_count
+    )
+    found = tuple(project(slots, pair_slots, rows, w_pair, (keys_other, values_other)))
 
     def another(state):
         first_rank, found = state
-        rows, slots, pair_slots, _, _ = lookup(first_rank, ())
-        more = project(slots, pair_slots, rows, w_pair)
+        numbers = numbers_at(first_rank)
+        rows = gather_slots(pick(numbers, item_ids, item_table, far_places))
+        slots, pair_slots, _ = locate(numbers, item_ids, table_rows, device_count)
+        more = project(slots, pair_slots, rows, w_pair, ())
         return first_rank + slot_rows, tuple(a + b for a, b in zip(found, more))
 
     _, (proj_mine, proj_other, own_rows) = lax.while_loop(
-        lambda state: state[0] < most, another, (jnp.int32(slot_rows), found)
+        lambda state: state[0] < most[0, 0], another, (jnp.int32(slot_rows), found)
     )
     side_queries, packed, embedded = pack(
-        proj_mine, swap_pair(proj_other), own_rows, slices, (keys_other,), feature_here
+        proj_mine, swap_pair(proj_other), own_rows, slices, feature_here
     )
     received = exchange(packed, column_groups())
     all_queries = lax.all_gather(
@@ -435,24 +520,20 @@
         )
 
     bias, live = zip(bias_of(index_here), bias_of(index_here + 1 - 2 * side))
-    summed, received = attend(all_queries, keys, values, bias, live, head_count, received)
+    summed, received = attend(
+        all_queries,
+        history_keys,
+        history_values,
+        keys_other,
+        values_other,
+        bias,
+        live,
+        head_count,
+        received,
+    )
     parts = exchange(summed.reshape(column, cand_here, width), column_groups())
 
-    own_proj = (
-        received[:, :, : 8 * feature_here]
-        .reshape(column, cand_here, 2, 4, feature_here)
-        .transpose(3, 1, 0, 2, 4)
-        .reshape(4, cand_here, width)
-        .astype(jnp.float32)
-    )
-    gate_u, own_v, own_queries, own_k = own_proj[0], own_proj[1], own_proj[2], own_proj[3]
-    self_scores = jnp.sum((own_queries * own_k).reshape(cand_here, head_count, head_size), axis=2)
-    self_scores = self_scores * scale + rab[:, 0][None, :]
-    self_term = jax.nn.silu(self_scores)[:, :, None] * own_v.reshape(
-        cand_here, head_count, head_size
-    )
-    self_term = self_term.reshape(cand_here, width)
-    gate = norm_gain[None, :] * gate_u
+    self_term, gate = own_parts(received, rab, norm_gain, cand_here)
 
     w_here = (
         received[:, :, 8 * feature_here :]

time: 168 us -> 160 us (0.952)
  waiting for transfers between devices: 23 us -> 15.3 us
  local copies, waits for them, and re-layouts: 7.63 us -> 4.1 us
    all_to_all x3, waiting for transfers between devices: 10.2 us -> 3.63 us  [exchange(): lax.all_to_all(blocks, 'seq', split_axis=0, concat_axis=0, tiled=True, ax...]
    ppermute x4, waiting for transfers between devices: 5.75 us -> 2.44 us  [swap_pair(): lax.ppermute(block, 'seq', [(i, i ^ 1) for i in range(lax.axis_size('seq'...]
    ppermute x1, starting transfers between devices: 10.2 us -> 12.6 us  [swap_core(): lax.ppermute(block, 'batch', [(i, i ^ 1) for i in range(lax.axis_size('ba...]
    select_n x1, other arithmetic: 0.06 us -> 1.8 us  [local(): jnp.where(side == 0, w_mine, w_other).reshape(4, feature_here, width)]
    pallas_call x2 -> x4, Pallas kernels: 7.31 us -> 7.72 us  [the longest x1 3.2 us: attend(): pl.pallas_call(lambda *refs: attend_kernel(head_size ** (-0.5), heads, *r...]
  transfers between devices with their start and end apart: 15 -> 15, of which waited for: 6 -> 6; matrix products, arithmetic and copies ran while one was open for 5% -> 4% of each run, Pallas kernels for 1% -> 2%
where the time goes in v5:
time: 160 us; the launch traced here: 159 us
  starting transfers between devices  83.8 us (52%)
  blocking collectives  36.2 us (23%)
  waiting for transfers between devices  15.3 us (10%)
  Pallas kernels  13.8 us (9%)
  local copies, waits for them, and re-layouts  4.1 us (3%)
  other arithmetic  4.04 us (3%)
    all_gather x1, blocking collectives, local(): lax.all_gather(side_queries, 'seq', axis=0, tiled=True, axis_index_groups...  36.2 us
    all_to_all x3, starting transfers between devices, exchange(): lax.all_to_all(blocks, 'seq', split_axis=0, concat_axis=0, tiled=True, ax...  32.3 us
    ppermute x4, starting transfers between devices, from_place(): lax.ppermute(block, 'seq', [(i, (i + 2 * shift) % count) for i in range(c...  17.8 us
    ppermute x1, starting transfers between devices, swap_core(): lax.ppermute(block, 'batch', [(i, i ^ 1) for i in range(lax.axis_size('ba...  12.6 us
    ppermute x4, starting transfers between devices, swap_pair(): lax.ppermute(block, 'seq', [(i, i ^ 1) for i in range(lax.axis_size('seq'...  11.5 us
    ppermute x3, starting transfers between devices, from_row(): lax.ppermute(block, 'batch', [(i, (i + 4 * shift) % count) for i in range...  9.54 us
    ppermute x3, waiting for transfers between devices, from_row(): lax.ppermute(block, 'batch', [(i, (i + 4 * shift) % count) for i in range...  6.84 us
    all_to_all x3, waiting for transfers between devices, exchange(): lax.all_to_all(blocks, 'seq', split_axis=0, concat_axis=0, tiled=True, ax...  3.63 us
  transfers between devices with their start and end apart: 15, of which 6 were waited for; matrix products, arithmetic and copies ran while one was open for 4% of the time, Pallas kernels for 2%

profile of v5, /device:TPU:1, one launch (start us, length us, event | category | flops | bytes accessed | tf_op | source)
XLA Modules:
  0.0 159.0 jit_solution(2087670505319465139)
XLA Ops:
  0.0 0.1 pad_add_fusion.2.refs_0_.numbers
  0.1 0.7 constant_dynamic-slice_fusion
  0.8 2.6 %shard_map.92 = bf16[4,32,1024]{2,1,0:T(8,128)(2,1)} custom-call(s32[2]{0:T(128)S(1)} %pad_add_fusion.2.refs_0_.numbers, s32[1,512]{1,0:T(1,128)S(1)} %bitcast.95, bf16[512,1024]{1,0:T(8,128)(2,1)} %table.1), custom_call_target="tpu_custom_call" | custom-call | flops 33554432 | bytes 1048576 | tf_op jit(solution)/shard_map/pallas_call | solution.py:109
  3.4 15.8 %all-to-all-start.1 = ((bf16[4,32,1024]{2,1,0:T(8,128)(2,1)}), bf16[4,32,1024]{2,1,0:T(8,128)(2,1)S(1)}, u32[]{:S(2)}, u32[]{:S(2)}) async-start(bf16[4,32,1024]{2,1,0:T(8,128)(2,1)} %shard_map.92), calls=%async_computation.1 | async-start | bytes 524288 | tf_op jit(solution)/shard_map/all_to_all | solution.py:17
  19.2 3.1 %collective-permute-start.9 = (bf16[256,1024]{1,0:T(8,128)(2,1)S(1)}, bf16[256,1024]{1,0:T(8,128)(2,1)S(1)}, u32[]{:S(2)}, u32[]{:S(2)}) collective-permute-start(bf16[256,1024]{1,0:T(8,128)(2,1)S(1)} %copy-done), channel_id=1, source_target_pairs={{0,1},{1,0},{2,3},{3,2},{4,5},{5,4},{6,7},{7,6},{8,9},{9,8},{10,11... | collective-permute-start | bytes 1572872 | tf_op jit(solution)/shard_map/ppermute | solution.py:32
  22.4 2.2 %collective-permute-start.8 = (bf16[132,1024]{1,0:T(8,128)(2,1)S(1)}, bf16[132,1024]{1,0:T(8,128)(2,1)}, u32[]{:S(2)}, u32[]{:S(2)}) collective-permute-start(bf16[132,1024]{1,0:T(8,128)(2,1)S(1)} %pad_maximum_fusion.2), channel_id=1, source_target_pairs={{0,1},{1,0},{2,3},{3,2},{4,5},{5,4},{6,7},{7,6},{8,9},{9,8},{10,11... | collective-permute-start | bytes 811016 | tf_op jit(solution)/shard_map/ppermute | solution.py:32
  24.5 3.1 %collective-permute-start.10 = (bf16[256,1024]{1,0:T(8,128)(2,1)S(1)}, bf16[256,1024]{1,0:T(8,128)(2,1)S(1)}, u32[]{:S(2)}, u32[]{:S(2)}) collective-permute-start(bf16[256,1024]{1,0:T(8,128)(2,1)S(1)} %copy-done.1), channel_id=1, source_target_pairs={{0,1},{1,0},{2,3},{3,2},{4,5},{5,4},{6,7},{7,6},{8,9},{9,8},{10,11... | collective-permute-start | bytes 1572872 | tf_op jit(solution)/shard_map/ppermute | solution.py:32
  27.7 1.7 %shard_map.91 = (s32[512,1]{1,0:T(8,128)S(1)}, s32[32,1]{1,0:T(8,128)S(1)}, s32[32,128]{1,0:T(8,128)}) custom-call(s32[2]{0:T(128)S(1)} %pad_add_fusion.2.refs_0_.numbers, s32[1,512]{1,0:T(1,128)S(1)} %bitcast.96), custom_call_target="tpu_custom_call" | custom-call | flops 16777216 | bytes 4096 | tf_op jit(solution)/shard_map/pallas_call | solution.py:173
  29.4 3.6 %all-to-all-done.1 = bf16[4,32,1024]{2,1,0:T(8,128)(2,1)S(1)} async-done(((bf16[4,32,1024]{2,1,0:T(8,128)(2,1)}), bf16[4,32,1024]{2,1,0:T(8,128)(2,1)S(1)}, u32[]{:S(2)}, u32[]{:S(2)}) %all-to-all-start.1) | async-done | bytes 262176 | tf_op jit(solution)/shard_map/all_to_all | solution.py:17
  33.0 4.3 %collective-permute-start.5 = (bf16[128,1024]{1,0:T(8,128)(2,1)S(1)}, bf16[128,1024]{1,0:T(8,128)(2,1)S(1)}, u32[]{:S(2)}, u32[]{:S(2)}) collective-permute-start(bf16[128,1024]{1,0:T(8,128)(2,1)S(1)} %bitcast.81), channel_id=1, source_target_pairs={{0,30},{1,31},{2,0},{3,1},{4,2},{5,3},{6,4},{7,5},{8,6},{9,7},{10,... | collective-permute-start | bytes 786440 | tf_op jit(solution)/shard_map/ppermute | solution.py:28
  37.3 0.7 fusion.5
  38.0 6.1 %collective-permute-start.4 = (bf16[128,1024]{1,0:T(8,128)(2,1)S(1)}, bf16[128,1024]{1,0:T(8,128)(2,1)S(1)}, u32[]{:S(2)}, u32[]{:S(2)}) collective-permute-start(bf16[128,1024]{1,0:T(8,128)(2,1)S(1)} %bitcast.82), channel_id=1, source_target_pairs={{0,2},{1,3},{2,4},{3,5},{4,6},{5,7},{6,8},{7,9},{8,10},{9,11},{10,... | collective-permute-start | bytes 786440 | tf_op jit(solution)/shard_map/ppermute | solution.py:28
  44.2 3.8 %collective-permute-start.6 = (bf16[64,1024]{1,0:T(8,128)(2,1)}, bf16[64,1024]{1,0:T(8,128)(2,1)S(1)}, u32[]{:S(2)}, u32[]{:S(2)}) collective-permute-start(bf16[64,1024]{1,0:T(8,128)(2,1)} %bitcast.14), channel_id=1, source_target_pairs={{0,4},{1,5},{2,6},{3,7},{4,8},{5,9},{6,10},{7,11},{8,12},{9,13},{1... | collective-permute-start | bytes 393224 | tf_op jit(solution)/shard_map/ppermute | solution.py:28
  47.9 3.6 %collective-permute-start.7 = (bf16[64,1024]{1,0:T(8,128)(2,1)}, bf16[64,1024]{1,0:T(8,128)(2,1)S(1)}, u32[]{:S(2)}, u32[]{:S(2)}) collective-permute-start(bf16[64,1024]{1,0:T(8,128)(2,1)} %bitcast.15), channel_id=1, source_target_pairs={{0,28},{1,29},{2,30},{3,31},{4,0},{5,1},{6,2},{7,3},{8,4},{9,5},{1... | collective-permute-start | bytes 393224 | tf_op jit(solution)/shard_map/ppermute | solution.py:28
  51.6 1.8 %broadcast_select_fusion.1 = (bf16[128,1024]{1,0:T(8,128)(2,1)}, bf16[128,1024]{1,0:T(8,128)(2,1)}) fusion(pred[]{:T(512)S(6)} %eq.17, bf16[132,1024]{1,0:T(8,128)(2,1)} %collective-permute-done.8, bf16[1024,4,32]{0,2,1:T(8,128)(2,1)S(1)} %copy-done.10), kind=kLoop, calls=%fused_computation.13 | loop fusion | flops 262144 | bytes 1048577 | tf_op jit(solution)/shard_map/jit(_where)/select_n | solution.py:483
  53.4 0.7 slice.48
  54.1 1.1 pad_maximum_fusion.1
  55.2 1.0 collective-permute-done.7.rows_4
  56.2 2.1 %shard_map.93 = (bf16[256,256]{1,0:T(8,128)(2,1)}, bf16[320,256]{1,0:T(8,128)(2,1)}, bf16[16,1024]{1,0:T(8,128)(2,1)S(1)}) custom-call(s32[512,1]{1,0:T(8,128)S(1)} %get-tuple-element.78.at, s32[32,1]{1,0:T(8,128)S(1)} %get-tuple-element.79.at_pair, bf16[128,1024]{1,0:T(8,128)(2,1)S(1)} %bitcast.83, bf16[128,1024]{1,0:T(8,128)(2,1)S(1)} %collective-permute-done.4.rows_1, ...), custom_call_target="tpu_custom_call" | custom-call | flops 402653184 | bytes 1572864 | tf_op jit(solution)/shard_map/pallas_call | solution.py:235
  58.3 1.8 %while.14 = (s32[]{:T(128)}, bf16[256,256]{1,0:T(8,128)(2,1)}, bf16[320,256]{1,0:T(8,128)(2,1)}, bf16[16,1024]{1,0:T(8,128)(2,1)S(1)}, s32[32,128]{1,0:T(8,128)}...) while((s32[]{:T(128)}, bf16[256,256]{1,0:T(8,128)(2,1)}, ...), condition=%wide.region_1.2_spmd, body=%wide.region_0.1_spmd.sunk | while | flops 453148672 | bytes 10162573 | solution.py:504
  58.3 1.2 slice.57
  60.1 3.1 %collective-permute-start.11 = (bf16[320,256]{1,0:T(8,128)(2,1)}, bf16[320,256]{1,0:T(8,128)(2,1)S(1)}, u32[]{:S(2)}, u32[]{:S(2)}) collective-permute-start(bf16[320,256]{1,0:T(8,128)(2,1)} %get-tuple-element.90), channel_id=1, source_target_pairs={{0,1},{1,0},{2,3},{3,2},{4,5},{5,4},{6,7},{7,6},{8,9},{9,8},{10,11... | collective-permute-start | bytes 491528 | tf_op jit(solution)/shard_map/ppermute | solution.py:32
  63.2 0.7 broadcast_select_fusion.3
  63.9 2.4 %collective-permute-done.11.refs_1_ = bf16[320,256]{1,0:T(8,128)(2,1)S(1)} collective-permute-done((bf16[320,256]{1,0:T(8,128)(2,1)}, bf16[320,256]{1,0:T(8,128)(2,1)S(1)}, u32[]{:S(2)}, u32[]{:S(2)}) %collective-permute-start.11) | collective-permute-done | bytes 163872 | tf_op jit(solution)/shard_map/ppermute | solution.py:32
  66.4 1.7 %shard_map.94 = (bf16[64,256]{1,0:T(8,128)(2,1)S(1)}, bf16[16,16,768]{2,1,0:T(8,128)(2,1)}, bf16[16,1024]{1,0:T(8,128)(2,1)S(1)}) custom-call(bf16[256,256]{1,0:T(8,128)(2,1)} %get-tuple-element.89.refs_0_, bf16[320,256]{1,0:T(8,128)(2,1)S(1)} %collective-permute-done.11.refs_1_, bf16[16,1024]{1,0:T(8,128)(2,1)S(1)} %get-tuple-element.91.refs_2_, ...), custom_call_target="tpu_custom_call" | custom-call | flops 65536 | bytes 524288 | tf_op jit(solution)/shard_map/pallas_call | solution.py:283
  68.1 6.4 %all-to-all-start.2 = ((bf16[16,16,768]{2,1,0:T(8,128)(2,1)}), bf16[16,16,768]{2,1,0:T(8,128)(2,1)S(1)}, u32[]{:S(2)}, u32[]{:S(2)}) async-start(bf16[16,16,768]{2,1,0:T(8,128)(2,1)} %get-tuple-element.93), calls=%async_computation.2 | async-start | bytes 786432 | tf_op jit(solution)/shard_map/all_to_all | solution.py:17
  75.2 0.0 copy-start.2
  75.2 0.1 convert_reduce_fusion
  75.3 0.6 copy-done.2
  75.9 0.1 convolution_bitcast_fusion.refs_6_
  76.0 0.1 convolution_bitcast_fusion.1.refs_5_
  76.1 36.2 %all_gather.3.refs_0_ = bf16[1024,256]{1,0:T(8,128)(2,1)S(1)} all-gather(bf16[64,256]{1,0:T(8,128)(2,1)S(1)} %get-tuple-element.92), channel_id=1, replica_groups={{0,2,4,6,8,10,12,14,16,18,20,22,24,26,28,30},{1,3,5,7,9,11,13,15,17,19,..., dimensions={0}, use_global_device_ids=true | all-gather | bytes 557056 | tf_op jit(solution)/shard_map/all_gather | solution.py:511
  112.3 3.2 %shard_map.95 = (bf16[256,1024]{1,0:T(8,128)(2,1)}, bf16[16,16,768]{2,1,0:T(8,128)(2,1)S(1)}) custom-call(bf16[1024,256]{1,0:T(8,128)(2,1)S(1)} %all_gather.3.refs_0_, bf16[256,1024]{1,0:T(8,128)(2,1)S(1)} %copy-done, bf16[256,1024]{1,0:T(8,128)(2,1)S(1)} %collective-permute-done.9.rest_0_.refs_2_, ...), custom_call_target="tpu_custom_call", output_to_operand_aliasing={{1}: (9, {})} | custom-call | flops 536870912 | bytes 3145728 | tf_op jit(solution)/shard_map/pallas_call | solution.py:335
  115.5 10.2 %all-to-all-start.3 = ((bf16[16,16,1024]{2,1,0:T(8,128)(2,1)}), bf16[16,16,1024]{2,1,0:T(8,128)(2,1)S(1)}, u32[]{:S(2)}, u32[]{:S(2)}) async-start(bf16[16,16,1024]{2,1,0:T(8,128)(2,1)} %bitcast.25), calls=%async_computation.3 | async-start | bytes 1048576 | tf_op jit(solution)/shard_map/all_to_all | solution.py:17
  125.7 0.1 copy_bitcast_fusion
  125.7 4.7 %collective-permute-start.14 = (bf16[1024,128]{1,0:T(8,128)(2,1)S(1)}, bf16[1024,128]{1,0:T(8,128)(2,1)S(1)}, u32[]{:S(2)}, u32[]{:S(2)}) collective-permute-start(bf16[1024,128]{1,0:T(8,128)(2,1)S(1)} %bitcast.76), channel_id=1, source_target_pairs={{0,384},{32,416},{64,448},{96,480},{128,0},{160,32},{192,64},{224,... | collective-permute-start | bytes 786440 | tf_op jit(solution)/shard_map/ppermute | solution.py:41
  130.4 2.2 %collective-permute-start.13 = (bf16[1024,128]{1,0:T(8,128)(2,1)S(1)}, bf16[1024,128]{1,0:T(8,128)(2,1)S(1)}, u32[]{:S(2)}, u32[]{:S(2)}) collective-permute-start(bf16[1024,128]{1,0:T(8,128)(2,1)S(1)} %bitcast.77), channel_id=1, source_target_pairs={{0,256},{32,288},{64,320},{96,352},{128,384},{160,416},{192,448},{... | collective-permute-start | bytes 786440 | tf_op jit(solution)/shard_map/ppermute | solution.py:41
  132.6 2.7 %collective-permute-start.12 = (bf16[1024,128]{1,0:T(8,128)(2,1)S(1)}, bf16[1024,128]{1,0:T(8,128)(2,1)S(1)}, u32[]{:S(2)}, u32[]{:S(2)}) collective-permute-start(bf16[1024,128]{1,0:T(8,128)(2,1)S(1)} %bitcast.78), channel_id=1, source_target_pairs={{0,128},{32,160},{64,192},{96,224},{128,256},{160,288},{192,320},{... | collective-permute-start | bytes 786440 | tf_op jit(solution)/shard_map/ppermute | solution.py:41
  135.3 3.8 %collective-permute-done.13.rest_2_ = bf16[1024,128]{1,0:T(8,128)(2,1)S(1)} collective-permute-done((bf16[1024,128]{1,0:T(8,128)(2,1)S(1)}, bf16[1024,128]{1,0:T(8,128)(2,1)S(1)}, u32[]{:S(2)}, u32[]{:S(2)}) %collective-permute-start.13) | collective-permute-done | bytes 262176 | tf_op jit(solution)/shard_map/ppermute | solution.py:41
  139.1 3.0 %collective-permute-done.12.rest_1_ = bf16[1024,128]{1,0:T(8,128)(2,1)S(1)} collective-permute-done((bf16[1024,128]{1,0:T(8,128)(2,1)S(1)}, bf16[1024,128]{1,0:T(8,128)(2,1)S(1)}, u32[]{:S(2)}, u32[]{:S(2)}) %collective-permute-start.12) | collective-permute-done | bytes 262176 | tf_op jit(solution)/shard_map/ppermute | solution.py:41
  142.1 0.1 pad_maximum_fusion
  142.3 0.0 copy-start.3
  142.3 12.6 %collective-permute-start.15 = (bf16[4,1024,128]{2,1,0:T(8,128)(2,1)S(1)}, bf16[4,1024,128]{2,1,0:T(8,128)(2,1)S(1)}, u32[]{:S(2)}, u32[]{:S(2)}) collective-permute-start(bf16[4,1024,128]{2,1,0:T(8,128)(2,1)S(1)} %pad_maximum_fusion), channel_id=1, source_target_pairs={{0,32},{32,0},{64,96},{96,64},{128,160},{160,128},{192,224},{224,1... | collective-permute-start | bytes 3145736 | tf_op jit(solution)/shard_map/ppermute | solution.py:36
  154.9 0.1 pad_add_fusion.1.numbers
  155.0 0.8 shard_map.96
  155.8 1.4 collective-permute-done.15
  157.2 0.1 slice_bitcast_fusion
  157.2 1.8 %shard_map.97 = bf16[16,1024]{1,0:T(8,128)(2,1)} custom-call(s32[3]{0:T(128)S(1)} %pad_add_fusion.1.numbers, bf16[16,16,1024]{2,1,0:T(8,128)(2,1)S(1)} %all-to-all-done.3.parts, f32[16,1024]{1,0:T(8,128)S(1)} %get-tuple-element.96.self_term, f32[16,1024]{1,0:T(8,128)S(1)} %get-tuple-element.97.gate, bf16[16,1024]{1,0:T(8,128)(2,1)S(1)} %get-tuple-element.98.embedded, ...), custom_call_target="tpu_custom_call" | custom-call | flops 33554432 | bytes 4194304 | tf_op jit(solution)/shard_map/pallas_call | solution.py:430
  (31 shorter events, 0.2 us)
Async XLA Ops:
  0.1 0.7 copy-start.11
  0.8 21.5 %copy-start.9 = (bf16[1024,4,32]{0,2,1:T(8,128)(2,1)S(1)}, bf16[1024,4,32]{0,2,1:T(8,128)(2,1)}, u32[]{:S(2)}) copy-start(bf16[1024,4,32]{0,2,1:T(8,128)(2,1)} %param.16) | copy-start | bytes 786436
  3.4 15.8 %copy-start = (bf16[256,1024]{1,0:T(8,128)(2,1)S(1)}, bf16[256,1024]{1,0:T(8,128)(2,1)}, u32[]{:S(2)}) copy-start(bf16[256,1024]{1,0:T(8,128)(2,1)} %refs_1_.1) | copy-start | bytes 1572868
  3.4 21.1 %copy-start.1 = (bf16[256,1024]{1,0:T(8,128)(2,1)S(1)}, bf16[256,1024]{1,0:T(8,128)(2,1)}, u32[]{:S(2)}) copy-start(bf16[256,1024]{1,0:T(8,128)(2,1)} %refs_3_.1) | copy-start | bytes 1572868
  3.4 29.6 %all-to-all-start.1 = ((bf16[4,32,1024]{2,1,0:T(8,128)(2,1)}), bf16[4,32,1024]{2,1,0:T(8,128)(2,1)S(1)}, u32[]{:S(2)}, u32[]{:S(2)}) async-start(bf16[4,32,1024]{2,1,0:T(8,128)(2,1)} %shard_map.92), calls=%async_computation.1 | async-start | bytes 524288 | tf_op jit(solution)/shard_map/all_to_all | solution.py:17
  19.2 28.8 %collective-permute-start.9 = (bf16[256,1024]{1,0:T(8,128)(2,1)S(1)}, bf16[256,1024]{1,0:T(8,128)(2,1)S(1)}, u32[]{:S(2)}, u32[]{:S(2)}) collective-permute-start(bf16[256,1024]{1,0:T(8,128)(2,1)S(1)} %copy-done), channel_id=1, source_target_pairs={{0,1},{1,0},{2,3},{3,2},{4,5},{5,4},{6,7},{7,6},{8,9},{9,8},{10,11... | collective-permute-start | bytes 1572872 | tf_op jit(solution)/shard_map/ppermute | solution.py:32
  22.4 21.8 %collective-permute-start.8 = (bf16[132,1024]{1,0:T(8,128)(2,1)S(1)}, bf16[132,1024]{1,0:T(8,128)(2,1)}, u32[]{:S(2)}, u32[]{:S(2)}) collective-permute-start(bf16[132,1024]{1,0:T(8,128)(2,1)S(1)} %pad_maximum_fusion.2), channel_id=1, source_target_pairs={{0,1},{1,0},{2,3},{3,2},{4,5},{5,4},{6,7},{7,6},{8,9},{9,8},{10,11... | collective-permute-start | bytes 811016 | tf_op jit(solution)/shard_map/ppermute | solution.py:32
  24.5 30.7 %collective-permute-start.10 = (bf16[256,1024]{1,0:T(8,128)(2,1)S(1)}, bf16[256,1024]{1,0:T(8,128)(2,1)S(1)}, u32[]{:S(2)}, u32[]{:S(2)}) collective-permute-start(bf16[256,1024]{1,0:T(8,128)(2,1)S(1)} %copy-done.1), channel_id=1, source_target_pairs={{0,1},{1,0},{2,3},{3,2},{4,5},{5,4},{6,7},{7,6},{8,9},{9,8},{10,11... | collective-permute-start | bytes 1572872 | tf_op jit(solution)/shard_map/ppermute | solution.py:32
  33.0 18.6 %copy-start.10 = (bf16[1024,4,32]{0,2,1:T(8,128)(2,1)S(1)}, bf16[1024,4,32]{0,2,1:T(8,128)(2,1)}, u32[]{:S(2)}) copy-start(bf16[1024,4,32]{0,2,1:T(8,128)(2,1)} %param.16) | copy-start | bytes 786436
  33.0 23.3 %collective-permute-start.5 = (bf16[128,1024]{1,0:T(8,128)(2,1)S(1)}, bf16[128,1024]{1,0:T(8,128)(2,1)S(1)}, u32[]{:S(2)}, u32[]{:S(2)}) collective-permute-start(bf16[128,1024]{1,0:T(8,128)(2,1)S(1)} %bitcast.81), channel_id=1, source_target_pairs={{0,30},{1,31},{2,0},{3,1},{4,2},{5,3},{6,4},{7,5},{8,6},{9,7},{10,... | collective-permute-start | bytes 786440 | tf_op jit(solution)/shard_map/ppermute | solution.py:28
  38.0 18.2 %collective-permute-start.4 = (bf16[128,1024]{1,0:T(8,128)(2,1)S(1)}, bf16[128,1024]{1,0:T(8,128)(2,1)S(1)}, u32[]{:S(2)}, u32[]{:S(2)}) collective-permute-start(bf16[128,1024]{1,0:T(8,128)(2,1)S(1)} %bitcast.82), channel_id=1, source_target_pairs={{0,2},{1,3},{2,4},{3,5},{4,6},{5,7},{6,8},{7,9},{8,10},{9,11},{10,... | collective-permute-start | bytes 786440 | tf_op jit(solution)/shard_map/ppermute | solution.py:28
  44.2 11.1 %collective-permute-start.6 = (bf16[64,1024]{1,0:T(8,128)(2,1)}, bf16[64,1024]{1,0:T(8,128)(2,1)S(1)}, u32[]{:S(2)}, u32[]{:S(2)}) collective-permute-start(bf16[64,1024]{1,0:T(8,128)(2,1)} %bitcast.14), channel_id=1, source_target_pairs={{0,4},{1,5},{2,6},{3,7},{4,8},{5,9},{6,10},{7,11},{8,12},{9,13},{1... | collective-permute-start | bytes 393224 | tf_op jit(solution)/shard_map/ppermute | solution.py:28
  47.9 8.3 %collective-permute-start.7 = (bf16[64,1024]{1,0:T(8,128)(2,1)}, bf16[64,1024]{1,0:T(8,128)(2,1)S(1)}, u32[]{:S(2)}, u32[]{:S(2)}) collective-permute-start(bf16[64,1024]{1,0:T(8,128)(2,1)} %bitcast.15), channel_id=1, source_target_pairs={{0,28},{1,29},{2,30},{3,31},{4,0},{5,1},{6,2},{7,3},{8,4},{9,5},{1... | collective-permute-start | bytes 393224 | tf_op jit(solution)/shard_map/ppermute | solution.py:28
  55.2 3.1 %copy-start.4 = (bf16[4,2,32,1024]{3,2,1,0:T(8,128)(2,1)}, bf16[4,2,32,1024]{3,2,1,0:T(8,128)(2,1)S(1)}, u32[]{:S(2)}) copy-start(bf16[4,2,32,1024]{3,2,1,0:T(8,128)(2,1)S(1)} %pad_maximum_fusion.1) | copy-start | bytes 1572868
  60.1 6.3 %collective-permute-start.11 = (bf16[320,256]{1,0:T(8,128)(2,1)}, bf16[320,256]{1,0:T(8,128)(2,1)S(1)}, u32[]{:S(2)}, u32[]{:S(2)}) collective-permute-start(bf16[320,256]{1,0:T(8,128)(2,1)} %get-tuple-element.90), channel_id=1, source_target_pairs={{0,1},{1,0},{2,3},{3,2},{4,5},{5,4},{6,7},{7,6},{8,9},{9,8},{10,11... | collective-permute-start | bytes 491528 | tf_op jit(solution)/shard_map/ppermute | solution.py:32
  68.1 44.2 %all-to-all-start.2 = ((bf16[16,16,768]{2,1,0:T(8,128)(2,1)}), bf16[16,16,768]{2,1,0:T(8,128)(2,1)S(1)}, u32[]{:S(2)}, u32[]{:S(2)}) async-start(bf16[16,16,768]{2,1,0:T(8,128)(2,1)} %get-tuple-element.93), calls=%async_computation.2 | async-start | bytes 786432 | tf_op jit(solution)/shard_map/all_to_all | solution.py:17
  75.2 0.7 copy-start.2
  115.5 41.8 %all-to-all-start.3 = ((bf16[16,16,1024]{2,1,0:T(8,128)(2,1)}), bf16[16,16,1024]{2,1,0:T(8,128)(2,1)S(1)}, u32[]{:S(2)}, u32[]{:S(2)}) async-start(bf16[16,16,1024]{2,1,0:T(8,128)(2,1)} %bitcast.25), calls=%async_computation.3 | async-start | bytes 1048576 | tf_op jit(solution)/shard_map/all_to_all | solution.py:17
  125.7 9.6 %collective-permute-start.14 = (bf16[1024,128]{1,0:T(8,128)(2,1)S(1)}, bf16[1024,128]{1,0:T(8,128)(2,1)S(1)}, u32[]{:S(2)}, u32[]{:S(2)}) collective-permute-start(bf16[1024,128]{1,0:T(8,128)(2,1)S(1)} %bitcast.76), channel_id=1, source_target_pairs={{0,384},{32,416},{64,448},{96,480},{128,0},{160,32},{192,64},{224,... | collective-permute-start | bytes 786440 | tf_op jit(solution)/shard_map/ppermute | solution.py:41
  130.4 8.7 %collective-permute-start.13 = (bf16[1024,128]{1,0:T(8,128)(2,1)S(1)}, bf16[1024,128]{1,0:T(8,128)(2,1)S(1)}, u32[]{:S(2)}, u32[]{:S(2)}) collective-permute-start(bf16[1024,128]{1,0:T(8,128)(2,1)S(1)} %bitcast.77), channel_id=1, source_target_pairs={{0,256},{32,288},{64,320},{96,352},{128,384},{160,416},{192,448},{... | collective-permute-start | bytes 786440 | tf_op jit(solution)/shard_map/ppermute | solution.py:41
  132.6 9.5 %collective-permute-start.12 = (bf16[1024,128]{1,0:T(8,128)(2,1)S(1)}, bf16[1024,128]{1,0:T(8,128)(2,1)S(1)}, u32[]{:S(2)}, u32[]{:S(2)}) collective-permute-start(bf16[1024,128]{1,0:T(8,128)(2,1)S(1)} %bitcast.78), channel_id=1, source_target_pairs={{0,128},{32,160},{64,192},{96,224},{128,256},{160,288},{192,320},{... | collective-permute-start | bytes 786440 | tf_op jit(solution)/shard_map/ppermute | solution.py:41
  142.3 12.7 %copy-start.3 = (f32[1024]{0:T(1024)S(1)}, f32[1024]{0:T(1024)}, u32[]{:S(2)}) copy-start(f32[1024]{0:T(1024)} %param.18) | copy-start | bytes 12292
  142.3 14.9 %collective-permute-start.15 = (bf16[4,1024,128]{2,1,0:T(8,128)(2,1)S(1)}, bf16[4,1024,128]{2,1,0:T(8,128)(2,1)S(1)}, u32[]{:S(2)}, u32[]{:S(2)}) collective-permute-start(bf16[4,1024,128]{2,1,0:T(8,128)(2,1)S(1)} %pad_maximum_fusion), channel_id=1, source_target_pairs={{0,32},{32,0},{64,96},{96,64},{128,160},{160,128},{192,224},{224,1... | collective-permute-start | bytes 3145736 | tf_op jit(solution)/shard_map/ppermute | solution.py:36

commit v6 on v5

--- a/solution.py
+++ b/solution.py
@@ -23,6 +23,11 @@
     return groups_of([list(range(lax.axis_size("seq") // 2))])
 
 
+def class_groups():
+    column = lax.axis_size("seq") // 2
+    return groups_of([list(range(at, column, 2)) for at in range(2)])
+
+
 def from_place(block, shift):
     count = lax.axis_size("seq")
     return lax.ppermute(block, "seq", [(i, (i + 2 * shift) % count) for i in range(count)])
@@ -30,6 +35,10 @@
 
 def swap_pair(block):
     return lax.ppermute(block, "seq", [(i, i ^ 1) for i in range(lax.axis_size("seq"))])
+
+
+def swap_place(block):
+    return lax.ppermute(block, "seq", [(i, i ^ 2) for i in range(lax.axis_size("seq"))])
 
 
 def swap_core(block):
@@ -158,7 +167,9 @@
     half = at // (count // 2)
     inner = at - half * (count // 2)
     owner_side = jnp.where(half == 0, side, 1 - side)
-    original = (inner // own) * (2 * own) + owner_side * own + lax.rem(inner, own)
+    kind = inner // (count // 4)
+    owner = 2 * ((inner - kind * (count // 4)) // own) + kind
+    original = owner * (2 * own) + owner_side * own + lax.rem(inner, own)
     spread(original == lax.broadcasted_iota(jnp.int32, (count, count), 1), slots)
     at = lax.broadcasted_iota(jnp.int32, (2 * own, count), 0)
     half = at // own
@@ -186,20 +197,28 @@
     )(numbers, ids.reshape(1, -1))
 
 
-def project_kernel(at, at_pair, rows_0, rows_1, rows_2, rows_3, rows_4, weights, *rest):
+def project_kernel(numbers, at, at_pair, rows_0, rows_1, rows_2, rows_3, rows_4, mine, other, *rest):
     proj_mine, proj_other, own_rows, slots = rest[-4:]
     cand_side, columns = proj_mine.shape
     own, width = own_rows.shape
     first = 0
     for rows in (rows_0, rows_1, rows_2, rows_3, rows_4):
         count = rows.shape[0]
-        slots[first : first + count, :] = silu(
-            lax.dot_general(
-                rows[...],
-                weights[...],
-                (((1,), (1,)), ((), ())),
-                preferred_element_type=jnp.float32,
+        product_mine, product_other = (
+            silu(
+                lax.dot_general(
+                    rows[...], part, (((1,), (1,)), ((), ())), preferred_element_type=jnp.float32
+                )
             )
+            for part in (mine[...], other[: mine.shape[0], :])
+        )
+        here = jnp.broadcast_to(numbers[0], product_mine.shape) % 2 == 0
+        lanes = mine.shape[0]
+        slots[first : first + count, :lanes] = jnp.where(
+            here, product_mine, product_other
+        ).astype(jnp.bfloat16)
+        slots[first : first + count, lanes:] = jnp.where(
+            here, product_other, product_mine
         ).astype(jnp.bfloat16)
         first += count
     place = lax.broadcasted_iota(jnp.int32, (cand_side, first), 1)
@@ -226,15 +245,17 @@
         ].astype(jnp.bfloat16)
 
 
-def project(at, at_pair, rows, weights, ready):
-    columns, width = weights.shape
+def project(numbers, at, at_pair, rows, mine, other, ready):
+    columns, width = 2 * mine.shape[0], mine.shape[1]
     cand_side = at.shape[0] // 2
     own = at_pair.shape[0] // 2
     slot_count = sum(piece.shape[0] for piece in rows)
     whole = pl.BlockSpec(memory_space=pltpu.VMEM)
     return pl.pallas_call(
         project_kernel,
-        in_specs=[whole] * (3 + len(rows)) + [pl.BlockSpec(memory_space=pl.ANY)] * len(ready),
+        in_specs=[pl.BlockSpec(memory_space=pltpu.SMEM)]
+        + [whole] * (4 + len(rows))
+        + [pl.BlockSpec(memory_space=pl.ANY)] * len(ready),
         out_specs=[whole] * 3,
         out_shape=[
             jax.ShapeDtypeStruct((cand_side, columns), jnp.bfloat16),
@@ -248,11 +269,11 @@
             bytes_accessed=2 * (slot_count + columns) * width,
             transcendentals=slot_count * columns,
         ),
-    )(at, at_pair, *rows, weights, *ready)
-
-
-def pack_kernel(feature_here, mine, arrived, own_rows, w_slice, *rest):
-    queries, packed, embedded = rest[-3:]
+    )(numbers, at, at_pair, *rows, mine, other, *ready)
+
+
+def pack_kernel(feature_here, mine, arrived, own_rows, *rest):
+    packed, embedded = rest[-2:]
     cand_side, columns = mine.shape
     own = own_rows.shape[0]
     proj = mine[...].astype(jnp.float32) + arrived[:cand_side, :].astype(jnp.float32)
@@ -263,29 +284,38 @@
             own_rows[:, lanes].astype(jnp.float32) + other.astype(jnp.float32)
         ).astype(jnp.bfloat16)
     block = 4 * feature_here
-    queries[...] = proj[:, block : block + 2 * feature_here].T.astype(jnp.bfloat16)
-    column, own, _ = packed.shape
-    columns = 2 * block
-    packed[:, :, :columns] = proj.astype(jnp.bfloat16).reshape(column, own, columns)
-    lanes = w_slice.shape[1]
-    for part in range(w_slice.shape[0] // own):
-        packed[:, :, columns + part * lanes : columns + (part + 1) * lanes] = jnp.broadcast_to(
-            w_slice[part * own : (part + 1) * own, :][None], (column, own, lanes)
-        )
-
-
-def pack(mine, arrived, own_rows, w_slice, feature_here):
+    queries = jnp.concatenate(
+        [
+            proj[:, side * block + 2 * feature_here : side * block + 3 * feature_here]
+            for side in range(2)
+        ],
+        axis=1,
+    ).T.astype(jnp.bfloat16)
+    proj = proj.astype(jnp.bfloat16)
+    column = packed.shape[0]
+    cand_class = cand_side // 2
+    for place in range(column):
+        kind = place % 2
+        first = kind * cand_class + place // 2 * own
+        packed[place, :, :columns] = proj[first : first + own, :]
+        for part in range(queries.shape[0] // own):
+            lanes = slice(columns + part * cand_class, columns + (part + 1) * cand_class)
+            packed[place, :, lanes] = queries[
+                part * own : (part + 1) * own, kind * cand_class : (kind + 1) * cand_class
+            ]
+
+
+def pack(mine, arrived, own_rows, ready, feature_here):
     cand_side, columns = mine.shape
     own = own_rows.shape[0]
     column = cand_side // own
-    packed_width = columns + w_slice.shape[0] * w_slice.shape[1] // own
+    packed_width = columns + 2 * feature_here * (cand_side // 2) // own
     whole = pl.BlockSpec(memory_space=pltpu.VMEM)
     return pl.pallas_call(
         lambda *refs: pack_kernel(feature_here, *refs),
-        in_specs=[whole] * 4,
-        out_specs=[whole] * 3,
+        in_specs=[whole] * 3 + [pl.BlockSpec(memory_space=pl.ANY)] * len(ready),
+        out_specs=[whole] * 2,
         out_shape=[
-            jax.ShapeDtypeStruct((2 * feature_here, cand_side), jnp.bfloat16),
             jax.ShapeDtypeStruct((column, own, packed_width), jnp.bfloat16),
             jax.ShapeDtypeStruct(own_rows.shape, jnp.bfloat16),
         ],
@@ -293,82 +323,125 @@
         cost_estimate=pl.CostEstimate(
             flops=cand_side * columns, bytes_accessed=8 * cand_side * columns, transcendentals=0
         ),
-    )(mine, arrived, own_rows, w_slice)
-
-
-def attend_kernel(scale, heads, *refs):
-    queries, keys_a, keys_b, values_a, values_b, bias_a, bias_b, live_a, live_b = refs[:9]
-    summed = refs[-2]
+    )(mine, arrived, own_rows, *ready)
+
+
+def spread_kernel(numbers, w_slice, other, out):
+    rows, lanes = w_slice.shape
+    half = rows // 2
+    first = other.shape[0] - half
+    theirs = jnp.concatenate(
+        [other[first:, :lanes], other[first:, lanes : 2 * lanes]], axis=0
+    )
+    here = jnp.broadcast_to(numbers[0], (rows, lanes)) % 2 == 0
+    ours = w_slice[...].astype(jnp.float32)
+    theirs = theirs.astype(jnp.float32)
+    top = jnp.where(here, ours, theirs).astype(jnp.bfloat16)
+    bottom = jnp.where(here, theirs, ours).astype(jnp.bfloat16)
+    for place in range(out.shape[0]):
+        out[place, :rows, :] = top
+        out[place, rows:, :] = bottom
+
+
+def spread(numbers, w_slice, other, column):
+    rows, lanes = w_slice.shape
+    whole = pl.BlockSpec(memory_space=pltpu.VMEM)
+    return pl.pallas_call(
+        spread_kernel,
+        in_specs=[pl.BlockSpec(memory_space=pltpu.SMEM), whole, whole],
+        out_specs=whole,
+        out_shape=jax.ShapeDtypeStruct((column, 2 * rows, lanes), jnp.bfloat16),
+        compiler_params=pltpu.CompilerParams(vmem_limit_bytes=32 * 1024 * 1024),
+        cost_estimate=pl.CostEstimate(
+            flops=rows * lanes, bytes_accessed=4 * column * rows * lanes, transcendentals=0
+        ),
+    )(numbers, w_slice, other)
+
+
+def attend_kernel(scale, heads, received, *refs):
+    keys_values, bias, live, summed = refs[:8], refs[8], refs[9], refs[-1]
     first_head = pl.program_id(0) * heads
-    head_size = keys_a.shape[1] // heads
+    cand, lanes = summed.shape
+    head_size = lanes // heads
+    events = keys_values[0].shape[0]
+    own = received.shape[1]
+    places = received.shape[0] // heads
+    parts = head_size // (places * own)
+    skip = received.shape[2] - parts * cand
     for head in range(heads):
+        head_queries = jnp.concatenate(
+            [
+                received[head * places + place, :, skip + part * cand : skip + (part + 1) * cand]
+                for place in range(places)
+                for part in range(parts)
+            ],
+            axis=0,
+        ).T
         lanes = slice(head * head_size, (head + 1) * head_size)
-        head_queries = queries[lanes, :].T
+        head_bias = 0.5 * bias[pl.ds(first_head + head, 1), :]
         total = None
-        for keys, values, bias, live in (
-            (keys_a, values_a, bias_a, live_a),
-            (keys_b, values_b, bias_b, live_b),
-        ):
+        for source in range(4):
+            keys, values = keys_values[2 * source], keys_values[2 * source + 1]
+            here = slice(source * events, (source + 1) * events)
             scores = lax.dot_general(
                 head_queries,
                 keys[:, lanes],
                 (((1,), (1,)), ((), ())),
                 preferred_element_type=jnp.float32,
             )
-            half_bias = 0.5 * bias[pl.ds(first_head + head, 1), :]
-            weights = half_silu(scores * (0.5 * scale) + half_bias)
-            weights = jnp.where(live[...] > 0.0, weights, 0.0).astype(jnp.bfloat16)
+            weights = half_silu(scores * (0.5 * scale) + head_bias[:, here])
+            weights = jnp.where(live[:, here] > 0.0, weights, 0.0).astype(jnp.bfloat16)
             part = jnp.dot(weights, values[:, lanes], preferred_element_type=jnp.float32)
             total = part if total is None else total + part
         summed[:, lanes] = total.astype(summed.dtype)
 
 
-def attend(queries, keys, values, keys_other, values_other, bias, live, head_count, through):
-    width, cand = queries.shape
-    events = keys.shape[0]
+def attend(received, keys, values, others, bias, live, cand, ready):
+    events, width = keys.shape
+    head_count = bias.shape[0]
     head_size = width // head_count
     heads = 4
     lanes = heads * head_size
-    bias_spec = pl.BlockSpec((head_count, events), lambda h: (0, 0))
-    live_spec = pl.BlockSpec((1, events), lambda h: (0, 0))
-    held = pl.BlockSpec(memory_space=pl.ANY)
+    column, own, packed_width = received.shape
+    steps = head_count // heads
+    first = pl.BlockSpec((events, lanes), lambda h: (0, h))
+    second = pl.BlockSpec((events, lanes), lambda h: (1, h))
+    key_values = [keys, values] + [array for other in others for array in (other, other)]
     return pl.pallas_call(
         lambda *refs: attend_kernel(head_size ** (-0.5), heads, *refs),
-        grid=(head_count // heads,),
+        grid=(steps,),
         in_specs=[
-            pl.BlockSpec((lanes, cand), lambda h: (h, 0)),
-            pl.BlockSpec((events, lanes), lambda h: (0, h)),
-            pl.BlockSpec((events, lanes), lambda h: (0, h)),
-            pl.BlockSpec((events, lanes), lambda h: (0, h)),
-            pl.BlockSpec((events, lanes), lambda h: (0, h)),
+            pl.BlockSpec((column // steps, own, packed_width), lambda h: (h, 0, 0)),
+            first,
+            first,
         ]
-        + [bias_spec] * 2
-        + [live_spec] * 2
-        + [held],
-        out_specs=[pl.BlockSpec((cand, lanes), lambda h: (0, h)), held],
-        out_shape=[
-            jax.ShapeDtypeStruct((cand, width), jnp.bfloat16),
-            jax.ShapeDtypeStruct(through.shape, through.dtype),
-        ],
-        input_output_aliases={9: 1},
-        compiler_params=pltpu.CompilerParams(vmem_limit_bytes=32 * 1024 * 1024),
-        cost_estimate=pl.CostEstimate(
-            flops=8 * cand * events * width,
-            bytes_accessed=8 * events * width + 4 * cand * width,
-            transcendentals=2 * cand * events * head_count,
-        ),
-    )(queries, keys, keys_other, values, values_other, *bias, *live, through)
-
-
-def own_kernel(scale, rab, received, gain, self_term, gate):
+        + [second, first] * len(others)
+        + [
+            pl.BlockSpec(bias.shape, lambda h: (0, 0)),
+            pl.BlockSpec(live.shape, lambda h: (0, 0)),
+        ]
+        + [pl.BlockSpec(memory_space=pl.ANY)] * len(ready),
+        out_specs=pl.BlockSpec((cand, lanes), lambda h: (0, h)),
+        out_shape=jax.ShapeDtypeStruct((cand, width), jnp.bfloat16),
+        compiler_params=pltpu.CompilerParams(vmem_limit_bytes=32 * 1024 * 1024),
+        cost_estimate=pl.CostEstimate(
+            flops=16 * cand * events * width,
+            bytes_accessed=16 * events * width + 4 * cand * width,
+            transcendentals=4 * cand * events * head_count,
+        ),
+    )(received, *key_values, bias, live, *ready)
+
+
+def own_kernel(scale, rab, received, gain, after, self_term, gate):
     own, width = self_term.shape
     column = received.shape[0]
-    lanes = width // column
+    lanes = width // column // 2
     gate_u, own_v, own_queries, own_k = (
         jnp.concatenate(
             [
-                received[place, :, part * lanes : (part + 1) * lanes].astype(jnp.float32)
+                received[place, :, first : first + lanes].astype(jnp.float32)
                 for place in range(column)
+                for first in (part * lanes, (part + 4) * lanes)
             ],
             axis=1,
         )
@@ -384,20 +457,21 @@
         self_term[:, head_lanes] = silu(score) * own_v[:, head_lanes]
 
 
-def own_parts(received, rab, gain, own):
+def own_parts(received, rab, gain, own, after):
     width = gain.shape[0]
     whole = pl.BlockSpec(memory_space=pltpu.VMEM)
     scale = (width // rab.shape[0]) ** (-0.5)
     return pl.pallas_call(
         lambda *refs: own_kernel(scale, *refs),
-        in_specs=[pl.BlockSpec(memory_space=pltpu.SMEM), whole, whole],
+        in_specs=[pl.BlockSpec(memory_space=pltpu.SMEM), whole, whole]
+        + [pl.BlockSpec(memory_space=pl.ANY)],
         out_specs=[whole] * 2,
         out_shape=[jax.ShapeDtypeStruct((own, width), jnp.float32)] * 2,
         compiler_params=pltpu.CompilerParams(vmem_limit_bytes=32 * 1024 * 1024),
         cost_estimate=pl.CostEstimate(
             flops=8 * own * width, bytes_accessed=32 * own * width, transcendentals=own
         ),
-    )(rab, received, gain.reshape(1, -1))
+    )(rab, received, gain.reshape(1, -1), after)
 
 
 def finish_kernel(numbers, parts, self_term, gate, embedded, *rest):
@@ -459,89 +533,62 @@
     out_lanes = width // (2 * row_count)
     length = lengths[0]
 
-    w_slice = lax.dynamic_slice_in_dim(w_out, (core * row_count + row) * out_lanes, out_lanes, 1)
-    slice_rows = w_slice.shape[0]
-
     far_places = column // near_places
-    w_mine = w_proj.transpose(1, 2, 0).reshape(4 * feature_here, width)
 
     def numbers_at(first_rank):
         return jnp.stack([index_here, first_rank])
 
-    picked = pick(numbers_at(jnp.int32(0)), item_ids, item_table, far_places)
-    picked, w_sent, *sent = lax.optimization_barrier(
-        (picked, w_mine, history_values, history_keys, w_slice)
-    )
-    values_sent, keys_sent, slice_sent = sent
+    numbers = numbers_at(jnp.int32(0))
+    picked = pick(numbers, item_ids, item_table, far_places)
+    picked, w_proj, values, keys, w_out = lax.optimization_barrier(
+        (picked, w_proj, history_values, history_keys, w_out)
+    )
     rows = gather_slots(picked)
-    w_other = swap_pair(jnp.concatenate([w_sent, slice_sent.reshape(-1, width)]))
-    slice_other = w_other[4 * feature_here :].reshape(w_slice.shape)
-    w_other = w_other[: 4 * feature_here]
-    keys_other, values_other = swap_pair(keys_sent), swap_pair(values_sent)
-    w_pair = jnp.stack(
-        [
-            jnp.where(side == 0, w_mine, w_other).reshape(4, feature_here, width),
-            jnp.where(side == 0, w_other, w_mine).reshape(4, feature_here, width),
-        ],
-        axis=1,
-    ).reshape(8 * feature_here, width)
-    slices = jnp.concatenate(
-        [jnp.where(side == 0, w_slice, slice_other), jnp.where(side == 0, slice_other, w_slice)]
-    )
-    slots, pair_slots, most = locate(
-        numbers_at(jnp.int32(0)), item_ids, table_rows, device_count
-    )
-    found = tuple(project(slots, pair_slots, rows, w_pair, (keys_other, values_other)))
+
+    w_mine = w_proj.transpose(1, 2, 0).reshape(4 * feature_here, width)
+    w_slice = lax.dynamic_slice_in_dim(w_out, (core * row_count + row) * out_lanes, out_lanes, 1)
+    w_half = w_slice.shape[0] // 2
+    w_sent = jnp.concatenate([w_slice[:w_half], w_slice[w_half:]], axis=1)
+    w_sent = jnp.concatenate([w_mine, jnp.tile(w_sent, (1, width // (2 * out_lanes)))])
+    w_other = swap_pair(w_sent)
+    w_here = exchange(spread(numbers, w_slice, w_other, column), column_groups())
+    w_here = w_here.reshape(width, out_lanes)
+
+    events_sent = jnp.concatenate([values, keys])
+    pair_events, place_events = swap_pair(events_sent), swap_place(events_sent)
+    others = pair_events, place_events, swap_pair(place_events)
+
+    slots, pair_slots, most = locate(numbers, item_ids, table_rows, device_count)
+    found = tuple(project(numbers, slots, pair_slots, rows, w_mine, w_other, (w_here, place_events, pair_events)))
 
     def another(state):
-        first_rank, found = state
+        first_rank, limit, found = state
         numbers = numbers_at(first_rank)
         rows = gather_slots(pick(numbers, item_ids, item_table, far_places))
         slots, pair_slots, _ = locate(numbers, item_ids, table_rows, device_count)
-        more = project(slots, pair_slots, rows, w_pair, ())
-        return first_rank + slot_rows, tuple(a + b for a, b in zip(found, more))
-
-    _, (proj_mine, proj_other, own_rows) = lax.while_loop(
-        lambda state: state[0] < most[0, 0], another, (jnp.int32(slot_rows), found)
-    )
-    side_queries, packed, embedded = pack(
-        proj_mine, swap_pair(proj_other), own_rows, slices, feature_here
+        more = project(numbers, slots, pair_slots, rows, w_mine, w_other, ())
+        return first_rank + slot_rows, limit, tuple(a + b for a, b in zip(found, more))
+
+    _, _, (proj_mine, proj_other, own_rows) = lax.while_loop(
+        lambda state: state[0] < state[1], another, (jnp.int32(slot_rows), most[0, 0], found)
+    )
+    packed, embedded = pack(
+        proj_mine, swap_pair(proj_other), own_rows, (), feature_here
     )
     received = exchange(packed, column_groups())
-    all_queries = lax.all_gather(
-        side_queries, "seq", axis=0, tiled=True, axis_index_groups=column_groups()
-    )
-
-    def bias_of(index):
-        positions = index * events_here + jnp.arange(events_here, dtype=jnp.int32)
-        return (
-            bucket_bias(rab, length - positions),
-            (positions < length).astype(jnp.float32)[None, :],
-        )
-
-    bias, live = zip(bias_of(index_here), bias_of(index_here + 1 - 2 * side))
-    summed, received = attend(
-        all_queries,
-        history_keys,
-        history_values,
-        keys_other,
-        values_other,
-        bias,
-        live,
-        head_count,
-        received,
-    )
-    parts = exchange(summed.reshape(column, cand_here, width), column_groups())
-
-    self_term, gate = own_parts(received, rab, norm_gain, cand_here)
-
-    w_here = (
-        received[:, :, 8 * feature_here :]
-        .reshape(column, cand_here, 2 * slice_rows // cand_here, out_lanes)
-        .transpose(0, 2, 1, 3)
-        .reshape(width, out_lanes)
-    )
+
+    sources = index_here ^ jnp.arange(4, dtype=jnp.int32)
+    positions = sources[:, None] * events_here + jnp.arange(events_here, dtype=jnp.int32)[None, :]
+    positions = positions.reshape(4 * events_here)
+    bias = bucket_bias(rab, length - positions)
+    live = (positions < length).astype(jnp.float32)[None, :]
+
     weights = [w_here] + [from_row(w_here, shift) for shift in range(1, row_count)]
+    summed = attend(
+        received, history_keys, history_values, others, bias, live, cand_side // 2, weights[1:]
+    )
+    parts = exchange(summed.reshape(column // 2, cand_here, width), class_groups())
+    self_term, gate = own_parts(received, rab, norm_gain, cand_here, summed)
     weights = [*weights, *swap_core(jnp.stack(weights))]
     numbers = jnp.stack([length, row, core])
     return finish(numbers, parts, self_term, gate, embedded, weights)

time: 160 us -> 178 us (1.11)
  blocking collectives: 36.2 us -> 0 us
  waiting for transfers between devices: 15.3 us -> 47.8 us
  local copies, waits for them, and re-layouts: 4.1 us -> 14.8 us
  starting transfers between devices: 83.8 us -> 93.3 us
  Pallas kernels: 13.8 us -> 17.3 us
  other arithmetic: 4.04 us -> 1.57 us
    all_gather x1 -> x0, blocking collectives: 36.2 us -> none  [local(): lax.all_gather(side_queries, 'seq', axis=0, tiled=True, axis_index_groups...]
    ppermute x4, waiting for transfers between devices: 1.01 us -> 17.7 us  [from_place(): lax.ppermute(block, 'seq', [(i, (i + 2 * shift) % count) for i in range(c...]
    all_to_all x3 -> x4, waiting for transfers between devices: 3.63 us -> 19.5 us  [exchange(): lax.all_to_all(blocks, 'seq', split_axis=0, concat_axis=0, tiled=True, ax...]
    all_to_all x3 -> x4, starting transfers between devices: 32.3 us -> 44.9 us  [exchange(): lax.all_to_all(blocks, 'seq', split_axis=0, concat_axis=0, tiled=True, ax...]
    unnamed x16 -> x40, local copies, waits for them, and re-layouts: 0.61 us -> 10 us
    ppermute x1, starting transfers between devices: 12.6 us -> 4.87 us  [swap_core(): lax.ppermute(block, 'batch', [(i, i ^ 1) for i in range(lax.axis_size('ba...]
    ppermute x0 -> x1, starting transfers between devices: none -> 2.63 us  [swap_place(): lax.ppermute(block, 'seq', [(i, i ^ 2) for i in range(lax.axis_size('seq'...]
    select_n x2 -> x0, other arithmetic: 2.51 us -> none  [the longest x1 1.8 us: local(): jnp.where(side == 0, w_mine, w_other).reshape(4, feature_here, width)]
  transfers between devices with their start and end apart: 15 -> 17, of which waited for: 6 -> 6; matrix products, arithmetic and copies ran while one was open for 4% -> 4% of each run, Pallas kernels for 2% -> 5%
where the time goes in v6:
time: 178 us; the launch traced here: 177 us
  starting transfers between devices  93.3 us (52%)
  waiting for transfers between devices  47.8 us (27%)
  Pallas kernels  17.3 us (10%)
  local copies, waits for them, and re-layouts  14.8 us (8%)
    all_to_all x4, starting transfers between devices, exchange(): lax.all_to_all(blocks, 'seq', split_axis=0, concat_axis=0, tiled=True, ax...  44.9 us
    all_to_all x4, waiting for transfers between devices, exchange(): lax.all_to_all(blocks, 'seq', split_axis=0, concat_axis=0, tiled=True, ax...  19.5 us
    ppermute x4, starting transfers between devices, from_place(): lax.ppermute(block, 'seq', [(i, (i + 2 * shift) % count) for i in range(c...  18.6 us
    ppermute x4, waiting for transfers between devices, from_place(): lax.ppermute(block, 'seq', [(i, (i + 2 * shift) % count) for i in range(c...  17.7 us
    ppermute x4, starting transfers between devices, swap_pair(): lax.ppermute(block, 'seq', [(i, i ^ 1) for i in range(lax.axis_size('seq'...  11.6 us
    ppermute x3, starting transfers between devices, from_row(): lax.ppermute(block, 'batch', [(i, (i + 4 * shift) % count) for i in range...  10.7 us
    unnamed x40, local copies, waits for them, and re-layouts  10 us
    ppermute x3, waiting for transfers between devices, from_row(): lax.ppermute(block, 'batch', [(i, (i + 4 * shift) % count) for i in range...  7.13 us
  transfers between devices with their start and end apart: 17, of which 6 were waited for; matrix products, arithmetic and copies ran while one was open for 4% of the time, Pallas kernels for 5%

profile of v6, /device:TPU:1, one launch (start us, length us, event | category | flops | bytes accessed | tf_op | source)
XLA Modules:
  0.0 176.5 jit_solution(4937276512266758820)
XLA Ops:
  0.1 0.6 copy-done.22
  0.7 2.6 %shard_map.92 = bf16[4,32,1024]{2,1,0:T(8,128)(2,1)} custom-call(s32[2]{0:T(128)S(1)} %pad_add_fusion.2.refs_0_.numbers, s32[1,512]{1,0:T(1,128)S(1)} %bitcast.84, bf16[512,1024]{1,0:T(8,128)(2,1)} %table.1), custom_call_target="tpu_custom_call" | custom-call | flops 33554432 | bytes 1048576 | tf_op jit(solution)/shard_map/pallas_call | solution.py:118
  3.3 15.8 %all-to-all-start.1 = ((bf16[4,32,1024]{2,1,0:T(8,128)(2,1)}), bf16[4,32,1024]{2,1,0:T(8,128)(2,1)S(1)}, u32[]{:S(2)}, u32[]{:S(2)}) async-start(bf16[4,32,1024]{2,1,0:T(8,128)(2,1)} %shard_map.92), calls=%async_computation.1 | async-start | bytes 524288 | tf_op jit(solution)/shard_map/all_to_all | solution.py:17
  19.0 0.8 constant_dynamic-slice_fusion
  19.9 3.3 %collective-permute-start.8 = (bf16[144,1024]{1,0:T(8,128)(2,1)S(1)}, bf16[144,1024]{1,0:T(8,128)(2,1)S(1)}, u32[]{:S(2)}, u32[]{:S(2)}) collective-permute-start(bf16[144,1024]{1,0:T(8,128)(2,1)S(1)} %pad_maximum_fusion.1), channel_id=1, source_target_pairs={{0,1},{1,0},{2,3},{3,2},{4,5},{5,4},{6,7},{7,6},{8,9},{9,8},{10,11... | collective-permute-start | bytes 884744 | tf_op jit(solution)/shard_map/ppermute | solution.py:37
  23.1 0.8 constant_dynamic-update-slice_fusion.1
  24.0 0.8 constant_dynamic-update-slice_fusion
  24.8 2.6 %collective-permute-start.9 = (bf16[512,1024]{1,0:T(8,128)(2,1)}, bf16[512,1024]{1,0:T(8,128)(2,1)S(1)}, u32[]{:S(2)}, u32[]{:S(2)}) collective-permute-start(bf16[512,1024]{1,0:T(8,128)(2,1)} %constant_dynamic-update-slice_fusion), channel_id=1, source_target_pairs={{0,2},{1,3},{2,0},{3,1},{4,6},{5,7},{6,4},{7,5},{8,10},{9,11},{10,... | collective-permute-start | bytes 3145736 | tf_op jit(solution)/shard_map/ppermute | solution.py:41
  27.5 2.2 %collective-permute-start.10 = (bf16[512,1024]{1,0:T(8,128)(2,1)}, bf16[512,1024]{1,0:T(8,128)(2,1)S(1)}, u32[]{:S(2)}, u32[]{:S(2)}) collective-permute-start(bf16[512,1024]{1,0:T(8,128)(2,1)} %constant_dynamic-update-slice_fusion), channel_id=1, source_target_pairs={{0,1},{1,0},{2,3},{3,2},{4,5},{5,4},{6,7},{7,6},{8,9},{9,8},{10,11... | collective-permute-start | bytes 3145736 | tf_op jit(solution)/shard_map/ppermute | solution.py:37
  29.6 0.7 constant_dynamic-slice_fusion.1.w_slice
  30.4 0.7 copy-done.14
  31.1 1.3 shard_map.93
  32.8 11.1 %all-to-all-start.2 = ((bf16[16,64,128]{2,1,0:T(8,128)(2,1)}), bf16[16,64,128]{2,1,0:T(8,128)(2,1)S(1)}, u32[]{:S(2)}, u32[]{:S(2)}) async-start(bf16[16,64,128]{2,1,0:T(8,128)(2,1)} %shard_map.93), calls=%async_computation.2 | async-start | bytes 524288 | tf_op jit(solution)/shard_map/all_to_all | solution.py:17
  43.9 0.7 fusion.5
  44.6 4.2 %collective-permute-start.6 = (bf16[64,1024]{1,0:T(8,128)(2,1)S(1)}, bf16[64,1024]{1,0:T(8,128)(2,1)S(1)}, u32[]{:S(2)}, u32[]{:S(2)}) collective-permute-start(bf16[64,1024]{1,0:T(8,128)(2,1)S(1)} %bitcast.82), channel_id=1, source_target_pairs={{0,4},{1,5},{2,6},{3,7},{4,8},{5,9},{6,10},{7,11},{8,12},{9,13},{1... | collective-permute-start | bytes 393224 | tf_op jit(solution)/shard_map/ppermute | solution.py:33
  48.7 3.1 %collective-permute-start.4 = (bf16[128,1024]{1,0:T(8,128)(2,1)S(1)}, bf16[128,1024]{1,0:T(8,128)(2,1)S(1)}, u32[]{:S(2)}, u32[]{:S(2)}) collective-permute-start(bf16[128,1024]{1,0:T(8,128)(2,1)S(1)} %bitcast.68), channel_id=1, source_target_pairs={{0,2},{1,3},{2,4},{3,5},{4,6},{5,7},{6,8},{7,9},{8,10},{9,11},{10,... | collective-permute-start | bytes 786440 | tf_op jit(solution)/shard_map/ppermute | solution.py:33
  51.8 3.4 %collective-permute-start.5 = (bf16[128,1024]{1,0:T(8,128)(2,1)S(1)}, bf16[128,1024]{1,0:T(8,128)(2,1)S(1)}, u32[]{:S(2)}, u32[]{:S(2)}) collective-permute-start(bf16[128,1024]{1,0:T(8,128)(2,1)S(1)} %bitcast.69), channel_id=1, source_target_pairs={{0,30},{1,31},{2,0},{3,1},{4,2},{5,3},{6,4},{7,5},{8,6},{9,7},{10,... | collective-permute-start | bytes 786440 | tf_op jit(solution)/shard_map/ppermute | solution.py:33
  55.3 17.7 %collective-permute-done.6.rows_3 = bf16[64,1024]{1,0:T(8,128)(2,1)S(1)} collective-permute-done((bf16[64,1024]{1,0:T(8,128)(2,1)S(1)}, bf16[64,1024]{1,0:T(8,128)(2,1)S(1)}, u32[]{:S(2)}, u32[]{:S(2)}) %collective-permute-start.6) | collective-permute-done | bytes 131104 | tf_op jit(solution)/shard_map/ppermute | solution.py:33
  73.0 8.0 %collective-permute-start.7 = (bf16[64,1024]{1,0:T(8,128)(2,1)}, bf16[64,1024]{1,0:T(8,128)(2,1)}, u32[]{:S(2)}, u32[]{:S(2)}) collective-permute-start(bf16[64,1024]{1,0:T(8,128)(2,1)} %bitcast.12), channel_id=1, source_target_pairs={{0,28},{1,29},{2,30},{3,31},{4,0},{5,1},{6,2},{7,3},{8,4},{9,5},{1... | collective-permute-start | bytes 393224 | tf_op jit(solution)/shard_map/ppermute | solution.py:33
  80.9 0.6 copy-done.11
  81.6 1.5 shard_map.91
  83.7 0.6 copy-done.12
  84.4 3.1 %shard_map.94 = (bf16[256,256]{1,0:T(8,128)(2,1)}, bf16[320,256]{1,0:T(8,128)(2,1)}, bf16[16,1024]{1,0:T(8,128)(2,1)}) custom-call(s32[2]{0:T(128)S(1)} %copy-done.12, s32[512,1]{1,0:T(8,128)S(1)} %get-tuple-element.80.at, s32[32,1]{1,0:T(8,128)S(1)} %get-tuple-element.81.at_pair, bf16[128,1024]{1,0:T(8,128)(2,1)S(1)} %bitcast.70, ...), custom_call_target="tpu_custom_call" | custom-call | flops 402653184 | bytes 1572864 | tf_op jit(solution)/shard_map/pallas_call | solution.py:254
  87.4 0.7 copy-done.23
  88.1 0.6 while.14
  88.8 2.8 %collective-permute-start.11 = (bf16[320,256]{1,0:T(8,128)(2,1)}, bf16[320,256]{1,0:T(8,128)(2,1)S(1)}, u32[]{:S(2)}, u32[]{:S(2)}) collective-permute-start(bf16[320,256]{1,0:T(8,128)(2,1)} %get-tuple-element.92), channel_id=1, source_target_pairs={{0,1},{1,0},{2,3},{3,2},{4,5},{5,4},{6,7},{7,6},{8,9},{9,8},{10,11... | collective-permute-start | bytes 491528 | tf_op jit(solution)/shard_map/ppermute | solution.py:37
  91.6 3.4 %collective-permute-done.11.refs_1_ = bf16[320,256]{1,0:T(8,128)(2,1)S(1)} collective-permute-done((bf16[320,256]{1,0:T(8,128)(2,1)}, bf16[320,256]{1,0:T(8,128)(2,1)S(1)}, u32[]{:S(2)}, u32[]{:S(2)}) %collective-permute-start.11) | collective-permute-done | bytes 163872 | tf_op jit(solution)/shard_map/ppermute | solution.py:37
  95.0 1.8 %shard_map.95 = (bf16[16,16,768]{2,1,0:T(8,128)(2,1)}, bf16[16,1024]{1,0:T(8,128)(2,1)S(1)}) custom-call(bf16[256,256]{1,0:T(8,128)(2,1)} %get-tuple-element.91.refs_0_, bf16[320,256]{1,0:T(8,128)(2,1)S(1)} %collective-permute-done.11.refs_1_, bf16[16,1024]{1,0:T(8,128)(2,1)} %get-tuple-element.93.refs_2_), custom_call_target="tpu_custom_call" | custom-call | flops 65536 | bytes 524288 | tf_op jit(solution)/shard_map/pallas_call | solution.py:314
  96.9 6.4 %all-to-all-start.3 = ((bf16[16,16,768]{2,1,0:T(8,128)(2,1)}), bf16[16,16,768]{2,1,0:T(8,128)(2,1)S(1)}, u32[]{:S(2)}, u32[]{:S(2)}) async-start(bf16[16,16,768]{2,1,0:T(8,128)(2,1)} %get-tuple-element.94), calls=%async_computation.3 | async-start | bytes 786432 | tf_op jit(solution)/shard_map/all_to_all | solution.py:17
  103.3 3.4 %collective-permute-start.12 = (bf16[512,1024]{1,0:T(8,128)(2,1)S(1)}, bf16[512,1024]{1,0:T(8,128)(2,1)S(1)}, u32[]{:S(2)}, u32[]{:S(2)}) collective-permute-start(bf16[512,1024]{1,0:T(8,128)(2,1)S(1)} %collective-permute-done.9.rest_1_.refs_5_.refs_6_), channel_id=1, source_target_pairs={{0,1},{1,0},{2,3},{3,2},{4,5},{5,4},{6,7},{7,6},{8,9},{9,8},{10,11... | collective-permute-start | bytes 3145736 | tf_op jit(solution)/shard_map/ppermute | solution.py:37
  107.4 3.2 %collective-permute-start.13 = (bf16[1024,128]{1,0:T(8,128)(2,1)S(1)}, bf16[1024,128]{1,0:T(8,128)(2,1)S(1)}, u32[]{:S(2)}, u32[]{:S(2)}) collective-permute-start(bf16[1024,128]{1,0:T(8,128)(2,1)S(1)} %bitcast.63), channel_id=1, source_target_pairs={{0,128},{32,160},{64,192},{96,224},{128,256},{160,288},{192,320},{... | collective-permute-start | bytes 786440 | tf_op jit(solution)/shard_map/ppermute | solution.py:50
  110.6 4.5 %collective-permute-start.14 = (bf16[1024,128]{1,0:T(8,128)(2,1)S(1)}, bf16[1024,128]{1,0:T(8,128)(2,1)S(1)}, u32[]{:S(2)}, u32[]{:S(2)}) collective-permute-start(bf16[1024,128]{1,0:T(8,128)(2,1)S(1)} %bitcast.64), channel_id=1, source_target_pairs={{0,256},{32,288},{64,320},{96,352},{128,384},{160,416},{192,448},{... | collective-permute-start | bytes 786440 | tf_op jit(solution)/shard_map/ppermute | solution.py:50
  115.1 3.0 %collective-permute-start.15 = (bf16[1024,128]{1,0:T(8,128)(2,1)S(1)}, bf16[1024,128]{1,0:T(8,128)(2,1)S(1)}, u32[]{:S(2)}, u32[]{:S(2)}) collective-permute-start(bf16[1024,128]{1,0:T(8,128)(2,1)S(1)} %bitcast.65), channel_id=1, source_target_pairs={{0,384},{32,416},{64,448},{96,480},{128,0},{160,32},{192,64},{224,... | collective-permute-start | bytes 786440 | tf_op jit(solution)/shard_map/ppermute | solution.py:50
  118.2 3.8 %collective-permute-done.14.refs_12_.rest_2_ = bf16[1024,128]{1,0:T(8,128)(2,1)S(1)} collective-permute-done((bf16[1024,128]{1,0:T(8,128)(2,1)S(1)}, bf16[1024,128]{1,0:T(8,128)(2,1)S(1)}, u32[]{:S(2)}, u32[]{:S(2)}) %collective-permute-start.14) | collective-permute-done | bytes 262176 | tf_op jit(solution)/shard_map/ppermute | solution.py:50
  122.1 3.3 %collective-permute-done.15.refs_13_.rest_3_ = bf16[1024,128]{1,0:T(8,128)(2,1)S(1)} collective-permute-done((bf16[1024,128]{1,0:T(8,128)(2,1)S(1)}, bf16[1024,128]{1,0:T(8,128)(2,1)S(1)}, u32[]{:S(2)}, u32[]{:S(2)}) %collective-permute-start.15) | collective-permute-done | bytes 262176 | tf_op jit(solution)/shard_map/ppermute | solution.py:50
  125.4 1.1 pad_maximum_fusion
  126.5 4.9 %collective-permute-start.16 = (bf16[4,1024,128]{2,1,0:T(8,128)(2,1)}, bf16[4,1024,128]{2,1,0:T(8,128)(2,1)}, u32[]{:S(2)}, u32[]{:S(2)}) collective-permute-start(bf16[4,1024,128]{2,1,0:T(8,128)(2,1)} %pad_maximum_fusion), channel_id=1, source_target_pairs={{0,32},{32,0},{64,96},{96,64},{128,160},{160,128},{192,224},{224,1... | collective-permute-start | bytes 3145736 | tf_op jit(solution)/shard_map/ppermute | solution.py:45
  132.2 1.0 copy-done
  133.2 1.2 copy-done.1
  134.4 0.9 copy-done.3
  135.4 1.0 copy-done.6
  136.4 1.0 copy-done.8
  137.5 4.4 %shard_map.96.refs_3_ = bf16[128,1024]{1,0:T(8,128)(2,1)} custom-call(bf16[16,16,768]{2,1,0:T(8,128)(2,1)S(1)} %all-to-all-done.3.refs_0_.refs_1_, bf16[256,1024]{1,0:T(8,128)(2,1)S(1)} %copy-done.8, bf16[256,1024]{1,0:T(8,128)(2,1)S(1)} %copy-done.6, bf16[512,1024]{1,0:T(8,128)(2,1)S(1)} %collective-permute-done.10.rest_2_.refs_3_.refs_4_, ...), custom_call_target="tpu_custom_call" | custom-call | flops 536870912 | bytes 4718592 | tf_op jit(solution)/shard_map/pallas_call | solution.py:410
  141.9 11.6 %all-to-all-start.4 = ((bf16[8,16,1024]{2,1,0:T(8,128)(2,1)}), bf16[8,16,1024]{2,1,0:T(8,128)(2,1)S(1)}, u32[]{:S(2)}, u32[]{:S(2)}) async-start(bf16[8,16,1024]{2,1,0:T(8,128)(2,1)} %bitcast.20), calls=%async_computation.4 | async-start | bytes 524288 | tf_op jit(solution)/shard_map/all_to_all | solution.py:17
  153.5 1.3 slice_bitcast_fusion
  154.8 0.9 shard_map.97
  155.7 19.1 %all-to-all-done.4.parts = bf16[8,16,1024]{2,1,0:T(8,128)(2,1)S(1)} async-done(((bf16[8,16,1024]{2,1,0:T(8,128)(2,1)}), bf16[8,16,1024]{2,1,0:T(8,128)(2,1)S(1)}, u32[]{:S(2)}, u32[]{:S(2)}) %all-to-all-start.4) | async-done | bytes 262176 | tf_op jit(solution)/shard_map/all_to_all | solution.py:17
  174.8 1.7 shard_map.98
  (53 shorter events, 2.2 us)
Async XLA Ops:
  0.0 0.7 copy-start.22
  0.1 30.3 %copy-start.10 = (s32[2]{0:T(128)}, s32[2]{0:T(128)S(1)}, u32[]{:S(2)}) copy-start(s32[2]{0:T(128)S(1)} %pad_add_fusion.2.refs_0_.numbers) | copy-start | bytes 28
  3.3 16.6 %copy-start.15 = (bf16[1024,4,32]{0,2,1:T(8,128)(2,1)S(1)}, bf16[1024,4,32]{0,2,1:T(8,128)(2,1)}, u32[]{:S(2)}) copy-start(bf16[1024,4,32]{0,2,1:T(8,128)(2,1)} %param.16) | copy-start | bytes 786436
  3.3 29.5 %all-to-all-start.1 = ((bf16[4,32,1024]{2,1,0:T(8,128)(2,1)}), bf16[4,32,1024]{2,1,0:T(8,128)(2,1)S(1)}, u32[]{:S(2)}, u32[]{:S(2)}) async-start(bf16[4,32,1024]{2,1,0:T(8,128)(2,1)} %shard_map.92), calls=%async_computation.1 | async-start | bytes 524288 | tf_op jit(solution)/shard_map/all_to_all | solution.py:17
  19.0 4.1 %copy-start.5 = (bf16[256,1024]{1,0:T(8,128)(2,1)S(1)}, bf16[256,1024]{1,0:T(8,128)(2,1)}, u32[]{:S(2)}) copy-start(bf16[256,1024]{1,0:T(8,128)(2,1)} %refs_2_.1) | copy-start | bytes 1572868
  19.9 4.1 %copy-start.7 = (bf16[256,1024]{1,0:T(8,128)(2,1)S(1)}, bf16[256,1024]{1,0:T(8,128)(2,1)}, u32[]{:S(2)}) copy-start(bf16[256,1024]{1,0:T(8,128)(2,1)} %refs_1_.1) | copy-start | bytes 1572868
  19.9 10.5 %collective-permute-start.8 = (bf16[144,1024]{1,0:T(8,128)(2,1)S(1)}, bf16[144,1024]{1,0:T(8,128)(2,1)S(1)}, u32[]{:S(2)}, u32[]{:S(2)}) collective-permute-start(bf16[144,1024]{1,0:T(8,128)(2,1)S(1)} %pad_maximum_fusion.1), channel_id=1, source_target_pairs={{0,1},{1,0},{2,3},{3,2},{4,5},{5,4},{6,7},{7,6},{8,9},{9,8},{10,11... | collective-permute-start | bytes 884744 | tf_op jit(solution)/shard_map/ppermute | solution.py:37
  24.8 58.9 %collective-permute-start.9 = (bf16[512,1024]{1,0:T(8,128)(2,1)}, bf16[512,1024]{1,0:T(8,128)(2,1)S(1)}, u32[]{:S(2)}, u32[]{:S(2)}) collective-permute-start(bf16[512,1024]{1,0:T(8,128)(2,1)} %constant_dynamic-update-slice_fusion), channel_id=1, source_target_pairs={{0,2},{1,3},{2,0},{3,1},{4,6},{5,7},{6,4},{7,5},{8,10},{9,11},{10,... | collective-permute-start | bytes 3145736 | tf_op jit(solution)/shard_map/ppermute | solution.py:41
  27.5 56.2 %collective-permute-start.10 = (bf16[512,1024]{1,0:T(8,128)(2,1)}, bf16[512,1024]{1,0:T(8,128)(2,1)S(1)}, u32[]{:S(2)}, u32[]{:S(2)}) collective-permute-start(bf16[512,1024]{1,0:T(8,128)(2,1)} %constant_dynamic-update-slice_fusion), channel_id=1, source_target_pairs={{0,1},{1,0},{2,3},{3,2},{4,5},{5,4},{6,7},{7,6},{8,9},{9,8},{10,11... | collective-permute-start | bytes 3145736 | tf_op jit(solution)/shard_map/ppermute | solution.py:37
  30.3 0.7 copy-start.14
  32.8 50.9 %all-to-all-start.2 = ((bf16[16,64,128]{2,1,0:T(8,128)(2,1)}), bf16[16,64,128]{2,1,0:T(8,128)(2,1)S(1)}, u32[]{:S(2)}, u32[]{:S(2)}) async-start(bf16[16,64,128]{2,1,0:T(8,128)(2,1)} %shard_map.93), calls=%async_computation.2 | async-start | bytes 524288 | tf_op jit(solution)/shard_map/all_to_all | solution.py:17
  44.6 28.4 %collective-permute-start.6 = (bf16[64,1024]{1,0:T(8,128)(2,1)S(1)}, bf16[64,1024]{1,0:T(8,128)(2,1)S(1)}, u32[]{:S(2)}, u32[]{:S(2)}) collective-permute-start(bf16[64,1024]{1,0:T(8,128)(2,1)S(1)} %bitcast.82), channel_id=1, source_target_pairs={{0,4},{1,5},{2,6},{3,7},{4,8},{5,9},{6,10},{7,11},{8,12},{9,13},{1... | collective-permute-start | bytes 393224 | tf_op jit(solution)/shard_map/ppermute | solution.py:33
  48.7 34.9 %collective-permute-start.4 = (bf16[128,1024]{1,0:T(8,128)(2,1)S(1)}, bf16[128,1024]{1,0:T(8,128)(2,1)S(1)}, u32[]{:S(2)}, u32[]{:S(2)}) collective-permute-start(bf16[128,1024]{1,0:T(8,128)(2,1)S(1)} %bitcast.68), channel_id=1, source_target_pairs={{0,2},{1,3},{2,4},{3,5},{4,6},{5,7},{6,8},{7,9},{8,10},{9,11},{10,... | collective-permute-start | bytes 786440 | tf_op jit(solution)/shard_map/ppermute | solution.py:33
  51.8 31.8 %collective-permute-start.5 = (bf16[128,1024]{1,0:T(8,128)(2,1)S(1)}, bf16[128,1024]{1,0:T(8,128)(2,1)S(1)}, u32[]{:S(2)}, u32[]{:S(2)}) collective-permute-start(bf16[128,1024]{1,0:T(8,128)(2,1)S(1)} %bitcast.69), channel_id=1, source_target_pairs={{0,30},{1,31},{2,0},{3,1},{4,2},{5,3},{6,4},{7,5},{8,6},{9,7},{10,... | collective-permute-start | bytes 786440 | tf_op jit(solution)/shard_map/ppermute | solution.py:33
  73.0 10.7 %collective-permute-start.7 = (bf16[64,1024]{1,0:T(8,128)(2,1)}, bf16[64,1024]{1,0:T(8,128)(2,1)}, u32[]{:S(2)}, u32[]{:S(2)}) collective-permute-start(bf16[64,1024]{1,0:T(8,128)(2,1)} %bitcast.12), channel_id=1, source_target_pairs={{0,28},{1,29},{2,30},{3,31},{4,0},{5,1},{6,2},{7,3},{8,4},{9,5},{1... | collective-permute-start | bytes 393224 | tf_op jit(solution)/shard_map/ppermute | solution.py:33
  80.9 0.7 copy-start.11
  83.7 0.7 copy-start.12
  87.4 0.7 copy-start.23
  88.8 6.3 %collective-permute-start.11 = (bf16[320,256]{1,0:T(8,128)(2,1)}, bf16[320,256]{1,0:T(8,128)(2,1)S(1)}, u32[]{:S(2)}, u32[]{:S(2)}) collective-permute-start(bf16[320,256]{1,0:T(8,128)(2,1)} %get-tuple-element.92), channel_id=1, source_target_pairs={{0,1},{1,0},{2,3},{3,2},{4,5},{5,4},{6,7},{7,6},{8,9},{9,8},{10,11... | collective-permute-start | bytes 491528 | tf_op jit(solution)/shard_map/ppermute | solution.py:37
  96.9 36.4 %all-to-all-start.3 = ((bf16[16,16,768]{2,1,0:T(8,128)(2,1)}), bf16[16,16,768]{2,1,0:T(8,128)(2,1)S(1)}, u32[]{:S(2)}, u32[]{:S(2)}) async-start(bf16[16,16,768]{2,1,0:T(8,128)(2,1)} %get-tuple-element.94), calls=%async_computation.3 | async-start | bytes 786432 | tf_op jit(solution)/shard_map/all_to_all | solution.py:17
  103.3 28.9 %collective-permute-start.12 = (bf16[512,1024]{1,0:T(8,128)(2,1)S(1)}, bf16[512,1024]{1,0:T(8,128)(2,1)S(1)}, u32[]{:S(2)}, u32[]{:S(2)}) collective-permute-start(bf16[512,1024]{1,0:T(8,128)(2,1)S(1)} %collective-permute-done.9.rest_1_.refs_5_.refs_6_), channel_id=1, source_target_pairs={{0,1},{1,0},{2,3},{3,2},{4,5},{5,4},{6,7},{7,6},{8,9},{9,8},{10,11... | collective-permute-start | bytes 3145736 | tf_op jit(solution)/shard_map/ppermute | solution.py:37
  107.4 10.8 %collective-permute-start.13 = (bf16[1024,128]{1,0:T(8,128)(2,1)S(1)}, bf16[1024,128]{1,0:T(8,128)(2,1)S(1)}, u32[]{:S(2)}, u32[]{:S(2)}) collective-permute-start(bf16[1024,128]{1,0:T(8,128)(2,1)S(1)} %bitcast.63), channel_id=1, source_target_pairs={{0,128},{32,160},{64,192},{96,224},{128,256},{160,288},{192,320},{... | collective-permute-start | bytes 786440 | tf_op jit(solution)/shard_map/ppermute | solution.py:50
  110.6 11.5 %collective-permute-start.14 = (bf16[1024,128]{1,0:T(8,128)(2,1)S(1)}, bf16[1024,128]{1,0:T(8,128)(2,1)S(1)}, u32[]{:S(2)}, u32[]{:S(2)}) collective-permute-start(bf16[1024,128]{1,0:T(8,128)(2,1)S(1)} %bitcast.64), channel_id=1, source_target_pairs={{0,256},{32,288},{64,320},{96,352},{128,384},{160,416},{192,448},{... | collective-permute-start | bytes 786440 | tf_op jit(solution)/shard_map/ppermute | solution.py:50
  115.1 10.2 %collective-permute-start.15 = (bf16[1024,128]{1,0:T(8,128)(2,1)S(1)}, bf16[1024,128]{1,0:T(8,128)(2,1)S(1)}, u32[]{:S(2)}, u32[]{:S(2)}) collective-permute-start(bf16[1024,128]{1,0:T(8,128)(2,1)S(1)} %bitcast.65), channel_id=1, source_target_pairs={{0,384},{32,416},{64,448},{96,480},{128,0},{160,32},{192,64},{224,... | collective-permute-start | bytes 786440 | tf_op jit(solution)/shard_map/ppermute | solution.py:50
  125.4 1.1 copy-start.2
  126.5 27.0 %collective-permute-start.16 = (bf16[4,1024,128]{2,1,0:T(8,128)(2,1)}, bf16[4,1024,128]{2,1,0:T(8,128)(2,1)}, u32[]{:S(2)}, u32[]{:S(2)}) collective-permute-start(bf16[4,1024,128]{2,1,0:T(8,128)(2,1)} %pad_maximum_fusion), channel_id=1, source_target_pairs={{0,32},{32,0},{64,96},{96,64},{128,160},{160,128},{192,224},{224,1... | collective-permute-start | bytes 3145736 | tf_op jit(solution)/shard_map/ppermute | solution.py:45
  131.4 0.7 copy-start.9
  132.2 1.0 copy-start
  133.2 1.2 copy-start.1
  134.4 0.9 copy-start.3
  135.4 1.0 copy-start.6
  136.4 1.0 copy-start.8
  141.9 32.9 %all-to-all-start.4 = ((bf16[8,16,1024]{2,1,0:T(8,128)(2,1)}), bf16[8,16,1024]{2,1,0:T(8,128)(2,1)S(1)}, u32[]{:S(2)}, u32[]{:S(2)}) async-start(bf16[8,16,1024]{2,1,0:T(8,128)(2,1)} %bitcast.20), calls=%async_computation.4 | async-start | bytes 524288 | tf_op jit(solution)/shard_map/all_to_all | solution.py:17
  153.5 1.3 copy-start.13
  154.8 20.0 %copy-start.4 = (bf16[1024,128]{1,0:T(8,128)(2,1)S(1)}, bf16[1024,128]{1,0:T(8,128)(2,1)}, u32[]{:S(2)}) copy-start(bf16[1024,128]{1,0:T(8,128)(2,1)} %copy-done.2) | copy-start | bytes 786436

commit v7 on v6

--- a/solution.py
+++ b/solution.py
@@ -25,7 +25,9 @@
 
 def class_groups():
     column = lax.axis_size("seq") // 2
-    return groups_of([list(range(at, column, 2)) for at in range(2)])
+    return groups_of(
+        [[place for place in range(column) if head_class(place) == kind] for kind in range(2)]
+    )
 
 
 def from_place(block, shift):
@@ -37,8 +39,21 @@
     return lax.ppermute(block, "seq", [(i, i ^ 1) for i in range(lax.axis_size("seq"))])
 
 
+def head_class(place):
+    return place // 2 % 2
+
+
+def partner_place(place, column):
+    return (place + 2 * (place % 2) - 1) % column
+
+
 def swap_place(block):
-    return lax.ppermute(block, "seq", [(i, i ^ 2) for i in range(lax.axis_size("seq"))])
+    count = lax.axis_size("seq")
+    return lax.ppermute(
+        block,
+        "seq",
+        [(i, 2 * partner_place(i // 2, count // 2) + i % 2) for i in range(count)],
+    )
 
 
 def swap_core(block):
@@ -65,16 +80,39 @@
     )
 
 
-def bucket_bias(rab_table, distance):
-    bucket_count = rab_table.shape[1]
-    powers = 2 ** jnp.arange(bucket_count - 1, dtype=jnp.int32)
-    bucket = jnp.sum((distance[:, None] >= powers[None, :]).astype(jnp.int32), axis=1)
-    hits = (bucket[None, :] == jnp.arange(bucket_count, dtype=jnp.int32)[:, None]).astype(
-        jnp.float32
-    )
-    return jnp.dot(
-        rab_table, hits, precision=lax.Precision.HIGHEST, preferred_element_type=jnp.float32
-    )
+def bias_kernel(numbers, rab, bias, live):
+    head_count, bucket_count = rab.shape
+    sources = numbers.shape[0] - 1
+    events = bias.shape[1] // sources
+    step = lax.broadcasted_iota(jnp.int32, (head_count, events), 1)
+    for source in range(sources):
+        here = slice(source * events, (source + 1) * events)
+        distance = numbers[0] - numbers[1 + source] * events - step
+        bucket = jnp.zeros((head_count, events), jnp.int32)
+        for power in range(bucket_count - 1):
+            bucket = bucket + (distance >= 2**power).astype(jnp.int32)
+        total = jnp.zeros((head_count, events), jnp.float32)
+        for entry in range(bucket_count):
+            total = total + jnp.where(bucket == entry, rab[:, entry : entry + 1], 0.0)
+        bias[:, here] = total
+        live[:, here] = (distance[:1] > 0).astype(jnp.float32)
+
+
+def biases(numbers, rab, events):
+    whole = pl.BlockSpec(memory_space=pltpu.VMEM)
+    count = (numbers.shape[0] - 1) * events
+    return pl.pallas_call(
+        bias_kernel,
+        in_specs=[pl.BlockSpec(memory_space=pltpu.SMEM), whole],
+        out_specs=[whole] * 2,
+        out_shape=[
+            jax.ShapeDtypeStruct((rab.shape[0], count), jnp.float32),
+            jax.ShapeDtypeStruct((1, count), jnp.float32),
+        ],
+        cost_estimate=pl.CostEstimate(
+            flops=64 * rab.shape[0] * count, bytes_accessed=40 * count, transcendentals=0
+        ),
+    )(numbers, rab)
 
 
 def silu(value):
@@ -129,6 +167,42 @@
     )(numbers, ids.reshape(1, -1), table)
 
 
+def split_kernel(head_size, kind, keys, values, kept, sent):
+    events, width = keys.shape
+
+    def place(parity):
+        for first, array in ((0, keys), (events, values)):
+            for head in range(0, width // head_size, 2):
+                lanes = slice(head // 2 * head_size, (head // 2 + 1) * head_size)
+                for out, which in ((kept, head + parity), (sent, head + 1 - parity)):
+                    out[first : first + events, lanes] = array[
+                        :, which * head_size : (which + 1) * head_size
+                    ]
+
+    @pl.when(kind[0] == 0)
+    def _():
+        place(0)
+
+    @pl.when(kind[0] != 0)
+    def _():
+        place(1)
+
+
+def split_heads(kind, keys, values, head_size):
+    whole = pl.BlockSpec(memory_space=pltpu.VMEM)
+    events, width = keys.shape
+    return pl.pallas_call(
+        lambda *refs: split_kernel(head_size, *refs),
+        in_specs=[pl.BlockSpec(memory_space=pltpu.SMEM), whole, whole],
+        out_specs=[whole] * 2,
+        out_shape=[jax.ShapeDtypeStruct((2 * events, width // 2), jnp.bfloat16)] * 2,
+        compiler_params=pltpu.CompilerParams(vmem_limit_bytes=32 * 1024 * 1024),
+        cost_estimate=pl.CostEstimate(
+            flops=4 * events * width, bytes_accessed=8 * events * width, transcendentals=0
+        ),
+    )(kind, keys, values)
+
+
 def locate_kernel(table_rows, numbers, ids, slots, pair_slots, most):
     count, devices = ids.shape[1], most.shape[0]
     index = numbers[0]
@@ -167,9 +241,7 @@
     half = at // (count // 2)
     inner = at - half * (count // 2)
     owner_side = jnp.where(half == 0, side, 1 - side)
-    kind = inner // (count // 4)
-    owner = 2 * ((inner - kind * (count // 4)) // own) + kind
-    original = owner * (2 * own) + owner_side * own + lax.rem(inner, own)
+    original = (inner // own) * (2 * own) + owner_side * own + lax.rem(inner, own)
     spread(original == lax.broadcasted_iota(jnp.int32, (count, count), 1), slots)
     at = lax.broadcasted_iota(jnp.int32, (2 * own, count), 0)
     half = at // own
@@ -272,8 +344,8 @@
     )(numbers, at, at_pair, *rows, mine, other, *ready)
 
 
-def pack_kernel(feature_here, mine, arrived, own_rows, *rest):
-    packed, embedded = rest[-2:]
+def pack_kernel(feature_here, numbers, mine, arrived, own_rows, w_slice, w_other, *rest):
+    queries, packed, embedded = rest[-3:]
     cand_side, columns = mine.shape
     own = own_rows.shape[0]
     proj = mine[...].astype(jnp.float32) + arrived[:cand_side, :].astype(jnp.float32)
@@ -284,38 +356,45 @@
             own_rows[:, lanes].astype(jnp.float32) + other.astype(jnp.float32)
         ).astype(jnp.bfloat16)
     block = 4 * feature_here
-    queries = jnp.concatenate(
+    queries[...] = jnp.concatenate(
         [
             proj[:, side * block + 2 * feature_here : side * block + 3 * feature_here]
             for side in range(2)
         ],
         axis=1,
     ).T.astype(jnp.bfloat16)
-    proj = proj.astype(jnp.bfloat16)
     column = packed.shape[0]
-    cand_class = cand_side // 2
-    for place in range(column):
-        kind = place % 2
-        first = kind * cand_class + place // 2 * own
-        packed[place, :, :columns] = proj[first : first + own, :]
-        for part in range(queries.shape[0] // own):
-            lanes = slice(columns + part * cand_class, columns + (part + 1) * cand_class)
-            packed[place, :, lanes] = queries[
-                part * own : (part + 1) * own, kind * cand_class : (kind + 1) * cand_class
-            ]
-
-
-def pack(mine, arrived, own_rows, ready, feature_here):
+    packed[:, :, :columns] = proj.astype(jnp.bfloat16).reshape(column, own, columns)
+    lanes = w_slice.shape[1]
+    first = w_other.shape[0] - own
+    here = jnp.broadcast_to(numbers[0], (own, lanes)) % 2 == 0
+    parts = w_slice.shape[0] // own
+    for part in range(parts):
+        ours = w_slice[part * own : (part + 1) * own, :].astype(jnp.float32)
+        theirs = w_other[first:, part * lanes : (part + 1) * lanes].astype(jnp.float32)
+        for place, rows in (
+            (part, jnp.where(here, ours, theirs)),
+            (parts + part, jnp.where(here, theirs, ours)),
+        ):
+            packed[:, :, columns + place * lanes : columns + (place + 1) * lanes] = (
+                jnp.broadcast_to(rows.astype(jnp.bfloat16)[None], (column, own, lanes))
+            )
+
+
+def pack(numbers, mine, arrived, own_rows, w_slice, w_other, feature_here, ready):
     cand_side, columns = mine.shape
     own = own_rows.shape[0]
     column = cand_side // own
-    packed_width = columns + 2 * feature_here * (cand_side // 2) // own
+    packed_width = columns + 2 * w_slice.shape[0] * w_slice.shape[1] // own
     whole = pl.BlockSpec(memory_space=pltpu.VMEM)
     return pl.pallas_call(
         lambda *refs: pack_kernel(feature_here, *refs),
-        in_specs=[whole] * 3 + [pl.BlockSpec(memory_space=pl.ANY)] * len(ready),
-        out_specs=[whole] * 2,
+        in_specs=[pl.BlockSpec(memory_space=pltpu.SMEM)]
+        + [whole] * 5
+        + [pl.BlockSpec(memory_space=pl.ANY)] * len(ready),
+        out_specs=[whole] * 3,
         out_shape=[
+            jax.ShapeDtypeStruct((2 * feature_here, cand_side), jnp.bfloat16),
             jax.ShapeDtypeStruct((column, own, packed_width), jnp.bfloat16),
             jax.ShapeDtypeStruct(own_rows.shape, jnp.bfloat16),
         ],
@@ -323,62 +402,19 @@
         cost_estimate=pl.CostEstimate(
             flops=cand_side * columns, bytes_accessed=8 * cand_side * columns, transcendentals=0
         ),
-    )(mine, arrived, own_rows, *ready)
-
-
-def spread_kernel(numbers, w_slice, other, out):
-    rows, lanes = w_slice.shape
-    half = rows // 2
-    first = other.shape[0] - half
-    theirs = jnp.concatenate(
-        [other[first:, :lanes], other[first:, lanes : 2 * lanes]], axis=0
-    )
-    here = jnp.broadcast_to(numbers[0], (rows, lanes)) % 2 == 0
-    ours = w_slice[...].astype(jnp.float32)
-    theirs = theirs.astype(jnp.float32)
-    top = jnp.where(here, ours, theirs).astype(jnp.bfloat16)
-    bottom = jnp.where(here, theirs, ours).astype(jnp.bfloat16)
-    for place in range(out.shape[0]):
-        out[place, :rows, :] = top
-        out[place, rows:, :] = bottom
-
-
-def spread(numbers, w_slice, other, column):
-    rows, lanes = w_slice.shape
-    whole = pl.BlockSpec(memory_space=pltpu.VMEM)
-    return pl.pallas_call(
-        spread_kernel,
-        in_specs=[pl.BlockSpec(memory_space=pltpu.SMEM), whole, whole],
-        out_specs=whole,
-        out_shape=jax.ShapeDtypeStruct((column, 2 * rows, lanes), jnp.bfloat16),
-        compiler_params=pltpu.CompilerParams(vmem_limit_bytes=32 * 1024 * 1024),
-        cost_estimate=pl.CostEstimate(
-            flops=rows * lanes, bytes_accessed=4 * column * rows * lanes, transcendentals=0
-        ),
-    )(numbers, w_slice, other)
-
-
-def attend_kernel(scale, heads, received, *refs):
-    keys_values, bias, live, summed = refs[:8], refs[8], refs[9], refs[-1]
+    )(numbers, mine, arrived, own_rows, w_slice, w_other, *ready)
+
+
+def attend_kernel(scale, heads, numbers, queries, *refs):
+    keys_values, bias, live, summed = refs[:8], refs[8], refs[9], refs[-2]
     first_head = pl.program_id(0) * heads
-    cand, lanes = summed.shape
-    head_size = lanes // heads
+    kind = numbers[0]
+    head_size = queries.shape[0] // heads
     events = keys_values[0].shape[0]
-    own = received.shape[1]
-    places = received.shape[0] // heads
-    parts = head_size // (places * own)
-    skip = received.shape[2] - parts * cand
     for head in range(heads):
-        head_queries = jnp.concatenate(
-            [
-                received[head * places + place, :, skip + part * cand : skip + (part + 1) * cand]
-                for place in range(places)
-                for part in range(parts)
-            ],
-            axis=0,
-        ).T
         lanes = slice(head * head_size, (head + 1) * head_size)
-        head_bias = 0.5 * bias[pl.ds(first_head + head, 1), :]
+        head_queries = queries[lanes, :].T
+        head_bias = 0.5 * bias[pl.ds(2 * (first_head + head) + kind, 1), :]
         total = None
         for source in range(4):
             keys, values = keys_values[2 * source], keys_values[2 * source + 1]
@@ -396,43 +432,45 @@
         summed[:, lanes] = total.astype(summed.dtype)
 
 
-def attend(received, keys, values, others, bias, live, cand, ready):
-    events, width = keys.shape
-    head_count = bias.shape[0]
-    head_size = width // head_count
-    heads = 4
+def attend(kind, queries, sources, bias, live, through):
+    width, cand = queries.shape
+    events = sources[0].shape[0] // 2
+    head_size = 2 * width // bias.shape[0]
+    heads = 2
     lanes = heads * head_size
-    column, own, packed_width = received.shape
-    steps = head_count // heads
     first = pl.BlockSpec((events, lanes), lambda h: (0, h))
     second = pl.BlockSpec((events, lanes), lambda h: (1, h))
-    key_values = [keys, values] + [array for other in others for array in (other, other)]
+    held = pl.BlockSpec(memory_space=pl.ANY)
+    operands = [array for source in sources for array in (source, source)]
     return pl.pallas_call(
         lambda *refs: attend_kernel(head_size ** (-0.5), heads, *refs),
-        grid=(steps,),
+        grid=(width // lanes,),
         in_specs=[
-            pl.BlockSpec((column // steps, own, packed_width), lambda h: (h, 0, 0)),
-            first,
-            first,
+            pl.BlockSpec(memory_space=pltpu.SMEM),
+            pl.BlockSpec((lanes, cand), lambda h: (h, 0)),
         ]
-        + [second, first] * len(others)
+        + [first, second] * len(sources)
         + [
             pl.BlockSpec(bias.shape, lambda h: (0, 0)),
             pl.BlockSpec(live.shape, lambda h: (0, 0)),
-        ]
-        + [pl.BlockSpec(memory_space=pl.ANY)] * len(ready),
-        out_specs=pl.BlockSpec((cand, lanes), lambda h: (0, h)),
-        out_shape=jax.ShapeDtypeStruct((cand, width), jnp.bfloat16),
+            held,
+        ],
+        out_specs=[pl.BlockSpec((cand, lanes), lambda h: (0, h)), held],
+        out_shape=[
+            jax.ShapeDtypeStruct((cand, width), jnp.float32),
+            jax.ShapeDtypeStruct(through.shape, through.dtype),
+        ],
+        input_output_aliases={12: 1},
         compiler_params=pltpu.CompilerParams(vmem_limit_bytes=32 * 1024 * 1024),
         cost_estimate=pl.CostEstimate(
             flops=16 * cand * events * width,
             bytes_accessed=16 * events * width + 4 * cand * width,
-            transcendentals=4 * cand * events * head_count,
-        ),
-    )(received, *key_values, bias, live, *ready)
-
-
-def own_kernel(scale, rab, received, gain, after, self_term, gate):
+            transcendentals=4 * cand * events * (width // head_size),
+        ),
+    )(kind, queries, *operands, bias, live, through)
+
+
+def own_kernel(scale, rab, received, gain, self_term, gate):
     own, width = self_term.shape
     column = received.shape[0]
     lanes = width // column // 2
@@ -457,28 +495,40 @@
         self_term[:, head_lanes] = silu(score) * own_v[:, head_lanes]
 
 
-def own_parts(received, rab, gain, own, after):
+def own_parts(received, rab, gain, own):
     width = gain.shape[0]
     whole = pl.BlockSpec(memory_space=pltpu.VMEM)
     scale = (width // rab.shape[0]) ** (-0.5)
     return pl.pallas_call(
         lambda *refs: own_kernel(scale, *refs),
-        in_specs=[pl.BlockSpec(memory_space=pltpu.SMEM), whole, whole]
-        + [pl.BlockSpec(memory_space=pl.ANY)],
+        in_specs=[pl.BlockSpec(memory_space=pltpu.SMEM), whole, whole],
         out_specs=[whole] * 2,
         out_shape=[jax.ShapeDtypeStruct((own, width), jnp.float32)] * 2,
         compiler_params=pltpu.CompilerParams(vmem_limit_bytes=32 * 1024 * 1024),
         cost_estimate=pl.CostEstimate(
             flops=8 * own * width, bytes_accessed=32 * own * width, transcendentals=own
         ),
-    )(rab, received, gain.reshape(1, -1), after)
-
-
-def finish_kernel(numbers, parts, self_term, gate, embedded, *rest):
+    )(rab, received, gain.reshape(1, -1))
+
+
+def finish_kernel(head_size, numbers, parts, self_term, gate, embedded, *rest):
     weights, scored = rest[:-1], rest[-1]
-    history_sum = parts[0].astype(jnp.float32)
-    for part in range(1, parts.shape[0]):
-        history_sum = history_sum + parts[part].astype(jnp.float32)
+    classes = []
+    for kind in range(2):
+        total = None
+        for part in range(parts.shape[0]):
+            if head_class(part) == kind:
+                rows = parts[part].astype(jnp.float32)
+                total = rows if total is None else total + rows
+        classes.append(total)
+    history_sum = jnp.concatenate(
+        [
+            classes[kind][:, first : first + head_size]
+            for first in range(0, classes[0].shape[1], head_size)
+            for kind in range(2)
+        ],
+        axis=1,
+    )
     length = jnp.full((1, 1), numbers[0], jnp.int32).astype(jnp.float32)
     attended = history_sum * lax.rsqrt(length) + self_term[...]
     centre = jnp.mean(attended, axis=1, keepdims=True)
@@ -498,11 +548,11 @@
         )
 
 
-def finish(numbers, parts, self_term, gate, embedded, weights):
+def finish(head_size, numbers, parts, self_term, gate, embedded, weights):
     whole = pl.BlockSpec(memory_space=pltpu.VMEM)
     rows, width = embedded.shape
     return pl.pallas_call(
-        finish_kernel,
+        lambda *refs: finish_kernel(head_size, *refs),
         in_specs=[pl.BlockSpec(memory_space=pltpu.SMEM)] + [whole] * (4 + len(weights)),
         out_specs=whole,
         out_shape=jax.ShapeDtypeStruct((rows, width), jnp.bfloat16),
@@ -551,15 +601,19 @@
     w_sent = jnp.concatenate([w_slice[:w_half], w_slice[w_half:]], axis=1)
     w_sent = jnp.concatenate([w_mine, jnp.tile(w_sent, (1, width // (2 * out_lanes)))])
     w_other = swap_pair(w_sent)
-    w_here = exchange(spread(numbers, w_slice, w_other, column), column_groups())
-    w_here = w_here.reshape(width, out_lanes)
-
-    events_sent = jnp.concatenate([values, keys])
-    pair_events, place_events = swap_pair(events_sent), swap_place(events_sent)
-    others = pair_events, place_events, swap_pair(place_events)
+
+    kind = head_class(place)
+
+    own_events, sent_events = split_heads(kind[None], keys, values, width // head_count)
+    place_events = swap_place(sent_events)
+    sources = own_events, swap_pair(own_events), place_events, swap_pair(place_events)
+
+    partner = 2 * partner_place(place, column) + side
+    devices = jnp.stack([length, index_here, index_here ^ 1, partner, partner ^ 1])
+    bias, live = biases(devices, rab, events_here)
 
     slots, pair_slots, most = locate(numbers, item_ids, table_rows, device_count)
-    found = tuple(project(numbers, slots, pair_slots, rows, w_mine, w_other, (w_here, place_events, pair_events)))
+    found = tuple(project(numbers, slots, pair_slots, rows, w_mine, w_other, (*sources[1:3], bias, live)))
 
     def another(state):
         first_rank, limit, found = state
@@ -572,26 +626,35 @@
     _, _, (proj_mine, proj_other, own_rows) = lax.while_loop(
         lambda state: state[0] < state[1], another, (jnp.int32(slot_rows), most[0, 0], found)
     )
-    packed, embedded = pack(
-        proj_mine, swap_pair(proj_other), own_rows, (), feature_here
+    side_queries, packed, embedded = pack(
+        numbers,
+        proj_mine,
+        swap_pair(proj_other),
+        own_rows,
+        w_slice,
+        w_other,
+        feature_here,
+        sources[3:],
     )
     received = exchange(packed, column_groups())
-
-    sources = index_here ^ jnp.arange(4, dtype=jnp.int32)
-    positions = sources[:, None] * events_here + jnp.arange(events_here, dtype=jnp.int32)[None, :]
-    positions = positions.reshape(4 * events_here)
-    bias = bucket_bias(rab, length - positions)
-    live = (positions < length).astype(jnp.float32)[None, :]
-
+    class_queries = lax.all_gather(
+        side_queries, "seq", axis=0, tiled=True, axis_index_groups=class_groups()
+    )
+
+    summed, received = attend(kind[None], class_queries, sources, bias, live, received)
+    parts = exchange(summed.reshape(column, cand_here, width // 2), column_groups())
+    self_term, gate = own_parts(received, rab, norm_gain, cand_here)
+
+    w_here = (
+        received[:, :, 8 * feature_here :]
+        .reshape(column, cand_here, 2 * w_slice.shape[0] // cand_here, out_lanes)
+        .transpose(0, 2, 1, 3)
+        .reshape(width, out_lanes)
+    )
     weights = [w_here] + [from_row(w_here, shift) for shift in range(1, row_count)]
-    summed = attend(
-        received, history_keys, history_values, others, bias, live, cand_side // 2, weights[1:]
-    )
-    parts = exchange(summed.reshape(column // 2, cand_here, width), class_groups())
-    self_term, gate = own_parts(received, rab, norm_gain, cand_here, summed)
     weights = [*weights, *swap_core(jnp.stack(weights))]
     numbers = jnp.stack([length, row, core])
-    return finish(numbers, parts, self_term, gate, embedded, weights)
+    return finish(width // head_count, numbers, parts, self_term, gate, embedded, weights)
 
 
 def solution(mesh):

time: 178 us -> 166 us (0.933)
  blocking collectives: 0 us -> 39.3 us
  waiting for transfers between devices: 47.8 us -> 12.7 us
  local copies, waits for them, and re-layouts: 14.8 us -> 5.6 us
  starting transfers between devices: 93.3 us -> 88.6 us
    all_gather x0 -> x1, blocking collectives: none -> 39.3 us  [local(): lax.all_gather(side_queries, 'seq', axis=0, tiled=True, axis_index_groups...]
    all_to_all x4 -> x3, waiting for transfers between devices: 19.5 us -> 1.5 us  [exchange(): lax.all_to_all(blocks, 'seq', split_axis=0, concat_axis=0, tiled=True, ax...]
    ppermute x4, waiting for transfers between devices: 17.7 us -> 0.01 us  [from_place(): lax.ppermute(block, 'seq', [(i, (i + 2 * shift) % count) for i in range(c...]
    all_to_all x4 -> x3, starting transfers between devices: 44.9 us -> 32.4 us  [exchange(): lax.all_to_all(blocks, 'seq', split_axis=0, concat_axis=0, tiled=True, ax...]
    unnamed x40 -> x21, local copies, waits for them, and re-layouts: 10 us -> 2.1 us
    ppermute x1, starting transfers between devices: 4.87 us -> 11.1 us  [swap_core(): lax.ppermute(block, 'batch', [(i, i ^ 1) for i in range(lax.axis_size('ba...]
    ppermute x1, starting transfers between devices: 2.63 us -> 5.94 us  [swap_place(): lax.ppermute(block, 'seq', [(i, 2 * partner_place(i // 2, count // 2) + i...]
    ppermute x3, waiting for transfers between devices: 7.13 us -> 4.42 us  [from_row(): lax.ppermute(block, 'batch', [(i, (i + 4 * shift) % count) for i in range...]
  transfers between devices with their start and end apart: 17 -> 16, of which waited for: 6 -> 6; matrix products, arithmetic and copies ran while one was open for 4% -> 2% of each run, Pallas kernels for 5% -> 4%
where the time goes in v7:
time: 166 us; the launch traced here: 165 us
  starting transfers between devices  88.6 us (53%)
  blocking collectives  39.3 us (24%)
  Pallas kernels  16.4 us (10%)
  waiting for transfers between devices  12.7 us (8%)
  local copies, waits for them, and re-layouts  5.6 us (3%)
    all_gather x1, blocking collectives, local(): lax.all_gather(side_queries, 'seq', axis=0, tiled=True, axis_index_groups...  39.3 us
    all_to_all x3, starting transfers between devices, exchange(): lax.all_to_all(blocks, 'seq', split_axis=0, concat_axis=0, tiled=True, ax...  32.4 us
    ppermute x4, starting transfers between devices, from_place(): lax.ppermute(block, 'seq', [(i, (i + 2 * shift) % count) for i in range(c...  17.7 us
    ppermute x1, starting transfers between devices, swap_core(): lax.ppermute(block, 'batch', [(i, i ^ 1) for i in range(lax.axis_size('ba...  11.1 us
    ppermute x3, starting transfers between devices, from_row(): lax.ppermute(block, 'batch', [(i, (i + 4 * shift) % count) for i in range...  10.8 us
    ppermute x4, starting transfers between devices, swap_pair(): lax.ppermute(block, 'seq', [(i, i ^ 1) for i in range(lax.axis_size('seq'...  10.6 us
    ppermute x1, starting transfers between devices, swap_place(): lax.ppermute(block, 'seq', [(i, 2 * partner_place(i // 2, count // 2) + i...  5.94 us
    ppermute x4, waiting for transfers between devices, swap_pair(): lax.ppermute(block, 'seq', [(i, i ^ 1) for i in range(lax.axis_size('seq'...  5.46 us
  transfers between devices with their start and end apart: 16, of which 6 were waited for; matrix products, arithmetic and copies ran while one was open for 2% of the time, Pallas kernels for 4%

profile of v7, /device:TPU:1, one launch (start us, length us, event | category | flops | bytes accessed | tf_op | source)
XLA Modules:
  0.0 164.5 jit_solution(7772245281226239651)
XLA Ops:
  0.0 0.1 pad_add_fusion.2.refs_0_.numbers
  0.1 0.6 copy-done.16
  0.7 2.6 %shard_map.92 = bf16[4,32,1024]{2,1,0:T(8,128)(2,1)} custom-call(s32[2]{0:T(128)S(1)} %pad_add_fusion.2.refs_0_.numbers, s32[1,512]{1,0:T(1,128)S(1)} %bitcast.78, bf16[512,1024]{1,0:T(8,128)(2,1)} %table.1), custom_call_target="tpu_custom_call" | custom-call | flops 33554432 | bytes 1048576 | tf_op jit(solution)/shard_map/pallas_call | solution.py:156
  3.3 15.8 %all-to-all-start.1 = ((bf16[4,32,1024]{2,1,0:T(8,128)(2,1)}), bf16[4,32,1024]{2,1,0:T(8,128)(2,1)S(1)}, u32[]{:S(2)}, u32[]{:S(2)}) async-start(bf16[4,32,1024]{2,1,0:T(8,128)(2,1)} %shard_map.92), calls=%async_computation.1 | async-start | bytes 524288 | tf_op jit(solution)/shard_map/all_to_all | solution.py:17
  19.1 0.2 shard_map.93
  19.3 3.1 %collective-permute-start.9 = (bf16[512,512]{1,0:T(8,128)(2,1)S(1)}, bf16[512,512]{1,0:T(8,128)(2,1)S(1)}, u32[]{:S(2)}, u32[]{:S(2)}) collective-permute-start(bf16[512,512]{1,0:T(8,128)(2,1)S(1)} %get-tuple-element.94.refs_2_.refs_3_), channel_id=1, source_target_pairs={{0,1},{1,0},{2,3},{3,2},{4,5},{5,4},{6,7},{7,6},{8,9},{9,8},{10,11... | collective-permute-start | bytes 1572872 | tf_op jit(solution)/shard_map/ppermute | solution.py:39
  22.4 5.9 %collective-permute-start.10 = (bf16[512,512]{1,0:T(8,128)(2,1)S(1)}, bf16[512,512]{1,0:T(8,128)(2,1)S(1)}, u32[]{:S(2)}, u32[]{:S(2)}) collective-permute-start(bf16[512,512]{1,0:T(8,128)(2,1)S(1)} %get-tuple-element.95), channel_id=1, source_target_pairs={{0,30},{1,31},{2,4},{3,5},{4,2},{5,3},{6,8},{7,9},{8,6},{9,7},{10,... | collective-permute-start | bytes 1572872 | tf_op jit(solution)/shard_map/ppermute | solution.py:52
  28.4 0.7 constant_dynamic-slice_fusion
  29.2 2.2 %collective-permute-start.8 = (bf16[144,1024]{1,0:T(8,128)(2,1)S(1)}, bf16[144,1024]{1,0:T(8,128)(2,1)S(1)}, u32[]{:S(2)}, u32[]{:S(2)}) collective-permute-start(bf16[144,1024]{1,0:T(8,128)(2,1)S(1)} %pad_maximum_fusion.1), channel_id=1, source_target_pairs={{0,1},{1,0},{2,3},{3,2},{4,5},{5,4},{6,7},{7,6},{8,9},{9,8},{10,11... | collective-permute-start | bytes 884744 | tf_op jit(solution)/shard_map/ppermute | solution.py:39
  31.4 1.5 all-to-all-done.1
  32.9 8.4 %collective-permute-start.4 = (bf16[128,1024]{1,0:T(8,128)(2,1)S(1)}, bf16[128,1024]{1,0:T(8,128)(2,1)S(1)}, u32[]{:S(2)}, u32[]{:S(2)}) collective-permute-start(bf16[128,1024]{1,0:T(8,128)(2,1)S(1)} %bitcast.61), channel_id=1, source_target_pairs={{0,2},{1,3},{2,4},{3,5},{4,6},{5,7},{6,8},{7,9},{8,10},{9,11},{10,... | collective-permute-start | bytes 786440 | tf_op jit(solution)/shard_map/ppermute | solution.py:35
  41.3 1.9 %collective-permute-start.5 = (bf16[128,1024]{1,0:T(8,128)(2,1)S(1)}, bf16[128,1024]{1,0:T(8,128)(2,1)S(1)}, u32[]{:S(2)}, u32[]{:S(2)}) collective-permute-start(bf16[128,1024]{1,0:T(8,128)(2,1)S(1)} %bitcast.62), channel_id=1, source_target_pairs={{0,30},{1,31},{2,0},{3,1},{4,2},{5,3},{6,4},{7,5},{8,6},{9,7},{10,... | collective-permute-start | bytes 786440 | tf_op jit(solution)/shard_map/ppermute | solution.py:35
  43.2 0.7 fusion.1
  44.0 0.7 copy-done.7
  44.7 3.8 %collective-permute-start.6 = (bf16[64,1024]{1,0:T(8,128)(2,1)}, bf16[64,1024]{1,0:T(8,128)(2,1)S(1)}, u32[]{:S(2)}, u32[]{:S(2)}) collective-permute-start(bf16[64,1024]{1,0:T(8,128)(2,1)} %bitcast.12), channel_id=1, source_target_pairs={{0,4},{1,5},{2,6},{3,7},{4,8},{5,9},{6,10},{7,11},{8,12},{9,13},{1... | collective-permute-start | bytes 393224 | tf_op jit(solution)/shard_map/ppermute | solution.py:35
  48.5 3.6 %collective-permute-start.7 = (bf16[64,1024]{1,0:T(8,128)(2,1)}, bf16[64,1024]{1,0:T(8,128)(2,1)S(1)}, u32[]{:S(2)}, u32[]{:S(2)}) collective-permute-start(bf16[64,1024]{1,0:T(8,128)(2,1)} %bitcast.13), channel_id=1, source_target_pairs={{0,28},{1,29},{2,30},{3,31},{4,0},{5,1},{6,2},{7,3},{8,4},{9,5},{1... | collective-permute-start | bytes 393224 | tf_op jit(solution)/shard_map/ppermute | solution.py:35
  52.8 1.2 shard_map.91
  54.0 0.6 slice.42
  54.6 0.6 stack.57.numbers
  55.2 1.5 shard_map.94
  56.7 3.1 %collective-permute-start.12 = (bf16[512,512]{1,0:T(8,128)(2,1)S(1)}, bf16[512,512]{1,0:T(8,128)(2,1)S(1)}, u32[]{:S(2)}, u32[]{:S(2)}) collective-permute-start(bf16[512,512]{1,0:T(8,128)(2,1)S(1)} %collective-permute-done.10.rest_1_.refs_6_.refs_7_), channel_id=1, source_target_pairs={{0,1},{1,0},{2,3},{3,2},{4,5},{5,4},{6,7},{7,6},{8,9},{9,8},{10,11... | collective-permute-start | bytes 1572872 | tf_op jit(solution)/shard_map/ppermute | solution.py:39
  59.8 0.0 copy-start.2
  59.8 0.7 copy-done.2
  60.6 3.1 %shard_map.95 = (bf16[256,256]{1,0:T(8,128)(2,1)}, bf16[320,256]{1,0:T(8,128)(2,1)}, bf16[16,1024]{1,0:T(8,128)(2,1)}) custom-call(s32[2]{0:T(128)S(1)} %pad_add_fusion.2.refs_0_.numbers, s32[512,1]{1,0:T(8,128)S(1)} %get-tuple-element.87.at, s32[32,1]{1,0:T(8,128)S(1)} %get-tuple-element.88.at_pair, bf16[128,1024]{1,0:T(8,128)(2,1)S(1)} %bitcast.63, ...), custom_call_target="tpu_custom_call" | custom-call | flops 402653184 | bytes 1572864 | tf_op jit(solution)/shard_map/pallas_call | solution.py:326
  63.6 0.6 while.14
  64.3 2.2 %collective-permute-start.11 = (bf16[320,256]{1,0:T(8,128)(2,1)}, bf16[320,256]{1,0:T(8,128)(2,1)S(1)}, u32[]{:S(2)}, u32[]{:S(2)}) collective-permute-start(bf16[320,256]{1,0:T(8,128)(2,1)} %get-tuple-element.103), channel_id=1, source_target_pairs={{0,1},{1,0},{2,3},{3,2},{4,5},{5,4},{6,7},{7,6},{8,9},{9,8},{10,11... | collective-permute-start | bytes 491528 | tf_op jit(solution)/shard_map/ppermute | solution.py:39
  66.5 0.7 constant_dynamic-slice_fusion.1.refs_4_
  67.2 1.5 collective-permute-done.12.refs_6_.refs_8_.refs_9_
  68.7 4.0 %collective-permute-done.11.refs_2_ = bf16[320,256]{1,0:T(8,128)(2,1)S(1)} collective-permute-done((bf16[320,256]{1,0:T(8,128)(2,1)}, bf16[320,256]{1,0:T(8,128)(2,1)S(1)}, u32[]{:S(2)}, u32[]{:S(2)}) %collective-permute-start.11) | collective-permute-done | bytes 163872 | tf_op jit(solution)/shard_map/ppermute | solution.py:39
  72.7 2.0 %shard_map.96 = (bf16[64,256]{1,0:T(8,128)(2,1)S(1)}, bf16[16,16,768]{2,1,0:T(8,128)(2,1)}, bf16[16,1024]{1,0:T(8,128)(2,1)S(1)}) custom-call(s32[2]{0:T(128)S(1)} %pad_add_fusion.2.refs_0_.numbers, bf16[256,256]{1,0:T(8,128)(2,1)} %get-tuple-element.102.refs_1_, bf16[320,256]{1,0:T(8,128)(2,1)S(1)} %collective-permute-done.11.refs_2_, ...), custom_call_target="tpu_custom_call" | custom-call | flops 65536 | bytes 524288 | tf_op jit(solution)/shard_map/pallas_call | solution.py:390
  74.6 7.4 %all-to-all-start.2 = ((bf16[16,16,768]{2,1,0:T(8,128)(2,1)}), bf16[16,16,768]{2,1,0:T(8,128)(2,1)S(1)}, u32[]{:S(2)}, u32[]{:S(2)}) async-start(bf16[16,16,768]{2,1,0:T(8,128)(2,1)} %get-tuple-element.106), calls=%async_computation.2 | async-start | bytes 786432 | tf_op jit(solution)/shard_map/all_to_all | solution.py:17
  82.0 39.3 %all_gather.3.refs_1_ = bf16[512,256]{1,0:T(8,128)(2,1)S(1)} all-gather(bf16[64,256]{1,0:T(8,128)(2,1)S(1)} %get-tuple-element.105), channel_id=1, replica_groups={{0,2,8,10,16,18,24,26},{4,6,12,14,20,22,28,30},{1,3,9,11,17,19,25,27},{..., dimensions={0}, use_global_device_ids=true | all-gather | bytes 294912 | tf_op jit(solution)/shard_map/all_gather | solution.py:640
  121.3 3.3 %shard_map.97 = (f32[256,512]{1,0:T(8,128)}, bf16[16,16,768]{2,1,0:T(8,128)(2,1)S(1)}) custom-call(s32[1]{0:T(128)} %bitcast.8.refs_0_, bf16[512,256]{1,0:T(8,128)(2,1)S(1)} %all_gather.3.refs_1_, bf16[512,512]{1,0:T(8,128)(2,1)S(1)} %get-tuple-element.94.refs_2_.refs_3_, ...), custom_call_target="tpu_custom_call", output_to_operand_aliasing={{1}: (12, {})} | custom-call | flops 536870912 | bytes 2621440 | tf_op jit(solution)/shard_map/pallas_call | solution.py:445
  124.6 9.2 %all-to-all-start.3 = ((f32[16,16,512]{2,1,0:T(8,128)}), f32[16,16,512]{2,1,0:T(8,128)S(1)}, u32[]{:S(2)}, u32[]{:S(2)}) async-start(f32[16,16,512]{2,1,0:T(8,128)} %bitcast.21), calls=%async_computation.3 | async-start | bytes 1048576 | tf_op jit(solution)/shard_map/all_to_all | solution.py:17
  133.8 0.1 copy_bitcast_fusion
  133.9 3.3 %collective-permute-start.13 = (bf16[1024,128]{1,0:T(8,128)(2,1)S(1)}, bf16[1024,128]{1,0:T(8,128)(2,1)S(1)}, u32[]{:S(2)}, u32[]{:S(2)}) collective-permute-start(bf16[1024,128]{1,0:T(8,128)(2,1)S(1)} %bitcast.64), channel_id=1, source_target_pairs={{0,128},{32,160},{64,192},{96,224},{128,256},{160,288},{192,320},{... | collective-permute-start | bytes 786440 | tf_op jit(solution)/shard_map/ppermute | solution.py:65
  137.2 4.5 %collective-permute-start.14 = (bf16[1024,128]{1,0:T(8,128)(2,1)S(1)}, bf16[1024,128]{1,0:T(8,128)(2,1)S(1)}, u32[]{:S(2)}, u32[]{:S(2)}) collective-permute-start(bf16[1024,128]{1,0:T(8,128)(2,1)S(1)} %bitcast.65), channel_id=1, source_target_pairs={{0,256},{32,288},{64,320},{96,352},{128,384},{160,416},{192,448},{... | collective-permute-start | bytes 786440 | tf_op jit(solution)/shard_map/ppermute | solution.py:65
  141.8 3.0 %collective-permute-start.15 = (bf16[1024,128]{1,0:T(8,128)(2,1)S(1)}, bf16[1024,128]{1,0:T(8,128)(2,1)S(1)}, u32[]{:S(2)}, u32[]{:S(2)}) collective-permute-start(bf16[1024,128]{1,0:T(8,128)(2,1)S(1)} %bitcast.66), channel_id=1, source_target_pairs={{0,384},{32,416},{64,448},{96,480},{128,0},{160,32},{192,64},{224,... | collective-permute-start | bytes 786440 | tf_op jit(solution)/shard_map/ppermute | solution.py:65
  144.8 1.6 collective-permute-done.14.refs_7_
  146.4 2.8 %collective-permute-done.15.refs_8_ = bf16[1024,128]{1,0:T(8,128)(2,1)S(1)} collective-permute-done((bf16[1024,128]{1,0:T(8,128)(2,1)S(1)}, bf16[1024,128]{1,0:T(8,128)(2,1)S(1)}, u32[]{:S(2)}, u32[]{:S(2)}) %collective-permute-start.15) | collective-permute-done | bytes 262176 | tf_op jit(solution)/shard_map/ppermute | solution.py:65
  149.2 0.1 pad_maximum_fusion
  149.3 0.0 copy-start.4
  149.3 11.1 %collective-permute-start.16 = (bf16[4,1024,128]{2,1,0:T(8,128)(2,1)S(1)}, bf16[4,1024,128]{2,1,0:T(8,128)(2,1)S(1)}, u32[]{:S(2)}, u32[]{:S(2)}) collective-permute-start(bf16[4,1024,128]{2,1,0:T(8,128)(2,1)S(1)} %pad_maximum_fusion), channel_id=1, source_target_pairs={{0,32},{32,0},{64,96},{96,64},{128,160},{160,128},{192,224},{224,1... | collective-permute-start | bytes 3145736 | tf_op jit(solution)/shard_map/ppermute | solution.py:60
  160.4 0.1 pad_add_fusion.1.refs_0_
  160.5 0.9 shard_map.98
  161.4 1.3 collective-permute-done.16
  162.7 0.1 slice_bitcast_fusion
  162.8 1.7 %shard_map.99 = bf16[16,1024]{1,0:T(8,128)(2,1)} custom-call(s32[3]{0:T(128)S(1)} %pad_add_fusion.1.refs_0_, f32[16,16,512]{2,1,0:T(8,128)S(1)} %all-to-all-done.3.refs_1_, f32[16,1024]{1,0:T(8,128)S(1)} %get-tuple-element.109.refs_2_, f32[16,1024]{1,0:T(8,128)S(1)} %get-tuple-element.110.refs_3_, bf16[16,1024]{1,0:T(8,128)(2,1)S(1)} %get-tuple-element.111.refs_4_, ...), custom_call_target="tpu_custom_call" | custom-call | flops 33554432 | bytes 4194304 | tf_op jit(solution)/shard_map/pallas_call | solution.py:554
  (29 shorter events, 0.1 us)
Async XLA Ops:
  0.0 0.7 copy-start.16
  0.7 18.4 %copy-start.1 = (bf16[256,1024]{1,0:T(8,128)(2,1)S(1)}, bf16[256,1024]{1,0:T(8,128)(2,1)}, u32[]{:S(2)}) copy-start(bf16[256,1024]{1,0:T(8,128)(2,1)} %refs_2_) | copy-start | bytes 1572868
  3.3 15.8 %copy-start = (bf16[256,1024]{1,0:T(8,128)(2,1)S(1)}, bf16[256,1024]{1,0:T(8,128)(2,1)}, u32[]{:S(2)}) copy-start(bf16[256,1024]{1,0:T(8,128)(2,1)} %refs_1_) | copy-start | bytes 1572868
  3.3 29.5 %all-to-all-start.1 = ((bf16[4,32,1024]{2,1,0:T(8,128)(2,1)}), bf16[4,32,1024]{2,1,0:T(8,128)(2,1)S(1)}, u32[]{:S(2)}, u32[]{:S(2)}) async-start(bf16[4,32,1024]{2,1,0:T(8,128)(2,1)} %shard_map.92), calls=%async_computation.1 | async-start | bytes 524288 | tf_op jit(solution)/shard_map/all_to_all | solution.py:17
  19.1 10.1 %copy-start.8 = (bf16[1024,4,32]{0,2,1:T(8,128)(2,1)S(1)}, bf16[1024,4,32]{0,2,1:T(8,128)(2,1)}, u32[]{:S(2)}) copy-start(bf16[1024,4,32]{0,2,1:T(8,128)(2,1)} %param.16) | copy-start | bytes 786436
  19.3 29.2 %collective-permute-start.9 = (bf16[512,512]{1,0:T(8,128)(2,1)S(1)}, bf16[512,512]{1,0:T(8,128)(2,1)S(1)}, u32[]{:S(2)}, u32[]{:S(2)}) collective-permute-start(bf16[512,512]{1,0:T(8,128)(2,1)S(1)} %get-tuple-element.94.refs_2_.refs_3_), channel_id=1, source_target_pairs={{0,1},{1,0},{2,3},{3,2},{4,5},{5,4},{6,7},{7,6},{8,9},{9,8},{10,11... | collective-permute-start | bytes 1572872 | tf_op jit(solution)/shard_map/ppermute | solution.py:39
  22.4 34.3 %collective-permute-start.10 = (bf16[512,512]{1,0:T(8,128)(2,1)S(1)}, bf16[512,512]{1,0:T(8,128)(2,1)S(1)}, u32[]{:S(2)}, u32[]{:S(2)}) collective-permute-start(bf16[512,512]{1,0:T(8,128)(2,1)S(1)} %get-tuple-element.95), channel_id=1, source_target_pairs={{0,30},{1,31},{2,4},{3,5},{4,2},{5,3},{6,8},{7,9},{8,6},{9,7},{10,... | collective-permute-start | bytes 1572872 | tf_op jit(solution)/shard_map/ppermute | solution.py:52
  29.2 14.8 %collective-permute-start.8 = (bf16[144,1024]{1,0:T(8,128)(2,1)S(1)}, bf16[144,1024]{1,0:T(8,128)(2,1)S(1)}, u32[]{:S(2)}, u32[]{:S(2)}) collective-permute-start(bf16[144,1024]{1,0:T(8,128)(2,1)S(1)} %pad_maximum_fusion.1), channel_id=1, source_target_pairs={{0,1},{1,0},{2,3},{3,2},{4,5},{5,4},{6,7},{7,6},{8,9},{9,8},{10,11... | collective-permute-start | bytes 884744 | tf_op jit(solution)/shard_map/ppermute | solution.py:39
  32.9 26.9 %collective-permute-start.4 = (bf16[128,1024]{1,0:T(8,128)(2,1)S(1)}, bf16[128,1024]{1,0:T(8,128)(2,1)S(1)}, u32[]{:S(2)}, u32[]{:S(2)}) collective-permute-start(bf16[128,1024]{1,0:T(8,128)(2,1)S(1)} %bitcast.61), channel_id=1, source_target_pairs={{0,2},{1,3},{2,4},{3,5},{4,6},{5,7},{6,8},{7,9},{8,10},{9,11},{10,... | collective-permute-start | bytes 786440 | tf_op jit(solution)/shard_map/ppermute | solution.py:35
  41.3 18.5 %collective-permute-start.5 = (bf16[128,1024]{1,0:T(8,128)(2,1)S(1)}, bf16[128,1024]{1,0:T(8,128)(2,1)S(1)}, u32[]{:S(2)}, u32[]{:S(2)}) collective-permute-start(bf16[128,1024]{1,0:T(8,128)(2,1)S(1)} %bitcast.62), channel_id=1, source_target_pairs={{0,30},{1,31},{2,0},{3,1},{4,2},{5,3},{6,4},{7,5},{8,6},{9,7},{10,... | collective-permute-start | bytes 786440 | tf_op jit(solution)/shard_map/ppermute | solution.py:35
  44.0 0.7 copy-start.7
  44.7 15.1 %collective-permute-start.6 = (bf16[64,1024]{1,0:T(8,128)(2,1)}, bf16[64,1024]{1,0:T(8,128)(2,1)S(1)}, u32[]{:S(2)}, u32[]{:S(2)}) collective-permute-start(bf16[64,1024]{1,0:T(8,128)(2,1)} %bitcast.12), channel_id=1, source_target_pairs={{0,4},{1,5},{2,6},{3,7},{4,8},{5,9},{6,10},{7,11},{8,12},{9,13},{1... | collective-permute-start | bytes 393224 | tf_op jit(solution)/shard_map/ppermute | solution.py:35
  48.5 11.3 %collective-permute-start.7 = (bf16[64,1024]{1,0:T(8,128)(2,1)}, bf16[64,1024]{1,0:T(8,128)(2,1)S(1)}, u32[]{:S(2)}, u32[]{:S(2)}) collective-permute-start(bf16[64,1024]{1,0:T(8,128)(2,1)} %bitcast.13), channel_id=1, source_target_pairs={{0,28},{1,29},{2,30},{3,31},{4,0},{5,1},{6,2},{7,3},{8,4},{9,5},{1... | collective-permute-start | bytes 393224 | tf_op jit(solution)/shard_map/ppermute | solution.py:35
  56.7 3.1 %copy-start.5 = (f32[1,1024]{1,0:T(1,128)S(1)}, f32[1,1024]{1,0:T(1,128)}, u32[]{:S(2)}) copy-start(f32[1,1024]{1,0:T(1,128)} %get-tuple-element.97.rest_3_.refs_11_) | copy-start | bytes 12292
  56.7 12.0 %collective-permute-start.12 = (bf16[512,512]{1,0:T(8,128)(2,1)S(1)}, bf16[512,512]{1,0:T(8,128)(2,1)S(1)}, u32[]{:S(2)}, u32[]{:S(2)}) collective-permute-start(bf16[512,512]{1,0:T(8,128)(2,1)S(1)} %collective-permute-done.10.rest_1_.refs_6_.refs_7_), channel_id=1, source_target_pairs={{0,1},{1,0},{2,3},{3,2},{4,5},{5,4},{6,7},{7,6},{8,9},{9,8},{10,11... | collective-permute-start | bytes 1572872 | tf_op jit(solution)/shard_map/ppermute | solution.py:39
  59.8 0.8 copy-start.2
  64.3 8.4 %collective-permute-start.11 = (bf16[320,256]{1,0:T(8,128)(2,1)}, bf16[320,256]{1,0:T(8,128)(2,1)S(1)}, u32[]{:S(2)}, u32[]{:S(2)}) collective-permute-start(bf16[320,256]{1,0:T(8,128)(2,1)} %get-tuple-element.103), channel_id=1, source_target_pairs={{0,1},{1,0},{2,3},{3,2},{4,5},{5,4},{6,7},{7,6},{8,9},{9,8},{10,11... | collective-permute-start | bytes 491528 | tf_op jit(solution)/shard_map/ppermute | solution.py:39
  74.6 46.7 %all-to-all-start.2 = ((bf16[16,16,768]{2,1,0:T(8,128)(2,1)}), bf16[16,16,768]{2,1,0:T(8,128)(2,1)S(1)}, u32[]{:S(2)}, u32[]{:S(2)}) async-start(bf16[16,16,768]{2,1,0:T(8,128)(2,1)} %get-tuple-element.106), calls=%async_computation.2 | async-start | bytes 786432 | tf_op jit(solution)/shard_map/all_to_all | solution.py:17
  82.0 39.3 %copy-start.3 = (f32[8,1024]{1,0:T(8,128)S(1)}, f32[8,1024]{1,0:T(8,128)}, u32[]{:S(2)}) copy-start(f32[8,1024]{1,0:T(8,128)} %get-tuple-element.96.rest_2_.refs_10_) | copy-start | bytes 98308
  124.6 38.2 %all-to-all-start.3 = ((f32[16,16,512]{2,1,0:T(8,128)}), f32[16,16,512]{2,1,0:T(8,128)S(1)}, u32[]{:S(2)}, u32[]{:S(2)}) async-start(f32[16,16,512]{2,1,0:T(8,128)} %bitcast.21), calls=%async_computation.3 | async-start | bytes 1048576 | tf_op jit(solution)/shard_map/all_to_all | solution.py:17
  133.9 10.9 %collective-permute-start.13 = (bf16[1024,128]{1,0:T(8,128)(2,1)S(1)}, bf16[1024,128]{1,0:T(8,128)(2,1)S(1)}, u32[]{:S(2)}, u32[]{:S(2)}) collective-permute-start(bf16[1024,128]{1,0:T(8,128)(2,1)S(1)} %bitcast.64), channel_id=1, source_target_pairs={{0,128},{32,160},{64,192},{96,224},{128,256},{160,288},{192,320},{... | collective-permute-start | bytes 786440 | tf_op jit(solution)/shard_map/ppermute | solution.py:65
  137.2 9.2 %collective-permute-start.14 = (bf16[1024,128]{1,0:T(8,128)(2,1)S(1)}, bf16[1024,128]{1,0:T(8,128)(2,1)S(1)}, u32[]{:S(2)}, u32[]{:S(2)}) collective-permute-start(bf16[1024,128]{1,0:T(8,128)(2,1)S(1)} %bitcast.65), channel_id=1, source_target_pairs={{0,256},{32,288},{64,320},{96,352},{128,384},{160,416},{192,448},{... | collective-permute-start | bytes 786440 | tf_op jit(solution)/shard_map/ppermute | solution.py:65
  141.8 7.4 %collective-permute-start.15 = (bf16[1024,128]{1,0:T(8,128)(2,1)S(1)}, bf16[1024,128]{1,0:T(8,128)(2,1)S(1)}, u32[]{:S(2)}, u32[]{:S(2)}) collective-permute-start(bf16[1024,128]{1,0:T(8,128)(2,1)S(1)} %bitcast.66), channel_id=1, source_target_pairs={{0,384},{32,416},{64,448},{96,480},{128,0},{160,32},{192,64},{224,... | collective-permute-start | bytes 786440 | tf_op jit(solution)/shard_map/ppermute | solution.py:65
  149.2 11.3 %copy-start.6 = (f32[1024]{0:T(1024)S(1)}, f32[1024]{0:T(1024)}, u32[]{:S(2)}) copy-start(f32[1024]{0:T(1024)} %param.18) | copy-start | bytes 12292
  149.3 11.2 %copy-start.4 = (f32[8,16]{1,0:T(8,128)S(1)}, f32[8,16]{1,0:T(8,128)}, u32[]{:S(2)}) copy-start(f32[8,16]{1,0:T(8,128)} %refs_0_.1) | copy-start | bytes 1540
  149.3 13.4 %collective-permute-start.16 = (bf16[4,1024,128]{2,1,0:T(8,128)(2,1)S(1)}, bf16[4,1024,128]{2,1,0:T(8,128)(2,1)S(1)}, u32[]{:S(2)}, u32[]{:S(2)}) collective-permute-start(bf16[4,1024,128]{2,1,0:T(8,128)(2,1)S(1)} %pad_maximum_fusion), channel_id=1, source_target_pairs={{0,32},{32,0},{64,96},{96,64},{128,160},{160,128},{192,224},{224,1... | collective-permute-start | bytes 3145736 | tf_op jit(solution)/shard_map/ppermute | solution.py:60
